TPU v7x, 256 devices: a whole 4x4x8 slice. The times are simulated.
256 devices in a mesh: dp: 8 (over x, core), mp: 32 (over z, y).
Axes of the slice: x: 4, y: 4, z: 8, core: 2. Of those that a mesh axis runs over, the one named last changes fastest.
Arguments:
- tokens: bfloat16 [8192, 8192], P('dp', 'mp'), may hold values from -6 to 6
- cotangent: bfloat16 [8192, 14336], P('dp', 'mp'), may hold values from -0.1875 to 0.1875
- frozen_up_weight: bfloat16 [8192, 14336], P(None, 'mp'), may hold values from -0.0625 to 0.0625
- down_factors: bfloat16 [64, 8192, 64], P('dp', 'mp'), may hold values from -0.0625 to 0.0625
- up_factors: bfloat16 [64, 64, 14336], P('dp', None, 'mp'), may hold values from -0.75 to 0.75
- used: int32 [8, 8], P('dp'), may hold values from 0 to 63, as said below
- sequence_slot: int32 [8, 8], P('dp'), may hold values from 0 to 7, each once within a row
Outputs:
- adjusted_projection: bfloat16 [8192, 14336], P('dp', 'mp')
- grad_a: float32 [64, 8192, 64], P('dp', 'mp')
- grad_b: float32 [64, 64, 14336], P('dp', None, 'mp')
Inputs may be any that keep to these rules, and one draw needn't show every extreme that they name: `used`: each row holds 8 distinct adapters; from the 8 adapters k*8 to (k+1)*8 - 1 of one index k of dp a row takes none or exactly 2.
All inputs are finite; a program needn't handle non-finite values.
Results may differ from a plain program's by a relative error of at most 0.0075.
Values may be sent and summed in bfloat16 or wider, within the bound.
No kernel may reach another device: no remote copies, remote signals or barrier semaphores. Data moves between devices by JAX's collectives and lax.ppermute only.
A program may use at most 128 MiB of HBM per device.

v0:
```python
import jax
import jax.numpy as jnp
from jax import lax
from jax.sharding import PartitionSpec as P

BLEND_MULTIPLIER = 2.0


def on_device(tokens, cotangent, frozen_up_weight, down_factors, up_factors, used, sequence_slot):
    groups = lax.axis_size("dp")
    tok_rows = tokens.shape[0]
    shard_width = tokens.shape[1]
    inner_dimension = down_factors.shape[2]
    bin_number = used.shape[1]
    adapters_per_holder = down_factors.shape[0]
    seq_len = tok_rows // sequence_slot.shape[1]
    token_slot = jnp.repeat(sequence_slot[0], seq_len)
    member = token_slot[:, None] == jnp.arange(bin_number)[None, :]
    bank_a, bank_b = (
        lax.all_gather(down_factors, "dp", axis=0, tiled=True),
        lax.all_gather(up_factors, "dp", axis=0, tiled=True),
    )
    picked_a = jnp.take(bank_a, used[0], axis=0)
    picked_b = jnp.take(bank_b, used[0], axis=0)
    a_flat = jnp.transpose(picked_a, (1, 0, 2)).reshape(shard_width, bin_number * inner_dimension)
    up_factor_flat = picked_b.reshape(bin_number * inner_dimension, -1)
    mask_f = member.astype(jnp.float32)
    mask_b = member.astype(jnp.bfloat16)
    inputs_all = jnp.dot(tokens, a_flat, preferred_element_type=jnp.float32).reshape(
        tok_rows, bin_number, inner_dimension
    )
    inputs_part = jnp.sum(inputs_all * mask_f[:, :, None], axis=1)
    back_all = lax.dot_general(
        cotangent, up_factor_flat, (((1,), (1,)), ((), ())), preferred_element_type=jnp.float32
    )
    returned_cotangent_piece = BLEND_MULTIPLIER * jnp.sum(
        back_all.reshape(tok_rows, bin_number, inner_dimension) * mask_f[:, :, None], axis=1
    )
    adapter_in = lax.psum(inputs_part, "mp")
    adapter_bf = adapter_in.astype(jnp.bfloat16)
    spread_input = (adapter_bf[:, None, :] * mask_b[:, :, None]).reshape(
        tok_rows, bin_number * inner_dimension
    )
    fixed_projection_result = jnp.dot(
        lax.all_gather(tokens, "mp", axis=1, tiled=True),
        frozen_up_weight,
        preferred_element_type=jnp.float32,
    )
    narrow_product_result = jnp.dot(
        spread_input, up_factor_flat, preferred_element_type=jnp.float32
    )
    adjusted_projection = (
        fixed_projection_result + BLEND_MULTIPLIER * narrow_product_result
    ).astype(jnp.bfloat16)
    adapter_back = lax.psum(returned_cotangent_piece, "mp")
    back_bf = adapter_back.astype(jnp.bfloat16)
    spread_back = (back_bf[:, None, :] * mask_b[:, :, None]).reshape(
        tok_rows, bin_number * inner_dimension
    )
    grad_a_flat = lax.dot_general(
        tokens, spread_back, (((0,), (0,)), ((), ())), preferred_element_type=jnp.float32
    )
    grad_a_slots = jnp.transpose(
        grad_a_flat.reshape(shard_width, bin_number, inner_dimension), (1, 0, 2)
    )
    second_derivative_plane = lax.dot_general(
        spread_input, cotangent, (((0,), (0,)), ((), ())), preferred_element_type=jnp.float32
    )
    second_derivative_bins = BLEND_MULTIPLIER * second_derivative_plane.reshape(
        bin_number, inner_dimension, -1
    )
    grad_a_bf = grad_a_slots.astype(jnp.bfloat16)
    grad_b_bf = second_derivative_bins.astype(jnp.bfloat16)
    adapter_count = adapters_per_holder * groups
    placing = (used[0][:, None] == jnp.arange(adapter_count)[None, :]).astype(jnp.bfloat16)
    full_a = jnp.einsum("ua,udr->adr", placing, grad_a_bf, preferred_element_type=jnp.float32)
    full_b = jnp.einsum("ua,urf->arf", placing, grad_b_bf, preferred_element_type=jnp.float32)
    grad_a, grad_b = (
        lax.psum_scatter(full_a.astype(jnp.bfloat16), "dp", scatter_dimension=0, tiled=True).astype(
            jnp.float32
        ),
        lax.psum_scatter(full_b.astype(jnp.bfloat16), "dp", scatter_dimension=0, tiled=True).astype(
            jnp.float32
        ),
    )
    return (adjusted_projection, grad_a, grad_b)


def solution(mesh):
    return jax.shard_map(
        on_device,
        mesh=mesh,
        in_specs=(
            P("dp", "mp"),
            P("dp", "mp"),
            P(None, "mp"),
            P("dp", "mp", None),
            P("dp", None, "mp"),
            P("dp", None),
            P("dp", None),
        ),
        out_specs=(P("dp", "mp"), P("dp", "mp", None), P("dp", None, "mp")),
        check_vma=False,
    )
```

profile of v0, /device:TPU:1, one launch (start us, length us, event | category | flops | bytes accessed | tf_op | source)
XLA Modules:
  0.0 417.1 jit_solution(9693883841574758728)
XLA Ops:
  8.0 0.0 copy-start
  8.0 0.0 copy-start.1
  8.0 0.0 all-gather.6.cloned.1.call-start
  8.1 0.7 all-gather.6.cloned.1.call-update
  8.8 0.0 all-gather.8.cloned.1.call-start
  8.8 0.7 all-gather.8.cloned.1.call-update
  9.5 0.0 reduce-scatter.7.cloned.1.call-start
  9.6 0.7 compare_and_fusion
  10.2 0.0 copy-start.6
  10.2 0.1 broadcast_in_dim.44
  10.3 0.7 broadcast_in_dim.45
  11.0 0.7 fusion.25
  11.6 0.0 copy-start.4
  11.6 0.7 broadcast_bitcast_fusion
  12.4 0.6 fusion.19
  13.0 29.7 %all-gather.6.cloned.1.call-done = bf16[64,256,64]{1,2,0:T(8,128)(2,1)} async-done(((bf16[8,256,64]{1,2,0:T(8,128)(2,1)}), bf16[64,256,64]{1,2,0:T(8,128)(2,1)}) %all-gather.6.cloned.1.call-update) | async-done | bytes 2097168 | tf_op jit(solution)/shard_map/all_gather | solution.py:20
  42.7 2.2 gather_fusion
  44.8 0.1 broadcast_select_fusion
  44.9 0.0 copy-done.6
  44.9 0.0 copy-done.4
  44.9 0.0 copy-done.1
  44.9 0.5 fusion.33
  45.4 34.1 %all-gather.8.cloned.1.call-done = bf16[64,64,448]{2,1,0:T(8,128)(2,1)} async-done(((bf16[8,64,448]{2,1,0:T(8,128)(2,1)}), bf16[64,64,448]{2,1,0:T(8,128)(2,1)}) %all-gather.8.cloned.1.call-update) | async-done | bytes 3670032 | tf_op jit(solution)/shard_map/all_gather | solution.py:21
  79.5 3.7 gather_fusion.1
  83.2 0.0 copy-start.3
  83.2 1.2 bitcast_select_fusion
  84.4 0.0 copy-done
  84.4 0.7 fusion.34
  85.1 0.0 copy-done.3
  85.1 1.2 multiply_reduce_fusion
  86.4 0.0 copy-start.5
  86.4 120.4 %all-reduce.2 = (bf16[1024,64]{0,1:T(8,128)(2,1)S(1)}, bf16[1024,64]{0,1:T(8,128)(2,1)S(1)}) all-reduce(f32[1024,64]{0,1:T(8,128)} %get-tuple-element.10, f32[1024,64]{0,1:T(8,128)S(1)} %broadcast_multiply_fusion.1), channel_id=1, replica_groups=mesh['dp'=8,'mp'=32] {'mp'}, use_global_device_ids=true, to_apply=%region_1.2 | all-reduce | flops 131072 | bytes 786432 | tf_op jit(solution)/shard_map/psum | solution.py:39
  206.7 0.1 broadcast_multiply_fusion
  206.8 0.4 convolution_convert_fusion.2
  207.3 0.0 copy-done.5
  207.3 0.8 fusion.28
  208.1 1.5 copy.21
  209.6 0.0 reduce-scatter.7.cloned.1.call-update
  209.6 0.0 reduce-scatter.9.cloned.1.call-start
  209.6 0.7 fusion.4
  210.4 1.4 convolution_convert_fusion
  211.7 4.3 %copy.19 = bf16[64,64,448]{2,1,0:T(8,128)(2,1)} copy(bf16[64,64,448]{2,0,1:T(8,128)(2,1)S(1)} %convolution_convert_fusion) | data formatting | bytes 7340032
  216.1 7.5 %reshape.138 = bf16[64,28672]{1,0:T(8,128)(2,1)} reshape(bf16[64,64,448]{2,1,0:T(8,128)(2,1)} %copy.19) | data formatting | bytes 7340032
  223.5 0.0 copy-start.2
  223.5 0.0 copy-start.7
  223.5 0.0 reduce-scatter.9.cloned.1.call-update
  223.6 0.2 all-gather.4.cloned.1.call-start
  223.8 0.3 all-gather.4.cloned.1.call-update
  224.1 0.4 copy-done.2
  224.6 0.0 copy-done.7
  224.6 2.0 fusion.2
  226.6 39.1 %reduce-scatter.7.cloned.1.call-done = bf16[8,16384]{1,0:T(8,128)(2,1)} async-done(((bf16[64,16384]{1,0:T(8,128)(2,1)}), bf16[8,16384]{1,0:T(8,128)(2,1)}) %reduce-scatter.7.cloned.1.call-update) | async-done | bytes 262160
  265.7 1.0 copy.37
  266.7 0.2 copy_convert_fusion.1
  266.8 1.0 copy.14
  267.8 0.0 copy-start.8
  267.8 39.4 %reduce-scatter.9.cloned.1.call-done = bf16[8,28672]{1,0:T(8,128)(2,1)} async-done(((bf16[64,28672]{1,0:T(8,128)(2,1)}), bf16[8,28672]{1,0:T(8,128)(2,1)}) %reduce-scatter.9.cloned.1.call-update) | async-done | bytes 458768
  307.2 1.6 reshape.139
  308.8 0.3 copy_convert_fusion
  309.1 1.6 copy.15
  310.7 85.1 %all-gather.4.cloned.1.call-done = bf16[1024,8192]{1,0:T(8,128)(2,1)} async-done(((bf16[1024,256]{1,0:T(8,128)(2,1)}), bf16[1024,8192]{1,0:T(8,128)(2,1)}) %all-gather.4.cloned.1.call-update) | async-done | bytes 16777232 | tf_op jit(solution)/shard_map/all_gather | solution.py:45
  395.8 0.0 copy-done.8
  395.8 14.2 %fusion.1 = bf16[1024,448]{0,1:T(8,128)(2,1)} fusion(f32[1024,448,1]{0,1,2:T(8,128)S(1)} %copy-done.8, bf16[1024,8192]{1,0:T(8,128)(2,1)} %all-gather.4.cloned.1.call-done, bf16[8192,448]{0,1:T(8,128)(2,1)} %param.9), kind=kOutput, calls=%fused_computation.8 | convolution fusion | flops 7517569024 | bytes 26869760 | tf_op jit(solution)/shard_map/dot_general | solution.py:44
  (2 shorter events, 0.0 us)
Async XLA Ops:
  8.0 76.4 %copy-start = (bf16[1024,448]{0,1:T(8,128)(2,1)S(1)}, bf16[1024,448]{0,1:T(8,128)(2,1)}, u32[]{:S(2)}) copy-start(bf16[1024,448]{0,1:T(8,128)(2,1)} %param.8) | copy-start | bytes 2752516
  8.0 36.9 %copy-start.1 = (bf16[1024,256]{1,0:T(8,128)(2,1)S(1)}, bf16[1024,256]{1,0:T(8,128)(2,1)}, u32[]{:S(2)}) copy-start(bf16[1024,256]{1,0:T(8,128)(2,1)} %param.7) | copy-start | bytes 1572868
  8.0 34.6 %all-gather.6.cloned.1.call-start = ((), (), s32[]{:S(2)}) async-start(), calls=%async_computation.3 | async-start | bytes 2359296 | tf_op jit(solution)/shard_map/all_gather | solution.py:20
  8.8 70.8 %all-gather.8.cloned.1.call-start = ((), (), s32[]{:S(2)}) async-start(), calls=%async_computation.4 | async-start | bytes 4718592 | tf_op jit(solution)/shard_map/all_gather | solution.py:21
  9.5 256.2 %reduce-scatter.7.cloned.1.call-start = ((), (), s32[]{:S(2)}) async-start(), calls=%async_computation.5 | async-start | bytes 2359296
  10.2 34.7 %copy-start.6 = (pred[8]{0:T(512)(128)(4,1)}, pred[8]{0:T(512)(128)(4,1)S(1)}, u32[]{:S(2)}) copy-start(pred[8]{0:T(512)(128)(4,1)S(1)} %compare_and_fusion) | copy-start | bytes 28
  11.6 33.3 %copy-start.4 = (s32[1024]{0:T(1024)}, s32[1024]{0:T(1024)S(1)}, u32[]{:S(2)}) copy-start(s32[1024]{0:T(1024)S(1)} %pad_clamp_fusion) | copy-start | bytes 12292
  83.2 1.9 copy-start.3
  86.4 120.9 %copy-start.5 = (s32[1,8]{1,0:T(1,128)S(1)}, s32[1,8]{1,0:T(1,128)}, u32[]{:S(2)}) copy-start(s32[1,8]{1,0:T(1,128)} %param.12) | copy-start | bytes 100
  209.6 97.6 %reduce-scatter.9.cloned.1.call-start = ((), (), s32[]{:S(2)}) async-start(), calls=%async_computation.6 | async-start | bytes 4128768
  223.5 1.0 copy-start.2
  223.5 1.0 copy-start.7
  223.6 172.2 %all-gather.4.cloned.1.call-start = ((), (), s32[]{:S(2)}) async-start(), calls=%async_computation.2 | async-start | bytes 17301504 | tf_op jit(solution)/shard_map/all_gather | solution.py:45
  267.8 128.0 %copy-start.8 = (f32[1024,448,1]{0,1,2:T(8,128)S(1)}, f32[1024,448,1]{0,1,2:T(8,128)}, u32[]{:S(2)}) copy-start(f32[1024,448,1]{0,1,2:T(8,128)} %fusion.2) | copy-start | bytes 5505028
Sparse Core Ops, SparseCore 0:
  10.7 31.8 all-gather.5
  44.5 34.9 all-gather.7
  209.7 55.9 reduce-scatter.6
  268.1 39.0 reduce-scatter.8
Sparse Core Ops, SparseCore 1:
  226.5 169.2 all-gather.3
where the time goes:
time: 420 us; the launch traced here: 417 us
  waiting for transfers between devices  229 us (55%)
  blocking collectives  120 us (29%)
  local copies, waits for them, and re-layouts  26.2 us (6%)
  matrix products  20.8 us (5%)
  between operations  15.4 us (4%)
  other arithmetic  5.01 us (1%)
    psum x1, blocking collectives, on_device(): adapter_in = lax.psum(inputs_part, 'mp')  120 us
    all_gather x1, waiting for transfers between devices, on_device(): lax.all_gather(tokens, 'mp', axis=1, tiled=True)  85.1 us
    unnamed x7, waiting for transfers between devices  80.2 us
    all_gather x1, waiting for transfers between devices, on_device(): lax.all_gather(up_factors, 'dp', axis=0, tiled=True)  34.1 us
    all_gather x1, waiting for transfers between devices, on_device(): lax.all_gather(down_factors, 'dp', axis=0, tiled=True)  29.7 us
    unnamed x25, local copies, waits for them, and re-layouts  18.9 us
    dot_general x1, matrix products, on_device(): jnp.dot(lax.all_gather(tokens, 'mp', axis=1, tiled=True), frozen_up_weigh...  14.2 us
  transfers between devices with their start and end apart: 5, of which 5 were waited for; matrix products, arithmetic and copies ran while one was open for 7% of the time, Pallas kernels for 0%

commit v1 on v0

v1 whole, which is shorter than its diff:
```python
import functools

import jax
import jax.numpy as jnp
from jax import lax
from jax.experimental import pallas as pl
from jax.experimental.pallas import tpu as pltpu
from jax.sharding import Mesh, PartitionSpec as P

BF = jnp.bfloat16
F32 = jnp.float32
DP = ("x", "core")
MP = ("z", "y")
VMEM = pl.BlockSpec(memory_space=pltpu.VMEM)
SMEM = pl.BlockSpec(memory_space=pltpu.SMEM)
LIMIT = 40 * 1024 * 1024


def pair_of(used, group, owner, per_owner, slots):
    low, high = jnp.int32(per_owner), jnp.int32(-1)
    for slot in range(slots):
        local = used[group, slot] - owner * per_owner
        inside = jnp.logical_and(local >= 0, local < per_owner)
        low = jnp.where(inside, jnp.minimum(low, local), low)
        high = jnp.where(inside, jnp.maximum(high, local), high)
    return low, high


def place_of(used, order, sequence, per_owner, slots):
    adapter = used[0, order[0, sequence]]
    owner = lax.div(adapter, jnp.int32(per_owner))
    second = jnp.int32(0)
    for slot in range(slots):
        other = used[0, slot]
        same = jnp.logical_and(lax.div(other, jnp.int32(per_owner)) == owner, other < adapter)
        second = jnp.where(same, jnp.int32(1), second)
    return owner * 2 + second


def pick_kernel(me, used, down, up, out):
    groups, slots = used.shape
    per_owner, rank, width = down.shape
    units = up.shape[2]
    for group in range(groups):
        low, high = pair_of(used, group, me[0], per_owner, slots)
        for place, local in ((0, low), (1, high)):
            index = jnp.clip(local, 0, per_owner - 1)
            out[group, place, :, 0:width] = down[index]
            out[group, place, :, width:width + units] = up[index]
            out[group, place, :, width + units:] = jnp.zeros((rank, out.shape[3] - width - units), BF)


def parts_kernel(used, order, factors, tokens, cot, out, *, rank, width, units):
    sequences = order.shape[1]
    length = tokens.shape[0] // sequences
    per_owner = sequences
    for i in range(sequences):
        place = place_of(used, order, i, per_owner, used.shape[1])
        own = factors[place]
        rows = tokens[i * length:(i + 1) * length, :]
        inputs = lax.dot_general(
            own[:, 0:width], rows, (((1,), (1,)), ((), ())), preferred_element_type=F32
        )
        back = 2.0 * jnp.dot(
            own[:, width:width + units],
            cot[:, i * length:(i + 1) * length],
            preferred_element_type=F32,
        )
        both = jnp.concatenate([inputs, back], axis=0)
        out[i * length:(i + 1) * length, :] = both.T.astype(BF)


def grads_kernel(used, order, factors, tokens, cot, both, send, delta, *, rank, width, units):
    sequences = order.shape[1]
    length = tokens.shape[0] // sequences
    per_owner = sequences
    send[...] = jnp.zeros(send.shape, BF)
    for i in range(sequences):
        place = place_of(used, order, i, per_owner, used.shape[1])
        span = slice(i * length, (i + 1) * length)
        turned = both[span, :].astype(F32).T.astype(BF)
        inputs, back = turned[0:rank, :], turned[rank:2 * rank, :]
        term_a = jnp.dot(back, tokens[span, :], preferred_element_type=F32)
        term_b = 2.0 * lax.dot_general(
            inputs, cot[:, span], (((1,), (1,)), ((), ())), preferred_element_type=F32
        )
        send[place, :, 0:width] = term_a.astype(BF)
        send[place, :, width:width + units] = term_b.astype(BF)
        up = factors[place][:, width:width + units]
        delta[:, span] = 2.0 * lax.dot_general(
            up, inputs, (((0,), (0,)), ((), ())), preferred_element_type=F32
        )


def sum_kernel(me, used, terms, grad_a, grad_b):
    groups, slots = used.shape
    per_owner, rank, width = grad_a.shape
    units = grad_b.shape[2]
    grad_a[...] = jnp.zeros(grad_a.shape, F32)
    grad_b[...] = jnp.zeros(grad_b.shape, F32)
    for group in range(groups):
        low, high = pair_of(used, group, me[0], per_owner, slots)

        @pl.when(high >= 0)
        def _():
            for place, local in ((0, low), (1, high)):
                grad_a[local] += terms[group, place, :, 0:width].astype(F32)
                grad_b[local] += terms[group, place, :, width:width + units].astype(F32)


def call(kernel, outs, specs):
    return pl.pallas_call(
        kernel,
        out_shape=outs,
        in_specs=specs,
        out_specs=jax.tree.map(lambda _: VMEM, outs),
        compiler_params=pltpu.CompilerParams(vmem_limit_bytes=LIMIT),
    )


def hop(value, axis, step):
    n = lax.axis_size(axis)
    return lax.ppermute(value, axis, [(i, (i + step) % n) for i in range(n)])


def on_device(tokens, cotangent, weight, down, up, used, order):
    n_y, n_z = lax.axis_size("y"), lax.axis_size("z")
    owners = lax.axis_size(DP)
    members = n_y * n_z
    rows, width = tokens.shape
    units = weight.shape[1]
    per_owner, _, rank = down.shape
    packed = -(-(width + units) // 128) * 128
    me = lax.axis_index(DP)
    whole = jax.ShapeDtypeStruct

    wide_tokens = lax.all_gather(tokens, "z", axis=1, tiled=True)

    weight_t = weight.T
    piece = n_y * width
    mine = lax.dynamic_slice(weight_t, (0, me * piece), (units, piece))
    spot = lax.axis_index("y")
    pieces = [
        hop(lax.dynamic_slice(mine, (0, lax.rem(spot + n_y - r, n_y) * width), (units, width)), "y", -r)
        if r else lax.dynamic_slice(mine, (0, spot * width), (units, width))
        for r in range(n_y)
    ]
    wide_weight = lax.all_gather(jnp.stack(pieces), DP, axis=2, tiled=True)

    down_t = jnp.transpose(down, (0, 2, 1))
    used_all = lax.all_to_all(
        jnp.broadcast_to(used[None], (owners,) + used.shape), DP, 0, 0, tiled=True
    ).reshape(owners, used.shape[1])
    me_arr = me.reshape(1).astype(jnp.int32)
    picked = call(pick_kernel, whole((owners, 2, rank, packed), BF), [SMEM, SMEM, VMEM, VMEM])(
        me_arr, used_all, down_t, up
    )
    factors = lax.all_to_all(picked, DP, 0, 0, tiled=True).reshape(owners * 2, rank, packed)
    cot_t = cotangent.T
    sizes = dict(rank=rank, width=width, units=units)
    part = call(
        functools.partial(parts_kernel, **sizes),
        whole((rows, 2 * rank), BF),
        [SMEM, SMEM, VMEM, VMEM, VMEM],
    )(used, order, factors, tokens, cot_t)
    share = rows // members
    parts = lax.all_to_all(part.reshape(members, share, 2 * rank), MP, 0, 0, tiled=True)
    summed = jnp.sum(parts.astype(F32), axis=0).astype(BF)
    both = lax.all_to_all(
        jnp.broadcast_to(summed[None], (members,) + summed.shape), MP, 0, 0, tiled=True
    ).reshape(rows, 2 * rank)
    send, delta = call(
        functools.partial(grads_kernel, **sizes),
        (whole((owners * 2, rank, packed), BF), whole((units, rows), F32)),
        [SMEM, SMEM, VMEM, VMEM, VMEM, VMEM],
    )(used, order, factors, tokens, cot_t, both)
    terms = lax.all_to_all(send.reshape(owners, 2, rank, packed), DP, 0, 0, tiled=True)
    grad_a, grad_b = call(
        sum_kernel,
        (whole((per_owner, rank, width), F32), whole((per_owner, rank, units), F32)),
        [SMEM, SMEM, VMEM],
    )(me_arr, used_all, terms)

    def product(r):
        return lax.dot_general(
            wide_weight[r], wide_tokens, (((1,), (1,)), ((), ())), preferred_element_type=F32
        )

    half = units // 2
    far = product(2).astype(BF)
    far_up, far_down = hop(far[:half], "y", 1), hop(far[half:], "y", -1)
    near_up, near_down = product(1), product(n_y - 1)
    near_up = jnp.concatenate([near_up[:half] + far_up.astype(F32), near_up[half:]]).astype(BF)
    near_down = jnp.concatenate(
        [near_down[:half], near_down[half:] + far_down.astype(F32)]
    ).astype(BF)
    got_up, got_down = hop(near_up, "y", 1), hop(near_down, "y", -1)
    out = product(0) + delta + got_up.astype(F32) + got_down.astype(F32)
    return out.astype(BF).T, jnp.transpose(grad_a, (0, 2, 1)), grad_b


def solution(mesh):
    grid = Mesh(mesh.devices.reshape(4, 2, 8, 4), ("x", "core", "z", "y"))
    return jax.shard_map(
        on_device,
        mesh=grid,
        in_specs=(
            P(DP, MP),
            P(DP, MP),
            P(None, MP),
            P(DP, MP, None),
            P(DP, None, MP),
            P(DP, None),
            P(DP, None),
        ),
        out_specs=(P(DP, MP), P(DP, MP, None), P(DP, None, MP)),
        check_vma=False,
    )
```

time: 420 us -> 209 us (0.50)
  waiting for transfers between devices: 229 us -> 76.1 us
  blocking collectives: 120 us -> 71.3 us
  local copies, waits for them, and re-layouts: 26.2 us -> 4.44 us
  starting transfers between devices: 0.38 us -> 17.8 us
  Pallas kernels: 0 us -> 5.56 us
  matrix products: 20.8 us -> 15.6 us
    psum x1 -> x0, blocking collectives: 120 us -> none  [on_device(): adapter_in = lax.psum(inputs_part, 'mp')]
    all_gather x3 -> x2, waiting for transfers between devices: 149 us -> 40.4 us  [the longest x1 40.4 us: on_device(): wide_weight = lax.all_gather(jnp.stack(pieces), DP, axis=2, tiled=True)]
    unnamed x7 -> x2, waiting for transfers between devices: 80.2 us -> 0.7 us
    all_to_all x0 -> x4, blocking collectives: none -> 71.3 us  [the longest x1 24 us: on_device(): lax.all_to_all(picked, DP, 0, 0, tiled=True)]
    ppermute x0 -> x7, waiting for transfers between devices: none -> 34.9 us  [hop(): return lax.ppermute(value, axis, [(i, (i + step) % n) for i in range(n)])]
    unnamed x25 -> x22, local copies, waits for them, and re-layouts: 18.9 us -> 2.52 us
    ppermute x0 -> x7, starting transfers between devices: none -> 10.9 us  [hop(): return lax.ppermute(value, axis, [(i, (i + step) % n) for i in range(n)])]
    all_to_all x0 -> x1, starting transfers between devices: none -> 6.79 us  [on_device(): lax.all_to_all(send.reshape(owners, 2, rank, packed), DP, 0, 0, tiled=True)]
  transfers between devices with their start and end apart: 5 -> 10, of which waited for: 5 -> 7; matrix products, arithmetic and copies ran while one was open for 7% -> 7% of each run, Pallas kernels for 0% -> 3%
where the time goes in v1:
time: 209 us; the launch traced here: 208 us
  waiting for transfers between devices  76.1 us (36%)
  blocking collectives  71.3 us (34%)
  starting transfers between devices  17.8 us (9%)
  matrix products  15.6 us (7%)
  between operations  14.3 us (7%)
  Pallas kernels  5.56 us (3%)
  local copies, waits for them, and re-layouts  4.44 us (2%)
  other arithmetic  3.29 us (2%)
    all_gather x1, waiting for transfers between devices, on_device(): wide_weight = lax.all_gather(jnp.stack(pieces), DP, axis=2, tiled=True)  40.4 us
    ppermute x7, waiting for transfers between devices, hop(): return lax.ppermute(value, axis, [(i, (i + step) % n) for i in range(n)])  34.9 us
    all_to_all x1, blocking collectives, on_device(): lax.all_to_all(picked, DP, 0, 0, tiled=True)  24 us
    all_to_all x1, blocking collectives, on_device(): lax.all_to_all(part.reshape(members, share, 2 * rank), MP, 0, 0, tiled=True)  19.8 us
    all_to_all x1, blocking collectives, on_device(): lax.all_to_all(jnp.broadcast_to(summed[None], (members,) + summed.shape),...  15.9 us
    dot_general x4, matrix products, product(): lax.dot_general(wide_weight[r], wide_tokens, (((1,), (1,)), ((), ())), pr...  15.6 us
    all_to_all x1, blocking collectives, on_device(): lax.all_to_all(jnp.broadcast_to(used[None], (owners,) + used.shape), DP,...  11.6 us
    ppermute x7, starting transfers between devices, hop(): return lax.ppermute(value, axis, [(i, (i + step) % n) for i in range(n)])  10.9 us
  transfers between devices with their start and end apart: 10, of which 7 were waited for; matrix products, arithmetic and copies ran while one was open for 7% of the time, Pallas kernels for 3%

profile of v1, /device:TPU:1, one launch (start us, length us, event | category | flops | bytes accessed | tf_op | source)
XLA Modules:
  0.0 208.3 jit_solution(13229860660922398743)
XLA Ops:
  7.2 0.0 all-gather.5.cloned.1.call-start
  7.2 0.7 all-gather.5.cloned.1.call-update
  7.9 0.0 all-gather.3.cloned.1.call-start
  8.0 1.7 dynamic-slice_bitcast_fusion.3
  9.7 0.0 copy-start.5
  9.7 0.0 copy-start.3
  9.7 0.0 copy-start.4
  9.7 3.6 %collective-permute-start = (bf16[448,256]{1,0:T(8,128)(2,1)S(1)}, bf16[448,256]{1,0:T(8,128)(2,1)S(1)}, u32[]{:S(2)}, u32[]{:S(2)}) collective-permute-start(bf16[448,256]{1,0:T(8,128)(2,1)S(1)} %get-tuple-element.12), channel_id=1, source_target_pairs={{0,3},{1,0},{2,1},{3,2},{4,7},{5,4},{6,5},{7,6},{8,11},{9,8},{10,9... | collective-permute-start | bytes 688136 | tf_op jit(solution)/shard_map/ppermute | solution.py:123
  13.4 0.0 collective-permute-start.2
  13.4 1.6 collective-permute-start.1
  15.0 2.8 %collective-permute-done = bf16[448,256]{1,0:T(8,128)(2,1)S(1)} collective-permute-done((bf16[448,256]{1,0:T(8,128)(2,1)S(1)}, bf16[448,256]{1,0:T(8,128)(2,1)S(1)}, u32[]{:S(2)}, u32[]{:S(2)}) %collective-permute-start) | collective-permute-done | bytes 229408 | tf_op jit(solution)/shard_map/ppermute | solution.py:123
  17.8 3.9 %collective-permute-done.2 = bf16[448,256]{1,0:T(8,128)(2,1)S(1)} collective-permute-done((bf16[448,256]{1,0:T(8,128)(2,1)S(1)}, bf16[448,256]{1,0:T(8,128)(2,1)S(1)}, u32[]{:S(2)}, u32[]{:S(2)}) %collective-permute-start.2) | collective-permute-done | bytes 229408 | tf_op jit(solution)/shard_map/ppermute | solution.py:123
  21.7 3.0 %collective-permute-done.1 = bf16[448,256]{1,0:T(8,128)(2,1)S(1)} collective-permute-done((bf16[448,256]{1,0:T(8,128)(2,1)S(1)}, bf16[448,256]{1,0:T(8,128)(2,1)S(1)}, u32[]{:S(2)}, u32[]{:S(2)}) %collective-permute-start.1) | collective-permute-done | bytes 229408 | tf_op jit(solution)/shard_map/ppermute | solution.py:123
  24.7 1.0 pad_maximum_fusion
  25.7 0.0 all-gather.3.cloned.1.call-update
  25.7 0.0 copy-done.5
  25.7 11.6 %all_to_all.25 = s32[8,1,8]{2,1,0:T(1,128)S(1)} all-to-all(s32[8,1,8]{2,1,0:T(1,128)S(1)} %broadcast_in_dim.7), channel_id=1, replica_groups=mesh['x'=4,'core'=2,'z'=8,'y'=4] {'x','core'}, dimensions={0} | all-to-all | bytes 512 | tf_op jit(solution)/shard_map/all_to_all | solution.py:151
  37.3 0.0 copy-done.3
  37.3 0.0 copy-done.4
  37.3 0.9 shard_map.94
  38.2 0.0 copy-start
  38.2 0.0 copy-start.1
  38.2 0.0 copy-start.6
  38.2 24.0 %all_to_all.26 = bf16[8,2,64,768]{3,2,1,0:T(8,128)(2,1)S(1)} all-to-all(bf16[8,2,64,768]{3,2,1,0:T(8,128)(2,1)S(1)} %shard_map.94), channel_id=1, replica_groups=mesh['x'=4,'core'=2,'z'=8,'y'=4] {'x','core'}, dimensions={0} | all-to-all | bytes 3145728 | tf_op jit(solution)/shard_map/all_to_all | solution.py:158
  62.3 0.0 copy-done
  62.3 0.0 copy-done.1
  62.3 0.0 copy-done.6
  62.3 1.1 shard_map.95
  63.4 19.8 %all_to_all.27 = bf16[32,32,128]{2,1,0:T(8,128)(2,1)S(1)} all-to-all(bf16[32,32,128]{2,1,0:T(8,128)(2,1)S(1)} %bitcast.53), channel_id=1, replica_groups=mesh['x'=4,'core'=2,'z'=8,'y'=4] {'z','y'}, dimensions={0} | all-to-all | bytes 524288 | tf_op jit(solution)/shard_map/all_to_all | solution.py:167
  83.3 0.1 reduce_sum.12
  83.4 15.9 %all_to_all.28 = bf16[32,32,128]{2,1,0:T(8,128)(2,1)S(1)} all-to-all(bf16[32,32,128]{2,1,0:T(8,128)(2,1)S(1)} %broadcast_in_dim.16), channel_id=1, replica_groups=mesh['x'=4,'core'=2,'z'=8,'y'=4] {'z','y'}, dimensions={0} | all-to-all | bytes 524288 | tf_op jit(solution)/shard_map/all_to_all | solution.py:169
  99.3 1.4 shard_map.96
  100.6 0.0 copy-start.2
  100.7 1.1 copy-done.2
  101.8 0.0 copy-start.7
  101.8 1.3 copy-done.7
  103.1 6.8 %all-to-all-start.4 = ((bf16[8,2,64,768]{3,2,1,0:T(8,128)(2,1)}), bf16[8,2,64,768]{3,2,1,0:T(8,128)(2,1)S(1)}, u32[]{:S(2)}, u32[]{:S(2)}) async-start(bf16[8,2,64,768]{3,2,1,0:T(8,128)(2,1)} %bitcast.51), calls=%async_computation.4 | async-start | bytes 3145728 | tf_op jit(solution)/shard_map/all_to_all | solution.py:177
  109.9 0.0 all-gather.5.cloned.1.call-done
  109.9 40.4 %all-gather.3.cloned.1.call-done = bf16[4,448,2048]{2,1,0:T(8,128)(2,1)} async-done(((bf16[4,448,256]{2,1,0:T(8,128)(2,1)}), bf16[4,448,2048]{2,1,0:T(8,128)(2,1)}) %all-gather.3.cloned.1.call-update) | async-done | bytes 7340048 | tf_op jit(solution)/shard_map/all_gather | solution.py:148
  150.4 5.0 %fusion.4 = bf16[448,1024]{1,0:T(8,128)(2,1)S(1)} fusion(bf16[1024,2048]{1,0:T(8,128)(2,1)} %all-gather.5.cloned.1.call-done, bf16[4,448,2048]{2,1,0:T(8,128)(2,1)} %all-gather.3.cloned.1.call-done), kind=kOutput, calls=%fused_computation.9 | convolution fusion | flops 1879506944 | bytes 6946816 | tf_op jit(solution)/shard_map/dot_general | solution.py:185
  155.3 0.1 fusion.8
  155.4 1.3 collective-permute-start.3
  156.7 1.5 collective-permute-start.5
  158.2 0.0 copy-done.9
  158.2 0.0 copy-done.10
  158.2 2.1 %fusion = f32[448,1024]{1,0:T(8,128)S(1)} fusion(bf16[1024,2048]{1,0:T(8,128)(2,1)S(1)} %copy-done.10, bf16[4,448,2048]{2,1,0:T(8,128)(2,1)S(1)} %copy-done.9), kind=kOutput, calls=%fused_computation.1 | convolution fusion | flops 1879048192 | bytes 7864320 | tf_op jit(solution)/shard_map/dot_general | solution.py:185
  160.3 2.1 %fusion.2 = f32[448,1024]{1,0:T(8,128)S(1)} fusion(bf16[1024,2048]{1,0:T(8,128)(2,1)S(1)} %copy-done.10, bf16[4,448,2048]{2,1,0:T(8,128)(2,1)S(1)} %copy-done.9), kind=kOutput, calls=%fused_computation.5 | convolution fusion | flops 1879048192 | bytes 7864320 | tf_op jit(solution)/shard_map/dot_general | solution.py:185
  162.4 0.1 slice.74
  162.5 0.1 slice.75
  162.6 5.7 %collective-permute-done.5 = bf16[224,1024]{1,0:T(8,128)(2,1)S(1)} collective-permute-done((bf16[224,1024]{1,0:T(8,128)(2,1)S(1)}, bf16[224,1024]{1,0:T(8,128)(2,1)S(1)}, u32[]{:S(2)}, u32[]{:S(2)}) %collective-permute-start.5) | collective-permute-done | bytes 458784 | tf_op jit(solution)/shard_map/ppermute | solution.py:123
  168.2 0.1 fusion.6
  168.4 1.0 pad_maximum_fusion.2
  169.3 2.8 %collective-permute-start.6 = (bf16[448,1024]{1,0:T(8,128)(2,1)}, bf16[448,1024]{1,0:T(8,128)(2,1)}, u32[]{:S(2)}, u32[]{:S(2)}) collective-permute-start(bf16[448,1024]{1,0:T(8,128)(2,1)} %pad_maximum_fusion.2), channel_id=1, source_target_pairs={{0,3},{1,0},{2,1},{3,2},{4,7},{5,4},{6,5},{7,6},{8,11},{9,8},{10,9... | collective-permute-start | bytes 2752520 | tf_op jit(solution)/shard_map/ppermute | solution.py:123
  172.2 0.0 collective-permute-done.3
  172.2 0.1 fusion.7
  172.3 0.0 copy-start.8
  172.3 1.0 pad_maximum_fusion.1
  173.3 0.0 collective-permute-start.4
  173.3 0.0 all-to-all-done.4.terms
  173.3 2.2 %shard_map.97 = (f32[8,64,256]{2,1,0:T(8,128)}, f32[8,64,448]{2,1,0:T(8,128)}) custom-call(s32[1]{0:T(128)} %bitcast.9.me, s32[8,8]{1,0:T(8,128)S(1)} %bitcast.56, bf16[8,2,64,768]{3,2,1,0:T(8,128)(2,1)S(1)} %all-to-all-done.4.terms), custom_call_target="tpu_custom_call" | custom-call | tf_op jit(solution)/shard_map/pallas_call | solution.py:178
  175.4 15.3 %collective-permute-done.6 = bf16[448,1024]{1,0:T(8,128)(2,1)} collective-permute-done((bf16[448,1024]{1,0:T(8,128)(2,1)}, bf16[448,1024]{1,0:T(8,128)(2,1)}, u32[]{:S(2)}, u32[]{:S(2)}) %collective-permute-start.6) | collective-permute-done | bytes 917536 | tf_op jit(solution)/shard_map/ppermute | solution.py:123
  190.8 4.3 %collective-permute-done.4 = bf16[448,1024]{1,0:T(8,128)(2,1)} collective-permute-done((bf16[448,1024]{1,0:T(8,128)(2,1)}, bf16[448,1024]{1,0:T(8,128)(2,1)}, u32[]{:S(2)}, u32[]{:S(2)}) %collective-permute-start.4) | collective-permute-done | bytes 917536 | tf_op jit(solution)/shard_map/ppermute | solution.py:123
  195.0 0.0 copy-done.8
  195.1 6.4 %fusion.5 = bf16[1024,448]{0,1:T(8,128)(2,1)} fusion(bf16[448,1024]{1,0:T(8,128)(2,1)} %collective-permute-done.6, bf16[448,1024]{1,0:T(8,128)(2,1)} %collective-permute-done.4, f32[448,1024]{1,0:T(8,128)S(1)} %copy-done.8, bf16[1024,2048]{1,0:T(8,128)(2,1)} %all-gather.5.cloned.1.call-done, bf16[4,448,2048]{2,1,0:T(8,128)(2,1)} %all-gather.3.cloned.1.call-done), kind=kOutput, calls=%fused_computation.10 | convolution fusion | flops 1881800704 | bytes 10616832 | tf_op jit(solution)/shard_map/dot_general | solution.py:185
  (4 shorter events, 0.0 us)
Async XLA Ops:
  7.2 102.8 %all-gather.5.cloned.1.call-start = ((), (), s32[]{:S(2)}) async-start(), calls=%async_computation.6 | async-start | bytes 4718592 | tf_op jit(solution)/shard_map/all_gather | solution.py:137
  7.9 142.5 %all-gather.3.cloned.1.call-start = ((), (), s32[]{:S(2)}) async-start(), calls=%async_computation.5 | async-start | bytes 8257536 | tf_op jit(solution)/shard_map/all_gather | solution.py:148
  9.7 16.0 %copy-start.5 = (s32[1,8]{1,0:T(1,128)S(1)}, s32[1,8]{1,0:T(1,128)}, u32[]{:S(2)}) copy-start(s32[1,8]{1,0:T(1,128)} %used.3) | copy-start | bytes 100
  9.7 27.6 %copy-start.3 = (bf16[8,64,448]{2,1,0:T(8,128)(2,1)S(1)}, bf16[8,64,448]{2,1,0:T(8,128)(2,1)}, u32[]{:S(2)}) copy-start(bf16[8,64,448]{2,1,0:T(8,128)(2,1)} %up.1) | copy-start | bytes 1376260
  9.7 27.6 %copy-start.4 = (bf16[8,256,64]{1,2,0:T(8,128)(2,1)S(1)}, bf16[8,256,64]{1,2,0:T(8,128)(2,1)}, u32[]{:S(2)}) copy-start(bf16[8,256,64]{1,2,0:T(8,128)(2,1)} %param.10) | copy-start | bytes 786436
  9.7 8.1 %collective-permute-start = (bf16[448,256]{1,0:T(8,128)(2,1)S(1)}, bf16[448,256]{1,0:T(8,128)(2,1)S(1)}, u32[]{:S(2)}, u32[]{:S(2)}) collective-permute-start(bf16[448,256]{1,0:T(8,128)(2,1)S(1)} %get-tuple-element.12), channel_id=1, source_target_pairs={{0,3},{1,0},{2,1},{3,2},{4,7},{5,4},{6,5},{7,6},{8,11},{9,8},{10,9... | collective-permute-start | bytes 688136 | tf_op jit(solution)/shard_map/ppermute | solution.py:123
  13.4 8.3 %collective-permute-start.2 = (bf16[448,256]{1,0:T(8,128)(2,1)S(1)}, bf16[448,256]{1,0:T(8,128)(2,1)S(1)}, u32[]{:S(2)}, u32[]{:S(2)}) collective-permute-start(bf16[448,256]{1,0:T(8,128)(2,1)S(1)} %get-tuple-element.13), channel_id=1, source_target_pairs={{0,1},{1,2},{2,3},{3,0},{4,5},{5,6},{6,7},{7,4},{8,9},{9,10},{10,1... | collective-permute-start | bytes 688136 | tf_op jit(solution)/shard_map/ppermute | solution.py:123
  13.4 11.3 %collective-permute-start.1 = (bf16[448,256]{1,0:T(8,128)(2,1)S(1)}, bf16[448,256]{1,0:T(8,128)(2,1)S(1)}, u32[]{:S(2)}, u32[]{:S(2)}) collective-permute-start(bf16[448,256]{1,0:T(8,128)(2,1)S(1)} %get-tuple-element.14), channel_id=1, source_target_pairs={{0,2},{1,3},{2,0},{3,1},{4,6},{5,7},{6,4},{7,5},{8,10},{9,11},{10,... | collective-permute-start | bytes 688136 | tf_op jit(solution)/shard_map/ppermute | solution.py:123
  38.2 24.1 %copy-start = (bf16[1024,256]{1,0:T(8,128)(2,1)S(1)}, bf16[1024,256]{1,0:T(8,128)(2,1)}, u32[]{:S(2)}) copy-start(bf16[1024,256]{1,0:T(8,128)(2,1)} %tokens.3) | copy-start | bytes 1572868
  38.2 24.1 %copy-start.1 = (bf16[1024,448]{0,1:T(8,128)(2,1)S(1)}, bf16[1024,448]{0,1:T(8,128)(2,1)}, u32[]{:S(2)}) copy-start(bf16[1024,448]{0,1:T(8,128)(2,1)} %param.8) | copy-start | bytes 2752516
  38.2 24.0 %copy-start.6 = (s32[1,8]{1,0:T(1,128)S(1)}, s32[1,8]{1,0:T(1,128)}, u32[]{:S(2)}) copy-start(s32[1,8]{1,0:T(1,128)} %order.3) | copy-start | bytes 100
  100.6 1.1 copy-start.2
  101.8 1.3 copy-start.7
  103.1 70.2 %all-to-all-start.4 = ((bf16[8,2,64,768]{3,2,1,0:T(8,128)(2,1)}), bf16[8,2,64,768]{3,2,1,0:T(8,128)(2,1)S(1)}, u32[]{:S(2)}, u32[]{:S(2)}) async-start(bf16[8,2,64,768]{3,2,1,0:T(8,128)(2,1)} %bitcast.51), calls=%async_computation.4 | async-start | bytes 3145728 | tf_op jit(solution)/shard_map/all_to_all | solution.py:177
  150.4 7.9 %copy-start.9 = (bf16[4,448,2048]{2,1,0:T(8,128)(2,1)S(1)}, bf16[4,448,2048]{2,1,0:T(8,128)(2,1)}, u32[]{:S(2)}) copy-start(bf16[4,448,2048]{2,1,0:T(8,128)(2,1)} %all-gather.3.cloned.1.call-done) | copy-start | bytes 22020100
  150.4 7.9 %copy-start.10 = (bf16[1024,2048]{1,0:T(8,128)(2,1)S(1)}, bf16[1024,2048]{1,0:T(8,128)(2,1)}, u32[]{:S(2)}) copy-start(bf16[1024,2048]{1,0:T(8,128)(2,1)} %all-gather.5.cloned.1.call-done) | copy-start | bytes 12582916
  155.4 16.7 %collective-permute-start.3 = (bf16[224,1024]{1,0:T(8,128)(2,1)S(1)}, bf16[224,1024]{1,0:T(8,128)(2,1)S(1)}, u32[]{:S(2)}, u32[]{:S(2)}) collective-permute-start(bf16[224,1024]{1,0:T(8,128)(2,1)S(1)} %get-tuple-element.15), channel_id=1, source_target_pairs={{0,1},{1,2},{2,3},{3,0},{4,5},{5,6},{6,7},{7,4},{8,9},{9,10},{10,1... | collective-permute-start | bytes 1376264 | tf_op jit(solution)/shard_map/ppermute | solution.py:123
  156.7 11.5 %collective-permute-start.5 = (bf16[224,1024]{1,0:T(8,128)(2,1)S(1)}, bf16[224,1024]{1,0:T(8,128)(2,1)S(1)}, u32[]{:S(2)}, u32[]{:S(2)}) collective-permute-start(bf16[224,1024]{1,0:T(8,128)(2,1)S(1)} %get-tuple-element.16), channel_id=1, source_target_pairs={{0,3},{1,0},{2,1},{3,2},{4,7},{5,4},{6,5},{7,6},{8,11},{9,8},{10,9... | collective-permute-start | bytes 1376264 | tf_op jit(solution)/shard_map/ppermute | solution.py:123
  169.3 21.4 %collective-permute-start.6 = (bf16[448,1024]{1,0:T(8,128)(2,1)}, bf16[448,1024]{1,0:T(8,128)(2,1)}, u32[]{:S(2)}, u32[]{:S(2)}) collective-permute-start(bf16[448,1024]{1,0:T(8,128)(2,1)} %pad_maximum_fusion.2), channel_id=1, source_target_pairs={{0,3},{1,0},{2,1},{3,2},{4,7},{5,4},{6,5},{7,6},{8,11},{9,8},{10,9... | collective-permute-start | bytes 2752520 | tf_op jit(solution)/shard_map/ppermute | solution.py:123
  172.3 22.8 %copy-start.8 = (f32[448,1024]{1,0:T(8,128)S(1)}, f32[448,1024]{1,0:T(8,128)}, u32[]{:S(2)}) copy-start(f32[448,1024]{1,0:T(8,128)} %copy-done.7) | copy-start | bytes 5505028
  173.3 21.8 %collective-permute-start.4 = (bf16[448,1024]{1,0:T(8,128)(2,1)}, bf16[448,1024]{1,0:T(8,128)(2,1)}, u32[]{:S(2)}, u32[]{:S(2)}) collective-permute-start(bf16[448,1024]{1,0:T(8,128)(2,1)} %pad_maximum_fusion.1), channel_id=1, source_target_pairs={{0,1},{1,2},{2,3},{3,0},{4,5},{5,6},{6,7},{7,4},{8,9},{9,10},{10,1... | collective-permute-start | bytes 2752520 | tf_op jit(solution)/shard_map/ppermute | solution.py:123
Sparse Core Ops, SparseCore 0:
  9.7 63.3 all-gather.4
  75.5 74.8 all-gather.2

commit v2 on v1

--- a/solution.py
+++ b/solution.py
@@ -108,6 +108,19 @@
                 grad_b[local] += terms[group, place, :, width:width + units].astype(F32)
 
 
+def place_kernel(me, *refs):
+    out = refs[-1]
+    width = refs[0].shape[2]
+    mid = refs[0].shape[0] // 2
+    x, core = lax.div(me[0], jnp.int32(2)), lax.rem(me[0], jnp.int32(2))
+    for other in range(2):
+        for piece, step, start in ((0, 0, 0), (1, 3, 0), (2, 1, 0), (3, 2, 0), (4, 2, mid)):
+            source = refs[5 * other + piece]
+            block = 2 * lax.rem(x + step, jnp.int32(4)) + (1 - core if other else core)
+            spot = pl.ds(pl.multiple_of(block * width, width), width)
+            out[start:start + source.shape[0], :, spot] = source[...]
+
+
 def call(kernel, outs, specs):
     return pl.pallas_call(
         kernel,
@@ -145,13 +158,21 @@
         if r else lax.dynamic_slice(mine, (0, spot * width), (units, width))
         for r in range(n_y)
     ]
-    wide_weight = lax.all_gather(jnp.stack(pieces), DP, axis=2, tiled=True)
+    own = jnp.stack(pieces)
+    from_left, from_right = hop(own, "x", 1), hop(own, "x", -1)
+    mid = n_y // 2
+    far_left, far_right = hop(from_left[:mid], "x", 1), hop(from_right[mid:], "x", -1)
+    held = (own, from_left, from_right, far_left, far_right)
+    swapped = tuple(hop(piece, "core", 1) for piece in held)
+    me_arr = me.reshape(1).astype(jnp.int32)
+    wide_weight = call(
+        place_kernel, whole((n_y, units, n_z * width), BF), [SMEM] + [VMEM] * 10
+    )(me_arr, *held, *swapped)
 
     down_t = jnp.transpose(down, (0, 2, 1))
     used_all = lax.all_to_all(
         jnp.broadcast_to(used[None], (owners,) + used.shape), DP, 0, 0, tiled=True
     ).reshape(owners, used.shape[1])
-    me_arr = me.reshape(1).astype(jnp.int32)
     picked = call(pick_kernel, whole((owners, 2, rank, packed), BF), [SMEM, SMEM, VMEM, VMEM])(
         me_arr, used_all, down_t, up
     )

time: 209 us -> 168 us (0.80)
  blocking collectives: 71.3 us -> 0 us
  starting transfers between devices: 17.8 us -> 55.1 us
  waiting for transfers between devices: 76.1 us -> 46.8 us
  local copies, waits for them, and re-layouts: 4.44 us -> 14.4 us
  Pallas kernels: 5.56 us -> 14.1 us
  matrix products: 15.6 us -> 18.6 us
    all_to_all x4 -> x0, blocking collectives: 71.3 us -> none  [the longest x1 24 us: on_device(): lax.all_to_all(picked, DP, 0, 0, tiled=True)]
    all_gather x1 -> x0, waiting for transfers between devices: 40.4 us -> none  [on_device(): wide_weight = lax.all_gather(jnp.stack(pieces), DP, axis=2, tiled=True)]
    all_to_all x0 -> x4, starting transfers between devices: none -> 30.7 us  [the longest x1 10.4 us: on_device(): lax.all_to_all(part.reshape(members, share, 2 * rank), MP, 0, 0, tiled=True)]
    ppermute x7 -> x16, starting transfers between devices: 10.9 us -> 18.6 us  [hop(): return lax.ppermute(value, axis, [(i, (i + step) % n) for i in range(n)])]
    pallas_call x0 -> x1, Pallas kernels: none -> 6.51 us  [on_device(): call(place_kernel, whole((n_y, units, n_z * width), BF), [SMEM] + [VMEM]...]
    all_to_all x0 -> x4, waiting for transfers between devices: none -> 6.28 us  [the longest x1 4.52 us: on_device(): lax.all_to_all(jnp.broadcast_to(used[None], (owners,) + used.shape), DP,...]
    ppermute x7 -> x16, waiting for transfers between devices: 34.9 us -> 39.8 us  [hop(): return lax.ppermute(value, axis, [(i, (i + step) % n) for i in range(n)])]
    unnamed x22, local copies, waits for them, and re-layouts: 2.52 us -> 6.84 us
  transfers between devices with their start and end apart: 10 -> 22, of which waited for: 7 -> 11; matrix products, arithmetic and copies ran while one was open for 7% -> 13% of each run, Pallas kernels for 3% -> 9%
where the time goes in v2:
time: 168 us; the launch traced here: 165 us
  starting transfers between devices  55.1 us (33%)
  waiting for transfers between devices  46.8 us (28%)
  matrix products  18.6 us (11%)
  local copies, waits for them, and re-layouts  14.4 us (9%)
  between operations  14.2 us (8%)
  Pallas kernels  14.1 us (8%)
  other arithmetic  2.36 us (1%)
    ppermute x16, waiting for transfers between devices, hop(): return lax.ppermute(value, axis, [(i, (i + step) % n) for i in range(n)])  39.8 us
    dot_general x4, matrix products, product(): lax.dot_general(wide_weight[r], wide_tokens, (((1,), (1,)), ((), ())), pr...  18.6 us
    ppermute x16, starting transfers between devices, hop(): return lax.ppermute(value, axis, [(i, (i + step) % n) for i in range(n)])  18.6 us
    all_to_all x1, starting transfers between devices, on_device(): lax.all_to_all(part.reshape(members, share, 2 * rank), MP, 0, 0, tiled=True)  10.4 us
    all_to_all x1, starting transfers between devices, on_device(): lax.all_to_all(jnp.broadcast_to(summed[None], (members,) + summed.shape),...  9.68 us
    unnamed x22, local copies, waits for them, and re-layouts  6.84 us
    pallas_call x1, Pallas kernels, on_device(): call(place_kernel, whole((n_y, units, n_z * width), BF), [SMEM] + [VMEM]...  6.51 us
    all_to_all x1, starting transfers between devices, on_device(): lax.all_to_all(jnp.broadcast_to(used[None], (owners,) + used.shape), DP,...  6.45 us
  transfers between devices with their start and end apart: 22, of which 11 were waited for; matrix products, arithmetic and copies ran while one was open for 13% of the time, Pallas kernels for 9%

profile of v2, /device:TPU:1, one launch (start us, length us, event | category | flops | bytes accessed | tf_op | source)
XLA Modules:
  0.0 165.5 jit_solution(5347194343777376457)
XLA Ops:
  7.2 0.0 all-gather.2.cloned.1.call-start
  7.2 0.7 all-gather.2.cloned.1.call-update
  7.9 1.3 broadcast_in_dim.7
  9.2 6.5 %all-to-all-start = ((s32[8,1,8]{2,1,0:T(1,128)}), s32[8,1,8]{2,1,0:T(1,128)S(1)}, u32[]{:S(2)}, u32[]{:S(2)}) async-start(s32[8,1,8]{2,1,0:T(1,128)} %broadcast_in_dim.7), calls=%async_computation | async-start | bytes 8192 | tf_op jit(solution)/shard_map/all_to_all | solution.py:173
  15.6 4.5 %all-to-all-done = s32[8,1,8]{2,1,0:T(1,128)S(1)} async-done(((s32[8,1,8]{2,1,0:T(1,128)}), s32[8,1,8]{2,1,0:T(1,128)S(1)}, u32[]{:S(2)}, u32[]{:S(2)}) %all-to-all-start) | async-done | bytes 288 | tf_op jit(solution)/shard_map/all_to_all | solution.py:173
  20.1 1.0 copy-done.4
  21.2 0.9 copy-done.5
  22.1 2.1 %shard_map.95 = bf16[8,2,64,768]{3,2,1,0:T(8,128)(2,1)} custom-call(s32[1]{0:T(128)} %bitcast.me, s32[8,8]{1,0:T(8,128)S(1)} %bitcast.54, bf16[8,64,256]{2,1,0:T(8,128)(2,1)S(1)} %bitcast.53, bf16[8,64,448]{2,1,0:T(8,128)(2,1)S(1)} %copy-done.4), custom_call_target="tpu_custom_call" | custom-call | tf_op jit(solution)/shard_map/pallas_call | solution.py:176
  24.2 4.2 %all-to-all-start.1 = ((bf16[8,2,64,768]{3,2,1,0:T(8,128)(2,1)}), bf16[8,2,64,768]{3,2,1,0:T(8,128)(2,1)S(1)}, u32[]{:S(2)}, u32[]{:S(2)}) async-start(bf16[8,2,64,768]{3,2,1,0:T(8,128)(2,1)} %shard_map.95), calls=%async_computation.1 | async-start | bytes 3145728 | tf_op jit(solution)/shard_map/all_to_all | solution.py:179
  28.4 1.7 %dynamic-slice_bitcast_fusion.3 = (bf16[1,448,256]{2,1,0:T(8,128)(2,1)S(1)}, bf16[448,256]{1,0:T(8,128)(2,1)S(1)}, bf16[448,256]{1,0:T(8,128)(2,1)S(1)}, bf16[448,256]{1,0:T(8,128)(2,1)S(1)}) fusion(bf16[8192,448]{0,1:T(8,128)(2,1)} %param.9, s32[]{:T(128)S(6)} %add.64, s32[]{:T(128)S(6)} %add.66, s32[]{:T(128)S(6)} %add.70, s32[]{:T(128)S(6)} %add.68), kind=kLoop, calls=%fused_computation.23 | loop fusion | bytes 1835024 | tf_op jit(solution)/shard_map/stack | solution.py:161
  30.1 2.1 %collective-permute-start = (bf16[448,256]{1,0:T(8,128)(2,1)S(1)}, bf16[448,256]{1,0:T(8,128)(2,1)S(1)}, u32[]{:S(2)}, u32[]{:S(2)}) collective-permute-start(bf16[448,256]{1,0:T(8,128)(2,1)S(1)} %get-tuple-element.12), channel_id=1, source_target_pairs={{0,3},{1,0},{2,1},{3,2},{4,7},{5,4},{6,5},{7,6},{8,11},{9,8},{10,9... | collective-permute-start | bytes 688136 | tf_op jit(solution)/shard_map/ppermute | solution.py:136
  32.3 0.3 collective-permute-start.1
  32.6 0.7 collective-permute-start.2
  33.3 4.2 %collective-permute-done = bf16[448,256]{1,0:T(8,128)(2,1)S(1)} collective-permute-done((bf16[448,256]{1,0:T(8,128)(2,1)S(1)}, bf16[448,256]{1,0:T(8,128)(2,1)S(1)}, u32[]{:S(2)}, u32[]{:S(2)}) %collective-permute-start) | collective-permute-done | bytes 229408 | tf_op jit(solution)/shard_map/ppermute | solution.py:136
  37.5 3.1 %collective-permute-done.1 = bf16[448,256]{1,0:T(8,128)(2,1)S(1)} collective-permute-done((bf16[448,256]{1,0:T(8,128)(2,1)S(1)}, bf16[448,256]{1,0:T(8,128)(2,1)S(1)}, u32[]{:S(2)}, u32[]{:S(2)}) %collective-permute-start.1) | collective-permute-done | bytes 229408 | tf_op jit(solution)/shard_map/ppermute | solution.py:136
  40.6 5.8 %collective-permute-done.2 = bf16[448,256]{1,0:T(8,128)(2,1)S(1)} collective-permute-done((bf16[448,256]{1,0:T(8,128)(2,1)S(1)}, bf16[448,256]{1,0:T(8,128)(2,1)S(1)}, u32[]{:S(2)}, u32[]{:S(2)}) %collective-permute-start.2) | collective-permute-done | bytes 229408 | tf_op jit(solution)/shard_map/ppermute | solution.py:136
  46.3 0.1 pad_maximum_fusion.refs_0_
  46.4 1.5 collective-permute-start.3
  47.9 1.3 collective-permute-start.4
  49.3 0.0 copy-start.1
  49.3 1.2 copy-done.1
  50.5 1.8 %shard_map.96 = bf16[1024,128]{1,0:T(8,128)(2,1)} custom-call(s32[1,8]{1,0:T(1,128)S(1)} %copy-done.6, s32[1,8]{1,0:T(1,128)S(1)} %copy-done.7, bf16[16,64,768]{2,1,0:T(8,128)(2,1)S(1)} %bitcast.47, bf16[1024,256]{1,0:T(8,128)(2,1)S(1)} %copy-done, bf16[448,1024]{1,0:T(8,128)(2,1)S(1)} %bitcast.49), custom_call_target="tpu_custom_call" | custom-call | tf_op jit(solution)/shard_map/pallas_call | solution.py:182
  52.3 10.4 %all-to-all-start.2 = ((bf16[32,32,128]{2,1,0:T(8,128)(2,1)}), bf16[32,32,128]{2,1,0:T(8,128)(2,1)S(1)}, u32[]{:S(2)}, u32[]{:S(2)}) async-start(bf16[32,32,128]{2,1,0:T(8,128)(2,1)} %bitcast.15), calls=%async_computation.2 | async-start | bytes 524288 | tf_op jit(solution)/shard_map/all_to_all | solution.py:188
  62.7 1.5 collective-permute-start.7
  64.2 5.2 %collective-permute-done.3.refs_1_ = bf16[4,448,256]{2,1,0:T(8,128)(2,1)} collective-permute-done((bf16[4,448,256]{2,1,0:T(8,128)(2,1)S(1)}, bf16[4,448,256]{2,1,0:T(8,128)(2,1)}, u32[]{:S(2)}, u32[]{:S(2)}) %collective-permute-start.3) | collective-permute-done | bytes 917536 | tf_op jit(solution)/shard_map/ppermute | solution.py:136
  69.4 1.8 %slice.50 = bf16[2,448,256]{2,1,0:T(8,128)(2,1)} slice(bf16[4,448,256]{2,1,0:T(8,128)(2,1)} %collective-permute-done.3.refs_1_), slice={[0:2], [0:448], [0:256]} | slice | bytes 917504 | tf_op jit(solution)/shard_map/slice | solution.py:164
  71.2 0.2 collective-permute-start.5
  71.4 1.8 %slice.51 = bf16[2,448,256]{2,1,0:T(8,128)(2,1)} slice(bf16[4,448,256]{2,1,0:T(8,128)(2,1)} %collective-permute-done.4.refs_2_), slice={[2:4], [0:448], [0:256]} | slice | bytes 917504 | tf_op jit(solution)/shard_map/slice | solution.py:164
  73.2 2.5 %collective-permute-start.6 = (bf16[2,448,256]{2,1,0:T(8,128)(2,1)}, bf16[2,448,256]{2,1,0:T(8,128)(2,1)}, u32[]{:S(2)}, u32[]{:S(2)}) collective-permute-start(bf16[2,448,256]{2,1,0:T(8,128)(2,1)} %slice.51), channel_id=1, source_target_pairs={{0,192},{64,0},{128,64},{192,128},{1,193},{65,1},{129,65},{193,129... | collective-permute-start | bytes 1376264 | tf_op jit(solution)/shard_map/ppermute | solution.py:136
  75.7 1.8 %collective-permute-start.8 = (bf16[4,448,256]{2,1,0:T(8,128)(2,1)}, bf16[4,448,256]{2,1,0:T(8,128)(2,1)}, u32[]{:S(2)}, u32[]{:S(2)}) collective-permute-start(bf16[4,448,256]{2,1,0:T(8,128)(2,1)} %collective-permute-done.3.refs_1_), channel_id=1, source_target_pairs={{0,32},{32,0},{1,33},{33,1},{2,34},{34,2},{3,35},{35,3},{4,36},{36... | collective-permute-start | bytes 2752520 | tf_op jit(solution)/shard_map/ppermute | solution.py:136
  77.5 0.1 reduce_sum.12
  77.5 0.7 broadcast_in_dim.16
  78.3 9.7 %all-to-all-start.3 = ((bf16[32,32,128]{2,1,0:T(8,128)(2,1)}), bf16[32,32,128]{2,1,0:T(8,128)(2,1)S(1)}, u32[]{:S(2)}, u32[]{:S(2)}) async-start(bf16[32,32,128]{2,1,0:T(8,128)(2,1)} %broadcast_in_dim.16), calls=%async_computation.3 | async-start | bytes 524288 | tf_op jit(solution)/shard_map/all_to_all | solution.py:190
  88.0 0.0 collective-permute-done.5.refs_3_
  88.0 0.9 collective-permute-start.10
  88.9 0.3 collective-permute-start.11
  89.1 0.0 collective-permute-done.7.refs_5_
  89.1 1.4 collective-permute-done.10.refs_8_
  90.5 0.7 collective-permute-done.11.refs_9_
  91.2 6.5 %shard_map.94 = bf16[4,448,2048]{2,1,0:T(8,128)(2,1)} custom-call(s32[1]{0:T(128)} %bitcast.me, bf16[4,448,256]{2,1,0:T(8,128)(2,1)S(1)} %pad_maximum_fusion.refs_0_, bf16[4,448,256]{2,1,0:T(8,128)(2,1)} %collective-permute-done.3.refs_1_, bf16[4,448,256]{2,1,0:T(8,128)(2,1)} %collective-permute-done.4.refs_2_, ...), custom_call_target="tpu_custom_call" | custom-call | tf_op jit(solution)/shard_map/pallas_call | solution.py:168
  97.7 1.8 %all-to-all-done.3 = bf16[32,32,128]{2,1,0:T(8,128)(2,1)S(1)} async-done(((bf16[32,32,128]{2,1,0:T(8,128)(2,1)}), bf16[32,32,128]{2,1,0:T(8,128)(2,1)S(1)}, u32[]{:S(2)}, u32[]{:S(2)}) %all-to-all-start.3) | async-done | bytes 262176 | tf_op jit(solution)/shard_map/all_to_all | solution.py:190
  99.4 1.2 copy-done.2
  100.6 1.4 shard_map.97
  102.0 1.1 copy-done.3
  103.2 1.3 copy-done.8
  104.5 5.8 %all-to-all-start.4 = ((bf16[8,2,64,768]{3,2,1,0:T(8,128)(2,1)}), bf16[8,2,64,768]{3,2,1,0:T(8,128)(2,1)S(1)}, u32[]{:S(2)}, u32[]{:S(2)}) async-start(bf16[8,2,64,768]{3,2,1,0:T(8,128)(2,1)} %bitcast.51), calls=%async_computation.4 | async-start | bytes 3145728 | tf_op jit(solution)/shard_map/all_to_all | solution.py:198
  110.3 5.0 %fusion.4 = bf16[448,1024]{1,0:T(8,128)(2,1)S(1)} fusion(bf16[1024,2048]{1,0:T(8,128)(2,1)} %all-gather.2.cloned.1.call-done, bf16[4,448,2048]{2,1,0:T(8,128)(2,1)} %shard_map.94), kind=kOutput, calls=%fused_computation.9 | convolution fusion | flops 1879506944 | bytes 6946816 | tf_op jit(solution)/shard_map/dot_general | solution.py:206
  115.3 0.1 fusion.8
  115.3 0.1 collective-permute-start.12
  115.4 2.7 %collective-permute-start.14 = (bf16[224,1024]{1,0:T(8,128)(2,1)S(1)}, bf16[224,1024]{1,0:T(8,128)(2,1)S(1)}, u32[]{:S(2)}, u32[]{:S(2)}) collective-permute-start(bf16[224,1024]{1,0:T(8,128)(2,1)S(1)} %get-tuple-element.16), channel_id=1, source_target_pairs={{0,3},{1,0},{2,1},{3,2},{4,7},{5,4},{6,5},{7,6},{8,11},{9,8},{10,9... | collective-permute-start | bytes 1376264 | tf_op jit(solution)/shard_map/ppermute | solution.py:136
  118.1 3.6 %fusion.2 = f32[448,1024]{1,0:T(8,128)S(1)} fusion(bf16[1024,2048]{1,0:T(8,128)(2,1)S(1)} %copy-done.10, bf16[4,448,2048]{2,1,0:T(8,128)(2,1)} %shard_map.94), kind=kOutput, calls=%fused_computation.5 | convolution fusion | flops 1879048192 | bytes 7864320 | tf_op jit(solution)/shard_map/dot_general | solution.py:206
  121.7 3.6 %fusion = f32[448,1024]{1,0:T(8,128)S(1)} fusion(bf16[1024,2048]{1,0:T(8,128)(2,1)S(1)} %copy-done.10, bf16[4,448,2048]{2,1,0:T(8,128)(2,1)} %shard_map.94), kind=kOutput, calls=%fused_computation.1 | convolution fusion | flops 1879048192 | bytes 7864320 | tf_op jit(solution)/shard_map/dot_general | solution.py:206
  125.3 0.1 slice.85
  125.4 0.1 slice.84
  125.4 3.2 %collective-permute-done.12 = bf16[224,1024]{1,0:T(8,128)(2,1)S(1)} collective-permute-done((bf16[224,1024]{1,0:T(8,128)(2,1)S(1)}, bf16[224,1024]{1,0:T(8,128)(2,1)S(1)}, u32[]{:S(2)}, u32[]{:S(2)}) %collective-permute-start.12) | collective-permute-done | bytes 458784 | tf_op jit(solution)/shard_map/ppermute | solution.py:136
  128.6 0.1 fusion.7
  128.7 1.0 pad_maximum_fusion.1
  129.7 0.1 fusion.6
  129.8 1.0 pad_maximum_fusion.2
  130.8 2.7 %collective-permute-start.15 = (bf16[448,1024]{1,0:T(8,128)(2,1)}, bf16[448,1024]{1,0:T(8,128)(2,1)}, u32[]{:S(2)}, u32[]{:S(2)}) collective-permute-start(bf16[448,1024]{1,0:T(8,128)(2,1)} %pad_maximum_fusion.2), channel_id=1, source_target_pairs={{0,3},{1,0},{2,1},{3,2},{4,7},{5,4},{6,5},{7,6},{8,11},{9,8},{10,9... | collective-permute-start | bytes 2752520 | tf_op jit(solution)/shard_map/ppermute | solution.py:136
  133.5 2.3 %shard_map.98 = (f32[8,64,256]{2,1,0:T(8,128)}, f32[8,64,448]{2,1,0:T(8,128)}) custom-call(s32[1]{0:T(128)} %bitcast.me, s32[8,8]{1,0:T(8,128)S(1)} %bitcast.55, bf16[8,2,64,768]{3,2,1,0:T(8,128)(2,1)S(1)} %all-to-all-done.4.terms), custom_call_target="tpu_custom_call" | custom-call | tf_op jit(solution)/shard_map/pallas_call | solution.py:199
  135.8 16.3 %collective-permute-done.13 = bf16[448,1024]{1,0:T(8,128)(2,1)} collective-permute-done((bf16[448,1024]{1,0:T(8,128)(2,1)}, bf16[448,1024]{1,0:T(8,128)(2,1)}, u32[]{:S(2)}, u32[]{:S(2)}) %collective-permute-start.13) | collective-permute-done | bytes 917536 | tf_op jit(solution)/shard_map/ppermute | solution.py:136
  152.1 0.1 collective-permute-done.15
  152.2 6.4 %fusion.5 = bf16[1024,448]{0,1:T(8,128)(2,1)} fusion(bf16[448,1024]{1,0:T(8,128)(2,1)} %collective-permute-done.15, bf16[448,1024]{1,0:T(8,128)(2,1)} %collective-permute-done.13, f32[448,1024]{1,0:T(8,128)S(1)} %copy-done.9, bf16[1024,2048]{1,0:T(8,128)(2,1)} %all-gather.2.cloned.1.call-done, bf16[4,448,2048]{2,1,0:T(8,128)(2,1)} %shard_map.94), kind=kOutput, calls=%fused_computation.10 | convolution fusion | flops 1881800704 | bytes 10616832 | tf_op jit(solution)/shard_map/dot_general | solution.py:206
  (26 shorter events, 0.1 us)
Async XLA Ops:
  7.2 103.1 %all-gather.2.cloned.1.call-start = ((), (), s32[]{:S(2)}) async-start(), calls=%async_computation.5 | async-start | bytes 4718592 | tf_op jit(solution)/shard_map/all_gather | solution.py:150
  9.2 11.0 %all-to-all-start = ((s32[8,1,8]{2,1,0:T(1,128)}), s32[8,1,8]{2,1,0:T(1,128)S(1)}, u32[]{:S(2)}, u32[]{:S(2)}) async-start(s32[8,1,8]{2,1,0:T(1,128)} %broadcast_in_dim.7), calls=%async_computation | async-start | bytes 8192 | tf_op jit(solution)/shard_map/all_to_all | solution.py:173
  20.1 1.0 copy-start.4
  21.2 0.9 copy-start.5
  24.2 25.1 %all-to-all-start.1 = ((bf16[8,2,64,768]{3,2,1,0:T(8,128)(2,1)}), bf16[8,2,64,768]{3,2,1,0:T(8,128)(2,1)S(1)}, u32[]{:S(2)}, u32[]{:S(2)}) async-start(bf16[8,2,64,768]{3,2,1,0:T(8,128)(2,1)} %shard_map.95), calls=%async_computation.1 | async-start | bytes 3145728 | tf_op jit(solution)/shard_map/all_to_all | solution.py:179
  28.4 20.9 %copy-start = (bf16[1024,256]{1,0:T(8,128)(2,1)S(1)}, bf16[1024,256]{1,0:T(8,128)(2,1)}, u32[]{:S(2)}) copy-start(bf16[1024,256]{1,0:T(8,128)(2,1)} %tokens.3) | copy-start | bytes 1572868
  28.4 20.9 %copy-start.6 = (s32[1,8]{1,0:T(1,128)S(1)}, s32[1,8]{1,0:T(1,128)}, u32[]{:S(2)}) copy-start(s32[1,8]{1,0:T(1,128)} %used.3) | copy-start | bytes 100
  28.4 20.9 %copy-start.7 = (s32[1,8]{1,0:T(1,128)S(1)}, s32[1,8]{1,0:T(1,128)}, u32[]{:S(2)}) copy-start(s32[1,8]{1,0:T(1,128)} %order.3) | copy-start | bytes 100
  30.1 7.4 %collective-permute-start = (bf16[448,256]{1,0:T(8,128)(2,1)S(1)}, bf16[448,256]{1,0:T(8,128)(2,1)S(1)}, u32[]{:S(2)}, u32[]{:S(2)}) collective-permute-start(bf16[448,256]{1,0:T(8,128)(2,1)S(1)} %get-tuple-element.12), channel_id=1, source_target_pairs={{0,3},{1,0},{2,1},{3,2},{4,7},{5,4},{6,5},{7,6},{8,11},{9,8},{10,9... | collective-permute-start | bytes 688136 | tf_op jit(solution)/shard_map/ppermute | solution.py:136
  32.3 8.3 %collective-permute-start.1 = (bf16[448,256]{1,0:T(8,128)(2,1)S(1)}, bf16[448,256]{1,0:T(8,128)(2,1)S(1)}, u32[]{:S(2)}, u32[]{:S(2)}) collective-permute-start(bf16[448,256]{1,0:T(8,128)(2,1)S(1)} %get-tuple-element.14), channel_id=1, source_target_pairs={{0,2},{1,3},{2,0},{3,1},{4,6},{5,7},{6,4},{7,5},{8,10},{9,11},{10,... | collective-permute-start | bytes 688136 | tf_op jit(solution)/shard_map/ppermute | solution.py:136
  32.6 13.7 %collective-permute-start.2 = (bf16[448,256]{1,0:T(8,128)(2,1)S(1)}, bf16[448,256]{1,0:T(8,128)(2,1)S(1)}, u32[]{:S(2)}, u32[]{:S(2)}) collective-permute-start(bf16[448,256]{1,0:T(8,128)(2,1)S(1)} %get-tuple-element.13), channel_id=1, source_target_pairs={{0,1},{1,2},{2,3},{3,0},{4,5},{5,6},{6,7},{7,4},{8,9},{9,10},{10,1... | collective-permute-start | bytes 688136 | tf_op jit(solution)/shard_map/ppermute | solution.py:136
  46.4 22.9 %collective-permute-start.3 = (bf16[4,448,256]{2,1,0:T(8,128)(2,1)S(1)}, bf16[4,448,256]{2,1,0:T(8,128)(2,1)}, u32[]{:S(2)}, u32[]{:S(2)}) collective-permute-start(bf16[4,448,256]{2,1,0:T(8,128)(2,1)S(1)} %pad_maximum_fusion.refs_0_), channel_id=1, source_target_pairs={{0,64},{64,128},{128,192},{192,0},{1,65},{65,129},{129,193},{193,1... | collective-permute-start | bytes 2752520 | tf_op jit(solution)/shard_map/ppermute | solution.py:136
  47.9 23.5 %collective-permute-start.4 = (bf16[4,448,256]{2,1,0:T(8,128)(2,1)S(1)}, bf16[4,448,256]{2,1,0:T(8,128)(2,1)}, u32[]{:S(2)}, u32[]{:S(2)}) collective-permute-start(bf16[4,448,256]{2,1,0:T(8,128)(2,1)S(1)} %pad_maximum_fusion.refs_0_), channel_id=1, source_target_pairs={{0,192},{64,0},{128,64},{192,128},{1,193},{65,1},{129,65},{193,129... | collective-permute-start | bytes 2752520 | tf_op jit(solution)/shard_map/ppermute | solution.py:136
  49.3 1.2 copy-start.1
  52.3 25.2 %all-to-all-start.2 = ((bf16[32,32,128]{2,1,0:T(8,128)(2,1)}), bf16[32,32,128]{2,1,0:T(8,128)(2,1)S(1)}, u32[]{:S(2)}, u32[]{:S(2)}) async-start(bf16[32,32,128]{2,1,0:T(8,128)(2,1)} %bitcast.15), calls=%async_computation.2 | async-start | bytes 524288 | tf_op jit(solution)/shard_map/all_to_all | solution.py:188
  62.7 26.5 %collective-permute-start.7 = (bf16[4,448,256]{2,1,0:T(8,128)(2,1)S(1)}, bf16[4,448,256]{2,1,0:T(8,128)(2,1)}, u32[]{:S(2)}, u32[]{:S(2)}) collective-permute-start(bf16[4,448,256]{2,1,0:T(8,128)(2,1)S(1)} %pad_maximum_fusion.refs_0_), channel_id=1, source_target_pairs={{0,32},{32,0},{1,33},{33,1},{2,34},{34,2},{3,35},{35,3},{4,36},{36... | collective-permute-start | bytes 2752520 | tf_op jit(solution)/shard_map/ppermute | solution.py:136
  71.2 16.8 %collective-permute-start.5 = (bf16[2,448,256]{2,1,0:T(8,128)(2,1)}, bf16[2,448,256]{2,1,0:T(8,128)(2,1)}, u32[]{:S(2)}, u32[]{:S(2)}) collective-permute-start(bf16[2,448,256]{2,1,0:T(8,128)(2,1)} %slice.50), channel_id=1, source_target_pairs={{0,64},{64,128},{128,192},{192,0},{1,65},{65,129},{129,193},{193,1... | collective-permute-start | bytes 1376264 | tf_op jit(solution)/shard_map/ppermute | solution.py:136
  73.2 15.7 %collective-permute-start.6 = (bf16[2,448,256]{2,1,0:T(8,128)(2,1)}, bf16[2,448,256]{2,1,0:T(8,128)(2,1)}, u32[]{:S(2)}, u32[]{:S(2)}) collective-permute-start(bf16[2,448,256]{2,1,0:T(8,128)(2,1)} %slice.51), channel_id=1, source_target_pairs={{0,192},{64,0},{128,64},{192,128},{1,193},{65,1},{129,65},{193,129... | collective-permute-start | bytes 1376264 | tf_op jit(solution)/shard_map/ppermute | solution.py:136
  75.7 15.5 %collective-permute-start.8 = (bf16[4,448,256]{2,1,0:T(8,128)(2,1)}, bf16[4,448,256]{2,1,0:T(8,128)(2,1)}, u32[]{:S(2)}, u32[]{:S(2)}) collective-permute-start(bf16[4,448,256]{2,1,0:T(8,128)(2,1)} %collective-permute-done.3.refs_1_), channel_id=1, source_target_pairs={{0,32},{32,0},{1,33},{33,1},{2,34},{34,2},{3,35},{35,3},{4,36},{36... | collective-permute-start | bytes 2752520 | tf_op jit(solution)/shard_map/ppermute | solution.py:136
  77.5 13.7 %collective-permute-start.9 = (bf16[4,448,256]{2,1,0:T(8,128)(2,1)}, bf16[4,448,256]{2,1,0:T(8,128)(2,1)}, u32[]{:S(2)}, u32[]{:S(2)}) collective-permute-start(bf16[4,448,256]{2,1,0:T(8,128)(2,1)} %collective-permute-done.4.refs_2_), channel_id=1, source_target_pairs={{0,32},{32,0},{1,33},{33,1},{2,34},{34,2},{3,35},{35,3},{4,36},{36... | collective-permute-start | bytes 2752520 | tf_op jit(solution)/shard_map/ppermute | solution.py:136
  78.3 21.2 %all-to-all-start.3 = ((bf16[32,32,128]{2,1,0:T(8,128)(2,1)}), bf16[32,32,128]{2,1,0:T(8,128)(2,1)S(1)}, u32[]{:S(2)}, u32[]{:S(2)}) async-start(bf16[32,32,128]{2,1,0:T(8,128)(2,1)} %broadcast_in_dim.16), calls=%async_computation.3 | async-start | bytes 524288 | tf_op jit(solution)/shard_map/all_to_all | solution.py:190
  88.0 2.5 %collective-permute-start.10 = (bf16[2,448,256]{2,1,0:T(8,128)(2,1)}, bf16[2,448,256]{2,1,0:T(8,128)(2,1)S(1)}, u32[]{:S(2)}, u32[]{:S(2)}) collective-permute-start(bf16[2,448,256]{2,1,0:T(8,128)(2,1)} %collective-permute-done.5.refs_3_), channel_id=1, source_target_pairs={{0,32},{32,0},{1,33},{33,1},{2,34},{34,2},{3,35},{35,3},{4,36},{36... | collective-permute-start | bytes 1376264 | tf_op jit(solution)/shard_map/ppermute | solution.py:136
  88.9 2.3 %collective-permute-start.11 = (bf16[2,448,256]{2,1,0:T(8,128)(2,1)}, bf16[2,448,256]{2,1,0:T(8,128)(2,1)S(1)}, u32[]{:S(2)}, u32[]{:S(2)}) collective-permute-start(bf16[2,448,256]{2,1,0:T(8,128)(2,1)} %collective-permute-done.6.refs_4_), channel_id=1, source_target_pairs={{0,32},{32,0},{1,33},{33,1},{2,34},{34,2},{3,35},{35,3},{4,36},{36... | collective-permute-start | bytes 1376264 | tf_op jit(solution)/shard_map/ppermute | solution.py:136
  99.4 1.2 copy-start.2
  102.0 1.1 copy-start.3
  103.1 1.3 copy-start.8
  104.5 29.0 %all-to-all-start.4 = ((bf16[8,2,64,768]{3,2,1,0:T(8,128)(2,1)}), bf16[8,2,64,768]{3,2,1,0:T(8,128)(2,1)S(1)}, u32[]{:S(2)}, u32[]{:S(2)}) async-start(bf16[8,2,64,768]{3,2,1,0:T(8,128)(2,1)} %bitcast.51), calls=%async_computation.4 | async-start | bytes 3145728 | tf_op jit(solution)/shard_map/all_to_all | solution.py:198
  110.3 7.8 %copy-start.10 = (bf16[1024,2048]{1,0:T(8,128)(2,1)S(1)}, bf16[1024,2048]{1,0:T(8,128)(2,1)}, u32[]{:S(2)}) copy-start(bf16[1024,2048]{1,0:T(8,128)(2,1)} %all-gather.2.cloned.1.call-done) | copy-start | bytes 12582916
  115.3 13.3 %collective-permute-start.12 = (bf16[224,1024]{1,0:T(8,128)(2,1)S(1)}, bf16[224,1024]{1,0:T(8,128)(2,1)S(1)}, u32[]{:S(2)}, u32[]{:S(2)}) collective-permute-start(bf16[224,1024]{1,0:T(8,128)(2,1)S(1)} %get-tuple-element.15), channel_id=1, source_target_pairs={{0,1},{1,2},{2,3},{3,0},{4,5},{5,6},{6,7},{7,4},{8,9},{9,10},{10,1... | collective-permute-start | bytes 1376264 | tf_op jit(solution)/shard_map/ppermute | solution.py:136
  115.4 14.3 %collective-permute-start.14 = (bf16[224,1024]{1,0:T(8,128)(2,1)S(1)}, bf16[224,1024]{1,0:T(8,128)(2,1)S(1)}, u32[]{:S(2)}, u32[]{:S(2)}) collective-permute-start(bf16[224,1024]{1,0:T(8,128)(2,1)S(1)} %get-tuple-element.16), channel_id=1, source_target_pairs={{0,3},{1,0},{2,1},{3,2},{4,7},{5,4},{6,5},{7,6},{8,11},{9,8},{10,9... | collective-permute-start | bytes 1376264 | tf_op jit(solution)/shard_map/ppermute | solution.py:136
  129.7 22.4 %collective-permute-start.13 = (bf16[448,1024]{1,0:T(8,128)(2,1)}, bf16[448,1024]{1,0:T(8,128)(2,1)}, u32[]{:S(2)}, u32[]{:S(2)}) collective-permute-start(bf16[448,1024]{1,0:T(8,128)(2,1)} %pad_maximum_fusion.1), channel_id=1, source_target_pairs={{0,1},{1,2},{2,3},{3,0},{4,5},{5,6},{6,7},{7,4},{8,9},{9,10},{10,1... | collective-permute-start | bytes 2752520 | tf_op jit(solution)/shard_map/ppermute | solution.py:136
  129.8 22.4 %copy-start.9 = (f32[448,1024]{1,0:T(8,128)S(1)}, f32[448,1024]{1,0:T(8,128)}, u32[]{:S(2)}) copy-start(f32[448,1024]{1,0:T(8,128)} %copy-done.8) | copy-start | bytes 5505028
  130.8 21.4 %collective-permute-start.15 = (bf16[448,1024]{1,0:T(8,128)(2,1)}, bf16[448,1024]{1,0:T(8,128)(2,1)}, u32[]{:S(2)}, u32[]{:S(2)}) collective-permute-start(bf16[448,1024]{1,0:T(8,128)(2,1)} %pad_maximum_fusion.2), channel_id=1, source_target_pairs={{0,3},{1,0},{2,1},{3,2},{4,7},{5,4},{6,5},{7,6},{8,11},{9,8},{10,9... | collective-permute-start | bytes 2752520 | tf_op jit(solution)/shard_map/ppermute | solution.py:136
Sparse Core Ops, SparseCore 0:
  9.7 68.4 all-gather.1

commit v3 on v1

--- a/solution.py
+++ b/solution.py
@@ -13,7 +13,6 @@
 MP = ("z", "y")
 VMEM = pl.BlockSpec(memory_space=pltpu.VMEM)
 SMEM = pl.BlockSpec(memory_space=pltpu.SMEM)
-LIMIT = 40 * 1024 * 1024
 
 
 def pair_of(used, group, owner, per_owner, slots):
@@ -108,13 +107,99 @@
                 grad_b[local] += terms[group, place, :, width:width + units].astype(F32)
 
 
-def call(kernel, outs, specs):
+def gather_rows(meta, r, weights, tokens, wide, rows):
+    width = tokens[0].shape[1]
+    x, core, z = meta[0], meta[1], meta[2]
+    mid = weights[0].shape[0] // 2
+    for other in range(2):
+        own, left, right, far_left, far_right = weights[5 * other:5 * other + 5]
+        far = far_left.at[r] if r < mid else far_right.at[r - mid]
+        for source, step in ((own.at[r], 0), (left.at[r], 3), (right.at[r], 1), (far, 2)):
+            block = 2 * lax.rem(x + step, jnp.int32(4)) + (1 - core if other else core)
+            place = lax.rem(block - z + 8, jnp.int32(8))
+            wide[:, pl.ds(pl.multiple_of(place * width, width), width)] = source[...]
+    if rows is not None:
+        half = tokens[7].shape[0]
+        own, f1, b1, f2, b2, f3, b3, f4, b4 = tokens
+        for place, source in ((0, own), (1, b1), (2, b2), (3, b3), (5, f3), (6, f2), (7, f1)):
+            rows[:, place * width:(place + 1) * width] = source[...]
+        rows[0:half, 4 * width:5 * width] = f4[...]
+        rows[half:2 * half, 4 * width:5 * width] = b4[...]
+
+
+def multiply(wide, rows, store):
+    step = 256
+
+    @pl.loop(0, rows.shape[0] // step)
+    def _(i):
+        span = pl.ds(pl.multiple_of(i * step, step), step)
+        store(span, lax.dot_general(
+            wide[...], rows[span, :], (((1,), (1,)), ((), ())), preferred_element_type=F32
+        ))
+
+
+def far_kernel(meta, *refs):
+    weights, tokens = refs[:10], refs[10:19]
+    up, down, wide, rows = refs[19:]
+    gather_rows(meta, 2, weights, tokens, wide, rows)
+    half = up.shape[0]
+
+    def store(span, value):
+        up[:, span] = value[:half].astype(BF)
+        down[:, span] = value[half:].astype(BF)
+
+    multiply(wide, rows, store)
+
+
+def near_kernel(meta, *refs):
+    weights, tokens = refs[:10], refs[10:19]
+    up_late, up_soon, down_soon, down_late, wide, rows = refs[19:]
+    half = up_late.shape[0]
+    gather_rows(meta, 1, weights, tokens, wide, rows)
+
+    def store_up(span, value):
+        up_late[:, span] = value[:half]
+        up_soon[:, span] = value[half:].astype(BF)
+
+    multiply(wide, rows, store_up)
+    gather_rows(meta, 3, weights, tokens, wide, None)
+
+    def store_down(span, value):
+        down_soon[:, span] = value[:half].astype(BF)
+        down_late[:, span] = value[half:]
+
+    multiply(wide, rows, store_down)
+
+
+def own_kernel(meta, *refs):
+    weights, tokens = refs[:10], refs[10:19]
+    delta, out, wide, rows = refs[19:]
+    gather_rows(meta, 0, weights, tokens, wide, rows)
+
+    def store(span, value):
+        out[:, span] = value + delta[:, span]
+
+    multiply(wide, rows, store)
+
+
+def join_kernel(base, up_late, up_soon, down_soon, down_late, out):
+    half = up_late.shape[0]
+    out[0:half, :] = (
+        base[0:half, :] + up_late[...].astype(F32) + down_soon[...].astype(F32)
+    ).astype(BF)
+    out[half:, :] = (
+        base[half:, :] + up_soon[...].astype(F32) + down_late[...].astype(F32)
+    ).astype(BF)
+
+
+def call(kernel, outs, specs, scratch=(), limit=16):
     return pl.pallas_call(
         kernel,
         out_shape=outs,
         in_specs=specs,
         out_specs=jax.tree.map(lambda _: VMEM, outs),
-        compiler_params=pltpu.CompilerParams(vmem_limit_bytes=LIMIT),
+        scratch_shapes=scratch,
+        compiler_params=pltpu.CompilerParams(vmem_limit_bytes=limit * 1024 * 1024),
     )
 
 
@@ -134,28 +219,34 @@
     me = lax.axis_index(DP)
     whole = jax.ShapeDtypeStruct
 
-    wide_tokens = lax.all_gather(tokens, "z", axis=1, tiled=True)
+    together = lax.optimization_barrier
+    x, core, z, y = (lax.axis_index(name) for name in ("x", "core", "z", "y"))
+    meta = jnp.stack([x, core, z, y]).astype(jnp.int32)
+    me_arr = me.reshape(1).astype(jnp.int32)
 
     weight_t = weight.T
     piece = n_y * width
     mine = lax.dynamic_slice(weight_t, (0, me * piece), (units, piece))
-    spot = lax.axis_index("y")
     pieces = [
-        hop(lax.dynamic_slice(mine, (0, lax.rem(spot + n_y - r, n_y) * width), (units, width)), "y", -r)
-        if r else lax.dynamic_slice(mine, (0, spot * width), (units, width))
+        hop(lax.dynamic_slice(mine, (0, lax.rem(y + n_y - r, n_y) * width), (units, width)), "y", -r)
+        if r else lax.dynamic_slice(mine, (0, y * width), (units, width))
         for r in range(n_y)
     ]
-    wide_weight = lax.all_gather(jnp.stack(pieces), DP, axis=2, tiled=True)
+    f1, b1 = hop(tokens, "z", 1), hop(tokens, "z", -1)
 
     down_t = jnp.transpose(down, (0, 2, 1))
     used_all = lax.all_to_all(
         jnp.broadcast_to(used[None], (owners,) + used.shape), DP, 0, 0, tiled=True
     ).reshape(owners, used.shape[1])
-    me_arr = me.reshape(1).astype(jnp.int32)
     picked = call(pick_kernel, whole((owners, 2, rank, packed), BF), [SMEM, SMEM, VMEM, VMEM])(
         me_arr, used_all, down_t, up
     )
+    picked, pieces, f1, b1 = together((picked, pieces, f1, b1))
+    own = jnp.stack(pieces)
+    from_left, from_right = hop(own, "x", 1), hop(own, "x", -1)
+    f2, b2 = hop(f1, "z", 1), hop(b1, "z", -1)
     factors = lax.all_to_all(picked, DP, 0, 0, tiled=True).reshape(owners * 2, rank, packed)
+    f3, b3 = hop(f2, "z", 1), hop(b2, "z", -1)
     cot_t = cotangent.T
     sizes = dict(rank=rank, width=width, units=units)
     part = call(
@@ -163,12 +254,33 @@
         whole((rows, 2 * rank), BF),
         [SMEM, SMEM, VMEM, VMEM, VMEM],
     )(used, order, factors, tokens, cot_t)
+    part, from_left, from_right, f2, b2 = together((part, from_left, from_right, f2, b2))
+    mid, halfway = n_y // 2, rows // 2
+    far_left, far_right = hop(from_left[:mid], "x", 1), hop(from_right[mid:], "x", -1)
+    f4, b4 = hop(f3[:halfway], "z", 1), hop(b3[halfway:], "z", -1)
+    held = (own, from_left, from_right, far_left, far_right)
+    swapped = tuple(hop(item, "core", 1) for item in held)
     share = rows // members
     parts = lax.all_to_all(part.reshape(members, share, 2 * rank), MP, 0, 0, tiled=True)
     summed = jnp.sum(parts.astype(F32), axis=0).astype(BF)
     both = lax.all_to_all(
         jnp.broadcast_to(summed[None], (members,) + summed.shape), MP, 0, 0, tiled=True
     ).reshape(rows, 2 * rank)
+
+    blocks = (meta, *held, *swapped, tokens, f1, b1, f2, b2, f3, b3, f4, b4)
+    specs = [SMEM] + [VMEM] * 19
+    scratch = [pltpu.VMEM((units, n_z * width), BF), pltpu.VMEM((rows, n_z * width), BF)]
+    half = units // 2
+    narrow, broad = whole((half, rows), BF), whole((half, rows), F32)
+    far_up, far_down = call(far_kernel, (narrow, narrow), specs, scratch, 32)(*blocks)
+    far_up, far_down = hop(far_up, "y", 1), hop(far_down, "y", -1)
+    up_late, up_soon, down_soon, down_late = call(
+        near_kernel, (broad, narrow, narrow, broad), specs, scratch, 32
+    )(*blocks)
+    up_soon, down_soon = hop(up_soon, "y", 1), hop(down_soon, "y", -1)
+    up_late = hop((up_late + far_up.astype(F32)).astype(BF), "y", 1)
+    down_late = hop((down_late + far_down.astype(F32)).astype(BF), "y", -1)
+
     send, delta = call(
         functools.partial(grads_kernel, **sizes),
         (whole((owners * 2, rank, packed), BF), whole((units, rows), F32)),
@@ -181,22 +293,11 @@
         [SMEM, SMEM, VMEM],
     )(me_arr, used_all, terms)
 
-    def product(r):
-        return lax.dot_general(
-            wide_weight[r], wide_tokens, (((1,), (1,)), ((), ())), preferred_element_type=F32
-        )
-
-    half = units // 2
-    far = product(2).astype(BF)
-    far_up, far_down = hop(far[:half], "y", 1), hop(far[half:], "y", -1)
-    near_up, near_down = product(1), product(n_y - 1)
-    near_up = jnp.concatenate([near_up[:half] + far_up.astype(F32), near_up[half:]]).astype(BF)
-    near_down = jnp.concatenate(
-        [near_down[:half], near_down[half:] + far_down.astype(F32)]
-    ).astype(BF)
-    got_up, got_down = hop(near_up, "y", 1), hop(near_down, "y", -1)
-    out = product(0) + delta + got_up.astype(F32) + got_down.astype(F32)
-    return out.astype(BF).T, jnp.transpose(grad_a, (0, 2, 1)), grad_b
+    base = call(own_kernel, whole((units, rows), F32), specs + [VMEM], scratch, 32)(*blocks, delta)
+    out = call(join_kernel, whole((units, rows), BF), [VMEM] * 5)(
+        base, up_late, up_soon, down_soon, down_late
+    )
+    return out.T, jnp.transpose(grad_a, (0, 2, 1)), grad_b
 
 
 def solution(mesh):

time: 209 us -> 181 us (0.87)
  blocking collectives: 71.3 us -> 10.6 us
  starting transfers between devices: 17.8 us -> 63.8 us
  waiting for transfers between devices: 76.1 us -> 49.3 us
  Pallas kernels: 5.56 us -> 32.3 us
  matrix products: 15.6 us -> 0 us
  local copies, waits for them, and re-layouts: 4.44 us -> 18.5 us
  between operations: 14.3 us -> 0.93 us
    all_to_all x3 -> x0, blocking collectives: 59.8 us -> none  [the longest x1 24 us: on_device(): lax.all_to_all(picked, DP, 0, 0, tiled=True)]
    all_gather x2 -> x0, waiting for transfers between devices: 40.4 us -> none  [the longest x1 40.4 us: on_device(): wide_weight = lax.all_gather(jnp.stack(pieces), DP, axis=2, tiled=True)]
    ppermute x7 -> x26, starting transfers between devices: 10.9 us -> 39.7 us  [hop(): return lax.ppermute(value, axis, [(i, (i + step) % n) for i in range(n)])]
    pallas_call x0 -> x4, Pallas kernels: none -> 26.3 us  [the longest x1 10.1 us: on_device(): call(near_kernel, (broad, narrow, narrow, broad), specs, scratch, 32)]
    all_to_all x0 -> x3, starting transfers between devices: none -> 19.3 us  [the longest x1 9.27 us: on_device(): lax.all_to_all(jnp.broadcast_to(summed[None], (members,) + summed.shape),...]
    dot_general x4 -> x0, matrix products: 15.6 us -> none  [product(): lax.dot_general(wide_weight[r], wide_tokens, (((1,), (1,)), ((), ())), pr...]
    ppermute x7 -> x26, waiting for transfers between devices: 34.9 us -> 49.3 us  [hop(): return lax.ppermute(value, axis, [(i, (i + step) % n) for i in range(n)])]
    unnamed x22 -> x40, local copies, waits for them, and re-layouts: 2.52 us -> 10.3 us
  transfers between devices with their start and end apart: 10 -> 30, of which waited for: 7 -> 7; matrix products, arithmetic and copies ran while one was open for 7% -> 7% of each run, Pallas kernels for 3% -> 17%
where the time goes in v3:
time: 181 us; the launch traced here: 180 us
  starting transfers between devices  63.8 us (35%)
  waiting for transfers between devices  49.3 us (27%)
  Pallas kernels  32.3 us (18%)
  local copies, waits for them, and re-layouts  18.5 us (10%)
  blocking collectives  10.6 us (6%)
  other arithmetic  4.5 us (2%)
    ppermute x26, waiting for transfers between devices, hop(): return lax.ppermute(value, axis, [(i, (i + step) % n) for i in range(n)])  49.3 us
    ppermute x26, starting transfers between devices, hop(): return lax.ppermute(value, axis, [(i, (i + step) % n) for i in range(n)])  39.7 us
    all_to_all x1, blocking collectives, on_device(): lax.all_to_all(jnp.broadcast_to(used[None], (owners,) + used.shape), DP,...  10.6 us
    unnamed x40, local copies, waits for them, and re-layouts  10.3 us
    pallas_call x1, Pallas kernels, on_device(): call(near_kernel, (broad, narrow, narrow, broad), specs, scratch, 32)  10.1 us
    all_to_all x1, starting transfers between devices, on_device(): lax.all_to_all(jnp.broadcast_to(summed[None], (members,) + summed.shape),...  9.27 us
    pallas_call x1, Pallas kernels, on_device(): call(far_kernel, (narrow, narrow), specs, scratch, 32)(*blocks)  7.84 us
    pallas_call x1, Pallas kernels, on_device(): call(own_kernel, whole((units, rows), F32), specs + [VMEM], scratch, 32)  7.13 us
  transfers between devices with their start and end apart: 30, of which 7 were waited for; matrix products, arithmetic and copies ran while one was open for 7% of the time, Pallas kernels for 17%

profile of v3, /device:TPU:1, one launch (start us, length us, event | category | flops | bytes accessed | tf_op | source)
XLA Modules:
  0.0 180.0 jit_solution(316122777869494567)
XLA Ops:
  0.7 6.5 %collective-permute-start.4 = (bf16[1024,256]{1,0:T(8,128)(2,1)}, bf16[1024,256]{1,0:T(8,128)(2,1)}, u32[]{:S(2)}, u32[]{:S(2)}) collective-permute-start(bf16[1024,256]{1,0:T(8,128)(2,1)} %refs_10_.5), channel_id=1, source_target_pairs={{0,28},{4,0},{8,4},{12,8},{16,12},{20,16},{24,20},{28,24},{1,29},{... | collective-permute-start | bytes 1572872 | tf_op jit(solution)/shard_map/ppermute | solution.py:208
  7.1 2.3 %dynamic-slice_bitcast_fusion = (bf16[448,256]{1,0:T(8,128)(2,1)S(1)}, bf16[448,256]{1,0:T(8,128)(2,1)S(1)}, bf16[448,256]{1,0:T(8,128)(2,1)}, bf16[448,256]{1,0:T(8,128)(2,1)S(1)}) fusion(bf16[8192,448]{0,1:T(8,128)(2,1)} %param.9, s32[]{:T(128)S(6)} %add.61, s32[]{:T(128)S(6)} %add.57, s32[]{:T(128)S(6)} %add.55, s32[]{:T(128)S(6)} %add.59), kind=kLoop, calls=%fused_computation.3 | loop fusion | bytes 1835024 | tf_op jit(solution)/shard_map/dynamic_slice | solution.py:231
  9.5 1.3 collective-permute-start.2
  10.8 1.4 collective-permute-start
  12.2 1.6 collective-permute-start.1
  13.9 10.6 %all_to_all.25 = s32[8,1,8]{2,1,0:T(1,128)S(1)} all-to-all(s32[8,1,8]{2,1,0:T(1,128)S(1)} %broadcast_in_dim.7), channel_id=1, replica_groups=mesh['x'=4,'core'=2,'z'=8,'y'=4] {'x','core'}, dimensions={0} | all-to-all | bytes 512 | tf_op jit(solution)/shard_map/all_to_all | solution.py:238
  24.5 0.9 shard_map.94
  25.4 1.2 copy-done.1
  26.6 0.7 copy-done.19
  27.4 4.2 %all-to-all-start.1 = ((bf16[8,2,64,768]{3,2,1,0:T(8,128)(2,1)}), bf16[8,2,64,768]{3,2,1,0:T(8,128)(2,1)S(1)}, u32[]{:S(2)}, u32[]{:S(2)}) async-start(bf16[8,2,64,768]{3,2,1,0:T(8,128)(2,1)} %copy-done.1), calls=%async_computation.1 | async-start | bytes 3145728 | tf_op jit(solution)/shard_map/all_to_all | solution.py:248
  31.5 1.4 pad_maximum_fusion.refs_0_
  33.0 2.7 %collective-permute-start.6 = (bf16[4,448,256]{2,1,0:T(8,128)(2,1)S(1)}, bf16[4,448,256]{2,1,0:T(8,128)(2,1)}, u32[]{:S(2)}, u32[]{:S(2)}) collective-permute-start(bf16[4,448,256]{2,1,0:T(8,128)(2,1)S(1)} %pad_maximum_fusion.refs_0_), channel_id=1, source_target_pairs={{0,192},{64,0},{128,64},{192,128},{1,193},{65,1},{129,65},{193,129... | collective-permute-start | bytes 2752520 | tf_op jit(solution)/shard_map/ppermute | solution.py:208
  35.7 0.6 collective-permute-start.11
  36.3 3.0 %collective-permute-start.8 = (bf16[1024,256]{1,0:T(8,128)(2,1)}, bf16[1024,256]{1,0:T(8,128)(2,1)}, u32[]{:S(2)}, u32[]{:S(2)}) collective-permute-start(bf16[1024,256]{1,0:T(8,128)(2,1)} %collective-permute-done.4.refs_12_), channel_id=1, source_target_pairs={{0,28},{4,0},{8,4},{12,8},{16,12},{20,16},{24,20},{28,24},{1,29},{... | collective-permute-start | bytes 1572872 | tf_op jit(solution)/shard_map/ppermute | solution.py:208
  39.3 7.5 %collective-permute-done.7.refs_13_ = bf16[1024,256]{1,0:T(8,128)(2,1)} collective-permute-done((bf16[1024,256]{1,0:T(8,128)(2,1)S(1)}, bf16[1024,256]{1,0:T(8,128)(2,1)}, u32[]{:S(2)}, u32[]{:S(2)}) %collective-permute-start.7) | collective-permute-done | bytes 524320 | tf_op jit(solution)/shard_map/ppermute | solution.py:208
  46.8 4.1 %collective-permute-done.8.refs_14_ = bf16[1024,256]{1,0:T(8,128)(2,1)} collective-permute-done((bf16[1024,256]{1,0:T(8,128)(2,1)}, bf16[1024,256]{1,0:T(8,128)(2,1)}, u32[]{:S(2)}, u32[]{:S(2)}) %collective-permute-start.8) | collective-permute-done | bytes 524320 | tf_op jit(solution)/shard_map/ppermute | solution.py:208
  50.9 3.4 %collective-permute-start.17 = (bf16[1024,256]{1,0:T(8,128)(2,1)}, bf16[1024,256]{1,0:T(8,128)(2,1)}, u32[]{:S(2)}, u32[]{:S(2)}) collective-permute-start(bf16[1024,256]{1,0:T(8,128)(2,1)} %collective-permute-done.8.refs_14_), channel_id=1, source_target_pairs={{0,28},{4,0},{8,4},{12,8},{16,12},{20,16},{24,20},{28,24},{1,29},{... | collective-permute-start | bytes 1572872 | tf_op jit(solution)/shard_map/ppermute | solution.py:208
  54.4 0.0 copy-start.6
  54.4 1.2 copy-done.6
  55.5 1.1 shard_map.95
  56.7 0.7 copy-done.11
  57.4 13.2 %collective-permute-done.6.refs_2_ = bf16[4,448,256]{2,1,0:T(8,128)(2,1)} collective-permute-done((bf16[4,448,256]{2,1,0:T(8,128)(2,1)S(1)}, bf16[4,448,256]{2,1,0:T(8,128)(2,1)}, u32[]{:S(2)}, u32[]{:S(2)}) %collective-permute-start.6) | collective-permute-done | bytes 917536 | tf_op jit(solution)/shard_map/ppermute | solution.py:208
  70.6 1.4 collective-permute-done.5.refs_1_
  71.9 5.9 %all-to-all-start.2 = ((bf16[32,32,128]{2,1,0:T(8,128)(2,1)}), bf16[32,32,128]{2,1,0:T(8,128)(2,1)}, u32[]{:S(2)}, u32[]{:S(2)}) async-start(bf16[32,32,128]{2,1,0:T(8,128)(2,1)} %bitcast.32), calls=%async_computation.2 | async-start | bytes 524288 | tf_op jit(solution)/shard_map/all_to_all | solution.py:264
  77.8 1.0 slice.12
  78.8 1.1 slice.13
  79.9 0.5 collective-permute-start.10
  80.4 1.0 collective-permute-start.9
  81.4 1.5 collective-permute-start.12
  83.0 0.1 collective-permute-start.13
  83.1 0.7 slice.16
  83.8 1.4 collective-permute-start.18
  85.2 5.9 %collective-permute-done.10.refs_4_ = bf16[2,448,256]{2,1,0:T(8,128)(2,1)} collective-permute-done((bf16[2,448,256]{2,1,0:T(8,128)(2,1)S(1)}, bf16[2,448,256]{2,1,0:T(8,128)(2,1)}, u32[]{:S(2)}, u32[]{:S(2)}) %collective-permute-start.10) | collective-permute-done | bytes 458784 | tf_op jit(solution)/shard_map/ppermute | solution.py:208
  91.1 1.9 %collective-permute-start.15 = (bf16[2,448,256]{2,1,0:T(8,128)(2,1)}, bf16[2,448,256]{2,1,0:T(8,128)(2,1)}, u32[]{:S(2)}, u32[]{:S(2)}) collective-permute-start(bf16[2,448,256]{2,1,0:T(8,128)(2,1)} %collective-permute-done.10.refs_4_), channel_id=1, source_target_pairs={{0,32},{32,0},{1,33},{33,1},{2,34},{34,2},{3,35},{35,3},{4,36},{36... | collective-permute-start | bytes 1376264 | tf_op jit(solution)/shard_map/ppermute | solution.py:208
  93.0 1.6 collective-permute-start.14
  94.7 1.6 reduce_sum.12
  96.3 1.4 broadcast_in_dim.16
  97.7 9.3 %all-to-all-start.3 = ((bf16[32,32,128]{2,1,0:T(8,128)(2,1)}), bf16[32,32,128]{2,1,0:T(8,128)(2,1)}, u32[]{:S(2)}, u32[]{:S(2)}) async-start(bf16[32,32,128]{2,1,0:T(8,128)(2,1)} %broadcast_in_dim.16), calls=%async_computation.3 | async-start | bytes 524288 | tf_op jit(solution)/shard_map/all_to_all | solution.py:266
  107.0 1.7 slice.17
  108.7 2.4 %collective-permute-start.19 = (bf16[512,256]{1,0:T(8,128)(2,1)}, bf16[512,256]{1,0:T(8,128)(2,1)}, u32[]{:S(2)}, u32[]{:S(2)}) collective-permute-start(bf16[512,256]{1,0:T(8,128)(2,1)} %slice.17), channel_id=1, source_target_pairs={{0,28},{4,0},{8,4},{12,8},{16,12},{20,16},{24,20},{28,24},{1,29},{... | collective-permute-start | bytes 786440 | tf_op jit(solution)/shard_map/ppermute | solution.py:208
  111.1 0.1 pad_add_fusion.meta
  111.2 8.9 %collective-permute-done.19.refs_18_ = bf16[512,256]{1,0:T(8,128)(2,1)} collective-permute-done((bf16[512,256]{1,0:T(8,128)(2,1)}, bf16[512,256]{1,0:T(8,128)(2,1)}, u32[]{:S(2)}, u32[]{:S(2)}) %collective-permute-start.19) | collective-permute-done | bytes 262176 | tf_op jit(solution)/shard_map/ppermute | solution.py:208
  120.1 1.0 copy-done.3
  121.1 7.8 %shard_map.99 = (bf16[224,1024]{1,0:T(8,128)(2,1)}, bf16[224,1024]{1,0:T(8,128)(2,1)S(1)}) custom-call(s32[4]{0:T(128)S(1)} %pad_add_fusion.meta, bf16[4,448,256]{2,1,0:T(8,128)(2,1)S(1)} %pad_maximum_fusion.refs_0_, bf16[4,448,256]{2,1,0:T(8,128)(2,1)} %collective-permute-done.5.refs_1_, bf16[4,448,256]{2,1,0:T(8,128)(2,1)} %collective-permute-done.6.refs_2_, ...), custom_call_target="tpu_custom_call" | custom-call | tf_op jit(solution)/shard_map/pallas_call | solution.py:275
  129.0 0.8 copy-done.16
  129.7 1.2 collective-permute-start.20
  130.9 1.2 copy-done.7
  132.1 1.8 %shard_map.96 = (bf16[16,64,768]{2,1,0:T(8,128)(2,1)S(1)}, f32[448,1024]{1,0:T(8,128)S(1)}) custom-call(s32[1,8]{1,0:T(1,128)S(1)} %copy-done.14, s32[1,8]{1,0:T(1,128)S(1)} %copy-done.15, bf16[16,64,768]{2,1,0:T(8,128)(2,1)S(1)} %bitcast.28, bf16[1024,256]{1,0:T(8,128)(2,1)S(1)} %copy-done, bf16[448,1024]{1,0:T(8,128)(2,1)S(1)} %bitcast.30, ...), custom_call_target="tpu_custom_call" | custom-call | tf_op jit(solution)/shard_map/pallas_call | solution.py:284
  133.9 1.3 copy-done.8
  135.2 1.1 copy-done.10
  136.3 4.9 %all-to-all-start.4 = ((bf16[8,2,64,768]{3,2,1,0:T(8,128)(2,1)}), bf16[8,2,64,768]{3,2,1,0:T(8,128)(2,1)S(1)}, u32[]{:S(2)}, u32[]{:S(2)}) async-start(bf16[8,2,64,768]{3,2,1,0:T(8,128)(2,1)} %bitcast.31), calls=%async_computation.4 | async-start | bytes 3145728 | tf_op jit(solution)/shard_map/all_to_all | solution.py:289
  141.2 1.5 collective-permute-start.24
  142.7 1.0 copy-done.4
  143.8 10.1 %shard_map.98 = (f32[224,1024]{1,0:T(8,128)S(1)}, bf16[224,1024]{1,0:T(8,128)(2,1)S(1)}, bf16[224,1024]{1,0:T(8,128)(2,1)S(1)}, f32[224,1024]{1,0:T(8,128)S(1)}) custom-call(s32[4]{0:T(128)S(1)} %pad_add_fusion.meta, bf16[4,448,256]{2,1,0:T(8,128)(2,1)S(1)} %pad_maximum_fusion.refs_0_, bf16[4,448,256]{2,1,0:T(8,128)(2,1)} %collective-permute-done.5.refs_1_, ...), custom_call_target="tpu_custom_call" | custom-call | tf_op jit(solution)/shard_map/pallas_call | solution.py:277
  153.9 0.1 collective-permute-start.22
  154.0 2.7 %collective-permute-start.23 = (bf16[224,1024]{1,0:T(8,128)(2,1)S(1)}, bf16[224,1024]{1,0:T(8,128)(2,1)S(1)}, u32[]{:S(2)}, u32[]{:S(2)}) collective-permute-start(bf16[224,1024]{1,0:T(8,128)(2,1)S(1)} %get-tuple-element.41), channel_id=1, source_target_pairs={{0,3},{1,0},{2,1},{3,2},{4,7},{5,4},{6,5},{7,6},{8,11},{9,8},{10,9... | collective-permute-start | bytes 1376264 | tf_op jit(solution)/shard_map/ppermute | solution.py:208
  156.6 1.3 add_convert_fusion.1
  158.0 0.3 collective-permute-start.21
  158.3 0.1 add_convert_fusion
  158.4 2.7 %collective-permute-start.25 = (bf16[224,1024]{1,0:T(8,128)(2,1)S(1)}, bf16[224,1024]{1,0:T(8,128)(2,1)S(1)}, u32[]{:S(2)}, u32[]{:S(2)}) collective-permute-start(bf16[224,1024]{1,0:T(8,128)(2,1)S(1)} %add_convert_fusion), channel_id=1, source_target_pairs={{0,3},{1,0},{2,1},{3,2},{4,7},{5,4},{6,5},{7,6},{8,11},{9,8},{10,9... | collective-permute-start | bytes 1376264 | tf_op jit(solution)/shard_map/ppermute | solution.py:208
  161.1 7.1 %shard_map.97.base = f32[448,1024]{1,0:T(8,128)S(1)} custom-call(s32[4]{0:T(128)S(1)} %pad_add_fusion.meta, bf16[4,448,256]{2,1,0:T(8,128)(2,1)S(1)} %pad_maximum_fusion.refs_0_, bf16[4,448,256]{2,1,0:T(8,128)(2,1)} %collective-permute-done.5.refs_1_, bf16[4,448,256]{2,1,0:T(8,128)(2,1)} %collective-permute-done.6.refs_2_, ...), custom_call_target="tpu_custom_call" | custom-call | tf_op jit(solution)/shard_map/pallas_call | solution.py:296
  168.3 8.3 %collective-permute-done.21.up_late = bf16[224,1024]{1,0:T(8,128)(2,1)S(1)} collective-permute-done((bf16[224,1024]{1,0:T(8,128)(2,1)S(1)}, bf16[224,1024]{1,0:T(8,128)(2,1)S(1)}, u32[]{:S(2)}, u32[]{:S(2)}) %collective-permute-start.21) | collective-permute-done | bytes 458784 | tf_op jit(solution)/shard_map/ppermute | solution.py:208
  176.6 1.2 shard_map.100
  177.8 2.2 %shard_map.101 = (f32[8,64,256]{2,1,0:T(8,128)}, f32[8,64,448]{2,1,0:T(8,128)}) custom-call(s32[1]{0:T(128)} %bitcast.4.me, s32[8,8]{1,0:T(8,128)S(1)} %bitcast.35, bf16[8,2,64,768]{3,2,1,0:T(8,128)(2,1)S(1)} %all-to-all-done.4.terms), custom_call_target="tpu_custom_call" | custom-call | tf_op jit(solution)/shard_map/pallas_call | solution.py:290
  (57 shorter events, 0.1 us)
Async XLA Ops:
  0.6 13.2 %copy-start.14 = (s32[1,8]{1,0:T(1,128)S(1)}, s32[1,8]{1,0:T(1,128)}, u32[]{:S(2)}) copy-start(s32[1,8]{1,0:T(1,128)} %used.3) | copy-start | bytes 100
  0.6 23.8 %copy-start.12 = (bf16[8,64,448]{2,1,0:T(8,128)(2,1)S(1)}, bf16[8,64,448]{2,1,0:T(8,128)(2,1)}, u32[]{:S(2)}) copy-start(bf16[8,64,448]{2,1,0:T(8,128)(2,1)} %up.1) | copy-start | bytes 1376260
  0.7 23.8 %copy-start.13 = (bf16[8,256,64]{1,2,0:T(8,128)(2,1)S(1)}, bf16[8,256,64]{1,2,0:T(8,128)(2,1)}, u32[]{:S(2)}) copy-start(bf16[8,256,64]{1,2,0:T(8,128)(2,1)} %param.10) | copy-start | bytes 786436
  0.7 26.0 %collective-permute-start.4 = (bf16[1024,256]{1,0:T(8,128)(2,1)}, bf16[1024,256]{1,0:T(8,128)(2,1)}, u32[]{:S(2)}, u32[]{:S(2)}) collective-permute-start(bf16[1024,256]{1,0:T(8,128)(2,1)} %refs_10_.5), channel_id=1, source_target_pairs={{0,28},{4,0},{8,4},{12,8},{16,12},{20,16},{24,20},{28,24},{1,29},{... | collective-permute-start | bytes 1572872 | tf_op jit(solution)/shard_map/ppermute | solution.py:208
  7.1 19.5 %collective-permute-start.3 = (bf16[1024,256]{1,0:T(8,128)(2,1)}, bf16[1024,256]{1,0:T(8,128)(2,1)S(1)}, u32[]{:S(2)}, u32[]{:S(2)}) collective-permute-start(bf16[1024,256]{1,0:T(8,128)(2,1)} %refs_10_.5), channel_id=1, source_target_pairs={{0,4},{4,8},{8,12},{12,16},{16,20},{20,24},{24,28},{28,0},{1,5},{5... | collective-permute-start | bytes 1572872 | tf_op jit(solution)/shard_map/ppermute | solution.py:208
  9.5 17.1 %collective-permute-start.2 = (bf16[448,256]{1,0:T(8,128)(2,1)S(1)}, bf16[448,256]{1,0:T(8,128)(2,1)S(1)}, u32[]{:S(2)}, u32[]{:S(2)}) collective-permute-start(bf16[448,256]{1,0:T(8,128)(2,1)S(1)} %get-tuple-element.47), channel_id=1, source_target_pairs={{0,1},{1,2},{2,3},{3,0},{4,5},{5,6},{6,7},{7,4},{8,9},{9,10},{10,1... | collective-permute-start | bytes 688136 | tf_op jit(solution)/shard_map/ppermute | solution.py:208
  10.8 15.8 %collective-permute-start = (bf16[448,256]{1,0:T(8,128)(2,1)S(1)}, bf16[448,256]{1,0:T(8,128)(2,1)S(1)}, u32[]{:S(2)}, u32[]{:S(2)}) collective-permute-start(bf16[448,256]{1,0:T(8,128)(2,1)S(1)} %get-tuple-element.48), channel_id=1, source_target_pairs={{0,3},{1,0},{2,1},{3,2},{4,7},{5,4},{6,5},{7,6},{8,11},{9,8},{10,9... | collective-permute-start | bytes 688136 | tf_op jit(solution)/shard_map/ppermute | solution.py:208
  12.2 14.4 %collective-permute-start.1 = (bf16[448,256]{1,0:T(8,128)(2,1)S(1)}, bf16[448,256]{1,0:T(8,128)(2,1)S(1)}, u32[]{:S(2)}, u32[]{:S(2)}) collective-permute-start(bf16[448,256]{1,0:T(8,128)(2,1)S(1)} %get-tuple-element.50), channel_id=1, source_target_pairs={{0,2},{1,3},{2,0},{3,1},{4,6},{5,7},{6,4},{7,5},{8,10},{9,11},{10,... | collective-permute-start | bytes 688136 | tf_op jit(solution)/shard_map/ppermute | solution.py:208
  25.4 1.2 copy-start.1
  26.6 4.9 %copy-start.17 = (bf16[448,256]{1,0:T(8,128)(2,1)}, bf16[448,256]{1,0:T(8,128)(2,1)S(1)}, u32[]{:S(2)}) copy-start(bf16[448,256]{1,0:T(8,128)(2,1)S(1)} %collective-permute-done.2) | copy-start | bytes 688132
  26.6 4.9 %copy-start.18 = (bf16[448,256]{1,0:T(8,128)(2,1)}, bf16[448,256]{1,0:T(8,128)(2,1)S(1)}, u32[]{:S(2)}) copy-start(bf16[448,256]{1,0:T(8,128)(2,1)S(1)} %collective-permute-done) | copy-start | bytes 688132
  26.6 0.8 copy-start.19
  27.4 5.6 %copy-start.2 = (bf16[1024,256]{1,0:T(8,128)(2,1)}, bf16[1024,256]{1,0:T(8,128)(2,1)S(1)}, u32[]{:S(2)}) copy-start(bf16[1024,256]{1,0:T(8,128)(2,1)S(1)} %collective-permute-done.3.refs_11_) | copy-start | bytes 1572868
  27.4 27.0 %copy-start = (bf16[1024,256]{1,0:T(8,128)(2,1)S(1)}, bf16[1024,256]{1,0:T(8,128)(2,1)}, u32[]{:S(2)}) copy-start(bf16[1024,256]{1,0:T(8,128)(2,1)} %refs_10_.5) | copy-start | bytes 1572868
  27.4 27.0 %copy-start.15 = (s32[1,8]{1,0:T(1,128)S(1)}, s32[1,8]{1,0:T(1,128)}, u32[]{:S(2)}) copy-start(s32[1,8]{1,0:T(1,128)} %order.3) | copy-start | bytes 100
  27.4 27.0 %all-to-all-start.1 = ((bf16[8,2,64,768]{3,2,1,0:T(8,128)(2,1)}), bf16[8,2,64,768]{3,2,1,0:T(8,128)(2,1)S(1)}, u32[]{:S(2)}, u32[]{:S(2)}) async-start(bf16[8,2,64,768]{3,2,1,0:T(8,128)(2,1)} %copy-done.1), calls=%async_computation.1 | async-start | bytes 3145728 | tf_op jit(solution)/shard_map/all_to_all | solution.py:248
  31.5 15.3 %collective-permute-start.7 = (bf16[1024,256]{1,0:T(8,128)(2,1)S(1)}, bf16[1024,256]{1,0:T(8,128)(2,1)}, u32[]{:S(2)}, u32[]{:S(2)}) collective-permute-start(bf16[1024,256]{1,0:T(8,128)(2,1)S(1)} %collective-permute-done.3.refs_11_), channel_id=1, source_target_pairs={{0,4},{4,8},{8,12},{12,16},{16,20},{20,24},{24,28},{28,0},{1,5},{5... | collective-permute-start | bytes 1572872 | tf_op jit(solution)/shard_map/ppermute | solution.py:208
  33.0 37.6 %collective-permute-start.6 = (bf16[4,448,256]{2,1,0:T(8,128)(2,1)S(1)}, bf16[4,448,256]{2,1,0:T(8,128)(2,1)}, u32[]{:S(2)}, u32[]{:S(2)}) collective-permute-start(bf16[4,448,256]{2,1,0:T(8,128)(2,1)S(1)} %pad_maximum_fusion.refs_0_), channel_id=1, source_target_pairs={{0,192},{64,0},{128,64},{192,128},{1,193},{65,1},{129,65},{193,129... | collective-permute-start | bytes 2752520 | tf_op jit(solution)/shard_map/ppermute | solution.py:208
  35.7 36.3 %collective-permute-start.5 = (bf16[4,448,256]{2,1,0:T(8,128)(2,1)S(1)}, bf16[4,448,256]{2,1,0:T(8,128)(2,1)}, u32[]{:S(2)}, u32[]{:S(2)}) collective-permute-start(bf16[4,448,256]{2,1,0:T(8,128)(2,1)S(1)} %pad_maximum_fusion.refs_0_), channel_id=1, source_target_pairs={{0,64},{64,128},{128,192},{192,0},{1,65},{65,129},{129,193},{193,1... | collective-permute-start | bytes 2752520 | tf_op jit(solution)/shard_map/ppermute | solution.py:208
  35.7 45.8 %collective-permute-start.11 = (bf16[4,448,256]{2,1,0:T(8,128)(2,1)S(1)}, bf16[4,448,256]{2,1,0:T(8,128)(2,1)}, u32[]{:S(2)}, u32[]{:S(2)}) collective-permute-start(bf16[4,448,256]{2,1,0:T(8,128)(2,1)S(1)} %pad_maximum_fusion.refs_0_), channel_id=1, source_target_pairs={{0,32},{32,0},{1,33},{33,1},{2,34},{34,2},{3,35},{35,3},{4,36},{36... | collective-permute-start | bytes 2752520 | tf_op jit(solution)/shard_map/ppermute | solution.py:208
  36.3 14.6 %collective-permute-start.8 = (bf16[1024,256]{1,0:T(8,128)(2,1)}, bf16[1024,256]{1,0:T(8,128)(2,1)}, u32[]{:S(2)}, u32[]{:S(2)}) collective-permute-start(bf16[1024,256]{1,0:T(8,128)(2,1)} %collective-permute-done.4.refs_12_), channel_id=1, source_target_pairs={{0,28},{4,0},{8,4},{12,8},{16,12},{20,16},{24,20},{28,24},{1,29},{... | collective-permute-start | bytes 1572872 | tf_op jit(solution)/shard_map/ppermute | solution.py:208
  46.8 36.2 %collective-permute-start.16 = (bf16[1024,256]{1,0:T(8,128)(2,1)}, bf16[1024,256]{1,0:T(8,128)(2,1)S(1)}, u32[]{:S(2)}, u32[]{:S(2)}) collective-permute-start(bf16[1024,256]{1,0:T(8,128)(2,1)} %collective-permute-done.7.refs_13_), channel_id=1, source_target_pairs={{0,4},{4,8},{8,12},{12,16},{16,20},{20,24},{24,28},{28,0},{1,5},{5... | collective-permute-start | bytes 1572872 | tf_op jit(solution)/shard_map/ppermute | solution.py:208
  50.9 32.9 %collective-permute-start.17 = (bf16[1024,256]{1,0:T(8,128)(2,1)}, bf16[1024,256]{1,0:T(8,128)(2,1)}, u32[]{:S(2)}, u32[]{:S(2)}) collective-permute-start(bf16[1024,256]{1,0:T(8,128)(2,1)} %collective-permute-done.8.refs_14_), channel_id=1, source_target_pairs={{0,28},{4,0},{8,4},{12,8},{16,12},{20,16},{24,20},{28,24},{1,29},{... | collective-permute-start | bytes 1572872 | tf_op jit(solution)/shard_map/ppermute | solution.py:208
  54.4 1.2 copy-start.6
  56.7 0.7 copy-start.11
  71.9 22.7 %all-to-all-start.2 = ((bf16[32,32,128]{2,1,0:T(8,128)(2,1)}), bf16[32,32,128]{2,1,0:T(8,128)(2,1)}, u32[]{:S(2)}, u32[]{:S(2)}) async-start(bf16[32,32,128]{2,1,0:T(8,128)(2,1)} %bitcast.32), calls=%async_computation.2 | async-start | bytes 524288 | tf_op jit(solution)/shard_map/all_to_all | solution.py:264
  79.9 11.2 %collective-permute-start.10 = (bf16[2,448,256]{2,1,0:T(8,128)(2,1)S(1)}, bf16[2,448,256]{2,1,0:T(8,128)(2,1)}, u32[]{:S(2)}, u32[]{:S(2)}) collective-permute-start(bf16[2,448,256]{2,1,0:T(8,128)(2,1)S(1)} %slice.13), channel_id=1, source_target_pairs={{0,192},{64,0},{128,64},{192,128},{1,193},{65,1},{129,65},{193,129... | collective-permute-start | bytes 1376264 | tf_op jit(solution)/shard_map/ppermute | solution.py:208
  80.4 12.6 %collective-permute-start.9 = (bf16[2,448,256]{2,1,0:T(8,128)(2,1)S(1)}, bf16[2,448,256]{2,1,0:T(8,128)(2,1)}, u32[]{:S(2)}, u32[]{:S(2)}) collective-permute-start(bf16[2,448,256]{2,1,0:T(8,128)(2,1)S(1)} %slice.12), channel_id=1, source_target_pairs={{0,64},{64,128},{128,192},{192,0},{1,65},{65,129},{129,193},{193,1... | collective-permute-start | bytes 1376264 | tf_op jit(solution)/shard_map/ppermute | solution.py:208
  81.4 38.6 %collective-permute-start.12 = (bf16[4,448,256]{2,1,0:T(8,128)(2,1)}, bf16[4,448,256]{2,1,0:T(8,128)(2,1)}, u32[]{:S(2)}, u32[]{:S(2)}) collective-permute-start(bf16[4,448,256]{2,1,0:T(8,128)(2,1)} %collective-permute-done.5.refs_1_), channel_id=1, source_target_pairs={{0,32},{32,0},{1,33},{33,1},{2,34},{34,2},{3,35},{35,3},{4,36},{36... | collective-permute-start | bytes 2752520 | tf_op jit(solution)/shard_map/ppermute | solution.py:208
  83.0 37.1 %collective-permute-start.13 = (bf16[4,448,256]{2,1,0:T(8,128)(2,1)}, bf16[4,448,256]{2,1,0:T(8,128)(2,1)}, u32[]{:S(2)}, u32[]{:S(2)}) collective-permute-start(bf16[4,448,256]{2,1,0:T(8,128)(2,1)} %collective-permute-done.6.refs_2_), channel_id=1, source_target_pairs={{0,32},{32,0},{1,33},{33,1},{2,34},{34,2},{3,35},{35,3},{4,36},{36... | collective-permute-start | bytes 2752520 | tf_op jit(solution)/shard_map/ppermute | solution.py:208
  83.8 24.9 %collective-permute-start.18 = (bf16[512,256]{1,0:T(8,128)(2,1)}, bf16[512,256]{1,0:T(8,128)(2,1)}, u32[]{:S(2)}, u32[]{:S(2)}) collective-permute-start(bf16[512,256]{1,0:T(8,128)(2,1)} %slice.16), channel_id=1, source_target_pairs={{0,4},{4,8},{8,12},{12,16},{16,20},{20,24},{24,28},{28,0},{1,5},{5... | collective-permute-start | bytes 786440 | tf_op jit(solution)/shard_map/ppermute | solution.py:208
  91.1 29.0 %collective-permute-start.15 = (bf16[2,448,256]{2,1,0:T(8,128)(2,1)}, bf16[2,448,256]{2,1,0:T(8,128)(2,1)}, u32[]{:S(2)}, u32[]{:S(2)}) collective-permute-start(bf16[2,448,256]{2,1,0:T(8,128)(2,1)} %collective-permute-done.10.refs_4_), channel_id=1, source_target_pairs={{0,32},{32,0},{1,33},{33,1},{2,34},{34,2},{3,35},{35,3},{4,36},{36... | collective-permute-start | bytes 1376264 | tf_op jit(solution)/shard_map/ppermute | solution.py:208
  93.0 27.1 %collective-permute-start.14 = (bf16[2,448,256]{2,1,0:T(8,128)(2,1)}, bf16[2,448,256]{2,1,0:T(8,128)(2,1)}, u32[]{:S(2)}, u32[]{:S(2)}) collective-permute-start(bf16[2,448,256]{2,1,0:T(8,128)(2,1)} %collective-permute-done.9.refs_3_), channel_id=1, source_target_pairs={{0,32},{32,0},{1,33},{33,1},{2,34},{34,2},{3,35},{35,3},{4,36},{36... | collective-permute-start | bytes 1376264 | tf_op jit(solution)/shard_map/ppermute | solution.py:208
  97.7 33.2 %all-to-all-start.3 = ((bf16[32,32,128]{2,1,0:T(8,128)(2,1)}), bf16[32,32,128]{2,1,0:T(8,128)(2,1)}, u32[]{:S(2)}, u32[]{:S(2)}) async-start(bf16[32,32,128]{2,1,0:T(8,128)(2,1)} %broadcast_in_dim.16), calls=%async_computation.3 | async-start | bytes 524288 | tf_op jit(solution)/shard_map/all_to_all | solution.py:266
  108.7 11.4 %collective-permute-start.19 = (bf16[512,256]{1,0:T(8,128)(2,1)}, bf16[512,256]{1,0:T(8,128)(2,1)}, u32[]{:S(2)}, u32[]{:S(2)}) collective-permute-start(bf16[512,256]{1,0:T(8,128)(2,1)} %slice.17), channel_id=1, source_target_pairs={{0,28},{4,0},{8,4},{12,8},{16,12},{20,16},{24,20},{28,24},{1,29},{... | collective-permute-start | bytes 786440 | tf_op jit(solution)/shard_map/ppermute | solution.py:208
  120.1 1.0 copy-start.3
  129.0 0.8 copy-start.16
  129.7 26.9 %collective-permute-start.20 = (bf16[224,1024]{1,0:T(8,128)(2,1)}, bf16[224,1024]{1,0:T(8,128)(2,1)}, u32[]{:S(2)}, u32[]{:S(2)}) collective-permute-start(bf16[224,1024]{1,0:T(8,128)(2,1)} %get-tuple-element.39), channel_id=1, source_target_pairs={{0,1},{1,2},{2,3},{3,0},{4,5},{5,6},{6,7},{7,4},{8,9},{9,10},{10,1... | collective-permute-start | bytes 1376264 | tf_op jit(solution)/shard_map/ppermute | solution.py:208
  130.9 1.2 copy-start.7
  133.9 1.3 copy-start.8
  135.2 1.1 copy-start.10
  136.3 41.5 %all-to-all-start.4 = ((bf16[8,2,64,768]{3,2,1,0:T(8,128)(2,1)}), bf16[8,2,64,768]{3,2,1,0:T(8,128)(2,1)S(1)}, u32[]{:S(2)}, u32[]{:S(2)}) async-start(bf16[8,2,64,768]{3,2,1,0:T(8,128)(2,1)} %bitcast.31), calls=%async_computation.4 | async-start | bytes 3145728 | tf_op jit(solution)/shard_map/all_to_all | solution.py:289
  141.2 17.1 %collective-permute-start.24 = (bf16[224,1024]{1,0:T(8,128)(2,1)}, bf16[224,1024]{1,0:T(8,128)(2,1)S(1)}, u32[]{:S(2)}, u32[]{:S(2)}) collective-permute-start(bf16[224,1024]{1,0:T(8,128)(2,1)} %copy-done.16), channel_id=1, source_target_pairs={{0,3},{1,0},{2,1},{3,2},{4,7},{5,4},{6,5},{7,6},{8,11},{9,8},{10,9... | collective-permute-start | bytes 1376264 | tf_op jit(solution)/shard_map/ppermute | solution.py:208
  142.7 1.0 copy-start.4
  153.9 14.4 %collective-permute-start.22 = (bf16[224,1024]{1,0:T(8,128)(2,1)S(1)}, bf16[224,1024]{1,0:T(8,128)(2,1)S(1)}, u32[]{:S(2)}, u32[]{:S(2)}) collective-permute-start(bf16[224,1024]{1,0:T(8,128)(2,1)S(1)} %get-tuple-element.40), channel_id=1, source_target_pairs={{0,1},{1,2},{2,3},{3,0},{4,5},{5,6},{6,7},{7,4},{8,9},{9,10},{10,1... | collective-permute-start | bytes 1376264 | tf_op jit(solution)/shard_map/ppermute | solution.py:208
  154.0 14.3 %collective-permute-start.23 = (bf16[224,1024]{1,0:T(8,128)(2,1)S(1)}, bf16[224,1024]{1,0:T(8,128)(2,1)S(1)}, u32[]{:S(2)}, u32[]{:S(2)}) collective-permute-start(bf16[224,1024]{1,0:T(8,128)(2,1)S(1)} %get-tuple-element.41), channel_id=1, source_target_pairs={{0,3},{1,0},{2,1},{3,2},{4,7},{5,4},{6,5},{7,6},{8,11},{9,8},{10,9... | collective-permute-start | bytes 1376264 | tf_op jit(solution)/shard_map/ppermute | solution.py:208
  156.6 4.5 %copy-start.5 = (bf16[1024,256]{1,0:T(8,128)(2,1)S(1)}, bf16[1024,256]{1,0:T(8,128)(2,1)}, u32[]{:S(2)}) copy-start(bf16[1024,256]{1,0:T(8,128)(2,1)} %copy-done.2) | copy-start | bytes 1572868
  156.6 4.5 %copy-start.9 = (f32[448,1024]{1,0:T(8,128)S(1)}, f32[448,1024]{1,0:T(8,128)}, u32[]{:S(2)}) copy-start(f32[448,1024]{1,0:T(8,128)} %copy-done.8) | copy-start | bytes 5505028
  158.0 18.7 %collective-permute-start.21 = (bf16[224,1024]{1,0:T(8,128)(2,1)S(1)}, bf16[224,1024]{1,0:T(8,128)(2,1)S(1)}, u32[]{:S(2)}, u32[]{:S(2)}) collective-permute-start(bf16[224,1024]{1,0:T(8,128)(2,1)S(1)} %add_convert_fusion.1), channel_id=1, source_target_pairs={{0,1},{1,2},{2,3},{3,0},{4,5},{5,6},{6,7},{7,4},{8,9},{9,10},{10,1... | collective-permute-start | bytes 1376264 | tf_op jit(solution)/shard_map/ppermute | solution.py:208
  158.4 18.2 %collective-permute-start.25 = (bf16[224,1024]{1,0:T(8,128)(2,1)S(1)}, bf16[224,1024]{1,0:T(8,128)(2,1)S(1)}, u32[]{:S(2)}, u32[]{:S(2)}) collective-permute-start(bf16[224,1024]{1,0:T(8,128)(2,1)S(1)} %add_convert_fusion), channel_id=1, source_target_pairs={{0,3},{1,0},{2,1},{3,2},{4,7},{5,4},{6,5},{7,6},{8,11},{9,8},{10,9... | collective-permute-start | bytes 1376264 | tf_op jit(solution)/shard_map/ppermute | solution.py:208

commit v4 on v1

--- a/solution.py
+++ b/solution.py
@@ -13,7 +13,6 @@
 MP = ("z", "y")
 VMEM = pl.BlockSpec(memory_space=pltpu.VMEM)
 SMEM = pl.BlockSpec(memory_space=pltpu.SMEM)
-LIMIT = 40 * 1024 * 1024
 
 
 def pair_of(used, group, owner, per_owner, slots):
@@ -108,13 +107,47 @@
                 grad_b[local] += terms[group, place, :, width:width + units].astype(F32)
 
 
-def call(kernel, outs, specs):
+def place_kernel(meta, *refs):
+    out = refs[-1]
+    count, units, _ = out.shape
+    width = refs[0].shape[1]
+    half = refs[3].shape[0]
+    x, core = meta[0], meta[1]
+    for other in range(2):
+        own, left, right, far_left, far_right = refs[5 * other:5 * other + 5]
+        for sources, step in (((own,), 0), ((left,), 3), ((right,), 1), ((far_left, far_right), 2)):
+            block = 2 * lax.rem(x + step, jnp.int32(4)) + (1 - core if other else core)
+            spot = pl.ds(pl.multiple_of(block * width, width), width)
+            for r in range(count):
+                for start in range(0, units, units // 2):
+                    at = r * units + start
+                    source = sources[at // half] if len(sources) == 2 else sources[0]
+                    low = at % half if len(sources) == 2 else at
+                    out[r, start:start + units // 2, spot] = source[low:low + units // 2, :]
+
+
+def copy_kernel(meta, source, out):
+    out[...] = source[...]
+
+
+def join_kernel(base, up_late, up_soon, down_soon, down_late, out):
+    half = up_late.shape[0]
+    out[0:half, :] = (
+        base[0:half, :] + up_late[...].astype(F32) + down_soon[...].astype(F32)
+    ).astype(BF)
+    out[half:, :] = (
+        base[half:, :] + up_soon[...].astype(F32) + down_late[...].astype(F32)
+    ).astype(BF)
+
+
+def call(kernel, outs, specs, scratch=(), limit=16):
     return pl.pallas_call(
         kernel,
         out_shape=outs,
         in_specs=specs,
         out_specs=jax.tree.map(lambda _: VMEM, outs),
-        compiler_params=pltpu.CompilerParams(vmem_limit_bytes=LIMIT),
+        scratch_shapes=scratch,
+        compiler_params=pltpu.CompilerParams(vmem_limit_bytes=limit * 1024 * 1024),
     )
 
 
@@ -134,27 +167,31 @@
     me = lax.axis_index(DP)
     whole = jax.ShapeDtypeStruct
 
+    together = lax.optimization_barrier
+    x, core, z, y = (lax.axis_index(name) for name in ("x", "core", "z", "y"))
+    meta = jnp.stack([x, core, z, y]).astype(jnp.int32)
+    me_arr = me.reshape(1).astype(jnp.int32)
+
     wide_tokens = lax.all_gather(tokens, "z", axis=1, tiled=True)
 
     weight_t = weight.T
     piece = n_y * width
     mine = lax.dynamic_slice(weight_t, (0, me * piece), (units, piece))
-    spot = lax.axis_index("y")
-    pieces = [
-        hop(lax.dynamic_slice(mine, (0, lax.rem(spot + n_y - r, n_y) * width), (units, width)), "y", -r)
-        if r else lax.dynamic_slice(mine, (0, spot * width), (units, width))
-        for r in range(n_y)
-    ]
-    wide_weight = lax.all_gather(jnp.stack(pieces), DP, axis=2, tiled=True)
+    pieces = tuple(
+        hop(lax.dynamic_slice(mine, (0, lax.rem(y + n_y - r, n_y) * width), (units, width)), "y", -r)
+        for r in range(1, n_y)
+    )
 
     down_t = jnp.transpose(down, (0, 2, 1))
     used_all = lax.all_to_all(
         jnp.broadcast_to(used[None], (owners,) + used.shape), DP, 0, 0, tiled=True
     ).reshape(owners, used.shape[1])
-    me_arr = me.reshape(1).astype(jnp.int32)
     picked = call(pick_kernel, whole((owners, 2, rank, packed), BF), [SMEM, SMEM, VMEM, VMEM])(
         me_arr, used_all, down_t, up
     )
+    picked, pieces = together((picked, pieces))
+    own = jnp.concatenate(pieces, axis=0)
+    from_left, from_right = hop(own, "x", 1), hop(own, "x", -1)
     factors = lax.all_to_all(picked, DP, 0, 0, tiled=True).reshape(owners * 2, rank, packed)
     cot_t = cotangent.T
     sizes = dict(rank=rank, width=width, units=units)
@@ -163,12 +200,46 @@
         whole((rows, 2 * rank), BF),
         [SMEM, SMEM, VMEM, VMEM, VMEM],
     )(used, order, factors, tokens, cot_t)
+    part, weight_t = together((part, weight_t))
+    own_weight = pl.pallas_call(
+        copy_kernel,
+        out_shape=whole((units, n_z * width), BF),
+        grid_spec=pltpu.PrefetchScalarGridSpec(
+            num_scalar_prefetch=1,
+            grid=(n_z,),
+            in_specs=[pl.BlockSpec((units, width), lambda i, meta: (0, i * n_y + meta[3]))],
+            out_specs=pl.BlockSpec((units, width), lambda i, meta: (0, i)),
+        ),
+    )(meta, weight_t)
+    middle = own.shape[0] // 2
+    far_left, far_right = hop(from_left[:middle], "x", 1), hop(from_right[middle:], "x", -1)
+    held = (own, from_left, from_right, far_left, far_right)
+    swapped = tuple(hop(item, "core", 1) for item in held)
+    wide_weight = call(
+        place_kernel, whole((n_y - 1, units, n_z * width), BF), [SMEM] + [VMEM] * 10, limit=24
+    )(meta, *held, *swapped)
     share = rows // members
     parts = lax.all_to_all(part.reshape(members, share, 2 * rank), MP, 0, 0, tiled=True)
     summed = jnp.sum(parts.astype(F32), axis=0).astype(BF)
     both = lax.all_to_all(
         jnp.broadcast_to(summed[None], (members,) + summed.shape), MP, 0, 0, tiled=True
     ).reshape(rows, 2 * rank)
+
+    half = units // 2
+
+    def product(weights):
+        return lax.dot_general(
+            weights, wide_tokens, (((1,), (1,)), ((), ())), preferred_element_type=F32
+        )
+
+    near, far, back = (wide_weight[r] for r in range(3))
+    far_up = hop(product(far[:half]).astype(BF), "y", 1)
+    far_down = hop(product(far[half:]).astype(BF), "y", -1)
+    up_soon = hop(product(near[half:]).astype(BF), "y", 1)
+    down_soon = hop(product(back[:half]).astype(BF), "y", -1)
+    up_late = hop((product(near[:half]) + far_up.astype(F32)).astype(BF), "y", 1)
+    down_late = hop((product(back[half:]) + far_down.astype(F32)).astype(BF), "y", -1)
+
     send, delta = call(
         functools.partial(grads_kernel, **sizes),
         (whole((owners * 2, rank, packed), BF), whole((units, rows), F32)),
@@ -181,22 +252,11 @@
         [SMEM, SMEM, VMEM],
     )(me_arr, used_all, terms)
 
-    def product(r):
-        return lax.dot_general(
-            wide_weight[r], wide_tokens, (((1,), (1,)), ((), ())), preferred_element_type=F32
-        )
-
-    half = units // 2
-    far = product(2).astype(BF)
-    far_up, far_down = hop(far[:half], "y", 1), hop(far[half:], "y", -1)
-    near_up, near_down = product(1), product(n_y - 1)
-    near_up = jnp.concatenate([near_up[:half] + far_up.astype(F32), near_up[half:]]).astype(BF)
-    near_down = jnp.concatenate(
-        [near_down[:half], near_down[half:] + far_down.astype(F32)]
-    ).astype(BF)
-    got_up, got_down = hop(near_up, "y", 1), hop(near_down, "y", -1)
-    out = product(0) + delta + got_up.astype(F32) + got_down.astype(F32)
-    return out.astype(BF).T, jnp.transpose(grad_a, (0, 2, 1)), grad_b
+    base = together(product(own_weight) + delta)
+    out = call(join_kernel, whole((units, rows), BF), [VMEM] * 5)(
+        base, up_late, up_soon, down_soon, down_late
+    )
+    return out.T, jnp.transpose(grad_a, (0, 2, 1)), grad_b
 
 
 def solution(mesh):

time: 209 us -> 197 us (0.943)
  waiting for transfers between devices: 76.1 us -> 43.9 us
  starting transfers between devices: 17.8 us -> 31.5 us
  blocking collectives: 71.3 us -> 58.1 us
  local copies, waits for them, and re-layouts: 4.44 us -> 16.4 us
  Pallas kernels: 5.56 us -> 16 us
  other arithmetic: 3.29 us -> 0.64 us
    all_gather x1 -> x0, waiting for transfers between devices: 40.4 us -> none  [on_device(): wide_weight = lax.all_gather(jnp.stack(pieces), DP, axis=2, tiled=True)]
    all_to_all x1 -> x0, blocking collectives: 15.9 us -> none  [on_device(): lax.all_to_all(jnp.broadcast_to(summed[None], (members,) + summed.shape),...]
    pallas_call x0 -> x3, Pallas kernels: none -> 10.4 us  [the longest x1 6.38 us: on_device(): pl.pallas_call(copy_kernel, out_shape=whole((units, n_z * width), BF), gr...]
    ppermute x7 -> x18, starting transfers between devices: 10.9 us -> 20.2 us  [hop(): return lax.ppermute(value, axis, [(i, (i + step) % n) for i in range(n)])]
    unnamed x22 -> x32, local copies, waits for them, and re-layouts: 2.52 us -> 9.84 us
    ppermute x7 -> x18, waiting for transfers between devices: 34.9 us -> 39.5 us  [hop(): return lax.ppermute(value, axis, [(i, (i + step) % n) for i in range(n)])]
    all_to_all x1, blocking collectives: 19.8 us -> 24 us  [on_device(): lax.all_to_all(part.reshape(members, share, 2 * rank), MP, 0, 0, tiled=True)]
    all_to_all x0 -> x1, starting transfers between devices: none -> 3.96 us  [on_device(): lax.all_to_all(jnp.broadcast_to(summed[None], (members,) + summed.shape),...]
  transfers between devices with their start and end apart: 10 -> 21, of which waited for: 7 -> 7; matrix products, arithmetic and copies ran while one was open for 7% -> 11% of each run, Pallas kernels for 3% -> 8%
where the time goes in v4:
time: 197 us; the launch traced here: 196 us
  blocking collectives  58.1 us (29%)
  waiting for transfers between devices  43.9 us (22%)
  starting transfers between devices  31.5 us (16%)
  local copies, waits for them, and re-layouts  16.4 us (8%)
  Pallas kernels  16 us (8%)
  matrix products  15.5 us (8%)
  between operations  14.3 us (7%)
    ppermute x18, waiting for transfers between devices, hop(): return lax.ppermute(value, axis, [(i, (i + step) % n) for i in range(n)])  39.5 us
    all_to_all x1, blocking collectives, on_device(): lax.all_to_all(part.reshape(members, share, 2 * rank), MP, 0, 0, tiled=True)  24 us
    all_to_all x1, blocking collectives, on_device(): lax.all_to_all(picked, DP, 0, 0, tiled=True)  23.8 us
    ppermute x18, starting transfers between devices, hop(): return lax.ppermute(value, axis, [(i, (i + step) % n) for i in range(n)])  20.2 us
    dot_general x7, matrix products, product(): lax.dot_general(weights, wide_tokens, (((1,), (1,)), ((), ())), preferred...  15.5 us
    all_to_all x1, blocking collectives, on_device(): lax.all_to_all(jnp.broadcast_to(used[None], (owners,) + used.shape), DP,...  10.3 us
    unnamed x32, local copies, waits for them, and re-layouts  9.84 us
    all_to_all x1, starting transfers between devices, on_device(): lax.all_to_all(send.reshape(owners, 2, rank, packed), DP, 0, 0, tiled=True)  7.34 us
  transfers between devices with their start and end apart: 21, of which 7 were waited for; matrix products, arithmetic and copies ran while one was open for 11% of the time, Pallas kernels for 8%

profile of v4, /device:TPU:1, one launch (start us, length us, event | category | flops | bytes accessed | tf_op | source)
XLA Modules:
  0.0 196.3 jit_solution(4843648506198513975)
XLA Ops:
  7.2 0.0 copy-start.7
  7.2 0.0 all-gather.2.cloned.1.call-start
  7.3 0.7 all-gather.2.cloned.1.call-update
  8.0 1.5 dynamic-slice_bitcast_fusion
  9.5 3.6 %collective-permute-start = (bf16[448,256]{1,0:T(8,128)(2,1)S(1)}, bf16[448,256]{1,0:T(8,128)(2,1)S(1)}, u32[]{:S(2)}, u32[]{:S(2)}) collective-permute-start(bf16[448,256]{1,0:T(8,128)(2,1)S(1)} %get-tuple-element.25), channel_id=1, source_target_pairs={{0,3},{1,0},{2,1},{3,2},{4,7},{5,4},{6,5},{7,6},{8,11},{9,8},{10,9... | collective-permute-start | bytes 688136 | tf_op jit(solution)/shard_map/ppermute | solution.py:156
  13.1 0.3 collective-permute-start.1
  13.5 0.7 collective-permute-start.2
  14.2 0.7 broadcast_in_dim.7
  14.8 10.3 %all_to_all.25 = s32[8,1,8]{2,1,0:T(1,128)S(1)} all-to-all(s32[8,1,8]{2,1,0:T(1,128)S(1)} %broadcast_in_dim.7), channel_id=1, replica_groups=mesh['x'=4,'core'=2,'z'=8,'y'=4] {'x','core'}, dimensions={0} | all-to-all | bytes 512 | tf_op jit(solution)/shard_map/all_to_all | solution.py:186
  25.1 1.1 copy-done.5
  26.2 1.0 copy-done.6
  27.1 0.9 shard_map.94
  28.0 0.0 collective-permute-done.1
  28.0 0.0 copy-start.13
  28.1 0.7 copy-done.13
  28.7 23.8 %all_to_all.26 = bf16[8,2,64,768]{3,2,1,0:T(8,128)(2,1)S(1)} all-to-all(bf16[8,2,64,768]{3,2,1,0:T(8,128)(2,1)S(1)} %shard_map.94), channel_id=1, replica_groups=mesh['x'=4,'core'=2,'z'=8,'y'=4] {'x','core'}, dimensions={0} | all-to-all | bytes 3145728 | tf_op jit(solution)/shard_map/all_to_all | solution.py:195
  52.6 1.1 shard_map.95
  53.7 24.0 %all_to_all.27 = bf16[32,32,128]{2,1,0:T(8,128)(2,1)S(1)} all-to-all(bf16[32,32,128]{2,1,0:T(8,128)(2,1)S(1)} %bitcast.54), channel_id=1, replica_groups=mesh['x'=4,'core'=2,'z'=8,'y'=4] {'z','y'}, dimensions={0} | all-to-all | bytes 524288 | tf_op jit(solution)/shard_map/all_to_all | solution.py:222
  77.7 0.1 reduce_sum.12
  77.7 0.7 broadcast_in_dim.16
  78.5 4.0 %all-to-all-start.3 = ((bf16[32,32,128]{2,1,0:T(8,128)(2,1)}), bf16[32,32,128]{2,1,0:T(8,128)(2,1)S(1)}, u32[]{:S(2)}, u32[]{:S(2)}) async-start(bf16[32,32,128]{2,1,0:T(8,128)(2,1)} %broadcast_in_dim.16), calls=%async_computation.3 | async-start | bytes 524288 | tf_op jit(solution)/shard_map/all_to_all | solution.py:224
  82.4 0.7 constant_dynamic-update-slice_fusion.2
  83.1 1.6 constant_dynamic-update-slice_fusion.1
  84.8 1.6 constant_dynamic-update-slice_fusion.refs_0_
  86.4 0.6 collective-permute-start.3
  87.0 2.1 %collective-permute-start.4 = (bf16[1344,256]{1,0:T(8,128)(2,1)}, bf16[1344,256]{1,0:T(8,128)(2,1)}, u32[]{:S(2)}, u32[]{:S(2)}) collective-permute-start(bf16[1344,256]{1,0:T(8,128)(2,1)} %constant_dynamic-update-slice_fusion.refs_0_), channel_id=1, source_target_pairs={{0,192},{64,0},{128,64},{192,128},{1,193},{65,1},{129,65},{193,129... | collective-permute-start | bytes 2064392 | tf_op jit(solution)/shard_map/ppermute | solution.py:156
  89.1 3.7 %all-to-all-done.3 = bf16[32,32,128]{2,1,0:T(8,128)(2,1)S(1)} async-done(((bf16[32,32,128]{2,1,0:T(8,128)(2,1)}), bf16[32,32,128]{2,1,0:T(8,128)(2,1)S(1)}, u32[]{:S(2)}, u32[]{:S(2)}) %all-to-all-start.3) | async-done | bytes 262176 | tf_op jit(solution)/shard_map/all_to_all | solution.py:224
  92.8 1.4 shard_map.97
  94.2 1.1 copy-done.4
  95.4 1.2 copy-done.10
  96.6 7.3 %all-to-all-start.4 = ((bf16[8,2,64,768]{3,2,1,0:T(8,128)(2,1)}), bf16[8,2,64,768]{3,2,1,0:T(8,128)(2,1)S(1)}, u32[]{:S(2)}, u32[]{:S(2)}) async-start(bf16[8,2,64,768]{3,2,1,0:T(8,128)(2,1)} %bitcast.52), calls=%async_computation.4 | async-start | bytes 3145728 | tf_op jit(solution)/shard_map/all_to_all | solution.py:248
  103.9 0.2 collective-permute-start.7
  104.1 1.0 slice.65
  105.1 1.6 collective-permute-start.5
  106.8 1.0 slice.66
  107.8 1.3 collective-permute-start.6
  109.1 2.1 %collective-permute-start.8 = (bf16[1344,256]{1,0:T(8,128)(2,1)}, bf16[1344,256]{1,0:T(8,128)(2,1)S(1)}, u32[]{:S(2)}, u32[]{:S(2)}) collective-permute-start(bf16[1344,256]{1,0:T(8,128)(2,1)} %collective-permute-done.3.refs_1_), channel_id=1, source_target_pairs={{0,32},{32,0},{1,33},{33,1},{2,34},{34,2},{3,35},{35,3},{4,36},{36... | collective-permute-start | bytes 2064392 | tf_op jit(solution)/shard_map/ppermute | solution.py:156
  111.2 20.7 %collective-permute-done.5.refs_3_ = bf16[672,256]{1,0:T(8,128)(2,1)S(1)} collective-permute-done((bf16[672,256]{1,0:T(8,128)(2,1)S(1)}, bf16[672,256]{1,0:T(8,128)(2,1)S(1)}, u32[]{:S(2)}, u32[]{:S(2)}) %collective-permute-start.5) | collective-permute-done | bytes 344096 | tf_op jit(solution)/shard_map/ppermute | solution.py:156
  131.9 0.7 collective-permute-start.10
  132.6 0.0 collective-permute-start.11
  132.6 0.6 pad_add_fusion.meta
  133.2 6.4 %shard_map.96 = bf16[448,2048]{1,0:T(8,128)(2,1)} custom-call(s32[4]{0:T(128)} %pad_add_fusion.meta, bf16[448,8192]{1,0:T(8,128)(2,1)} %bitcast.59), custom_call_target="tpu_custom_call" | custom-call | tf_op jit(solution)/shard_map/pallas_call | solution.py:204
  139.7 2.8 %shard_map.98 = bf16[3,448,2048]{2,1,0:T(8,128)(2,1)S(1)} custom-call(s32[4]{0:T(128)S(1)} %copy-done.8, bf16[1344,256]{1,0:T(8,128)(2,1)} %constant_dynamic-update-slice_fusion.refs_0_, bf16[1344,256]{1,0:T(8,128)(2,1)} %collective-permute-done.3.refs_1_, bf16[1344,256]{1,0:T(8,128)(2,1)} %collective-permute-done.4.refs_2_, ...), custom_call_target="tpu_custom_call" | custom-call | tf_op jit(solution)/shard_map/pallas_call | solution.py:218
  142.5 2.4 %copy-done = bf16[3,448,2048]{2,1,0:T(8,128)(2,1)} copy-done((bf16[3,448,2048]{2,1,0:T(8,128)(2,1)}, bf16[3,448,2048]{2,1,0:T(8,128)(2,1)S(1)}, u32[]{:S(2)}) %copy-start) | copy-done | bytes 5505048
  144.9 2.2 %shard_map.100 = (f32[8,64,256]{2,1,0:T(8,128)}, f32[8,64,448]{2,1,0:T(8,128)}) custom-call(s32[1]{0:T(128)} %bitcast.4.me, s32[8,8]{1,0:T(8,128)S(1)} %bitcast.57, bf16[8,2,64,768]{3,2,1,0:T(8,128)(2,1)S(1)} %all-to-all-done.4.terms), custom_call_target="tpu_custom_call" | custom-call | tf_op jit(solution)/shard_map/pallas_call | solution.py:249
  147.1 4.0 %convolution_convert_fusion = bf16[224,1024]{1,0:T(8,128)(2,1)S(1)} fusion(bf16[1024,2048]{1,0:T(8,128)(2,1)} %all-gather.2.cloned.1.call-done, bf16[3,448,2048]{2,1,0:T(8,128)(2,1)} %copy-done), kind=kOutput, calls=%fused_computation.5 | convolution fusion | flops 939753472 | bytes 5570560 | tf_op jit(solution)/shard_map/dot_general | solution.py:231
  151.2 1.0 collective-permute-start.16
  152.2 3.8 %convolution_convert_fusion.3 = bf16[224,1024]{1,0:T(8,128)(2,1)S(1)} fusion(bf16[1024,2048]{1,0:T(8,128)(2,1)} %all-gather.2.cloned.1.call-done, bf16[3,448,2048]{2,1,0:T(8,128)(2,1)S(1)} %copy-done.1), kind=kOutput, calls=%fused_computation.8 | convolution fusion | flops 939753472 | bytes 5570560 | tf_op jit(solution)/shard_map/dot_general | solution.py:231
  155.9 0.4 collective-permute-start.12
  156.4 1.4 convolution_convert_fusion.2
  157.8 0.1 collective-permute-start.14
  157.9 1.4 convolution_convert_fusion.1
  159.3 2.7 %collective-permute-start.15 = (bf16[224,1024]{1,0:T(8,128)(2,1)S(1)}, bf16[224,1024]{1,0:T(8,128)(2,1)S(1)}, u32[]{:S(2)}, u32[]{:S(2)}) collective-permute-start(bf16[224,1024]{1,0:T(8,128)(2,1)S(1)} %convolution_convert_fusion.1), channel_id=1, source_target_pairs={{0,3},{1,0},{2,1},{3,2},{4,7},{5,4},{6,5},{7,6},{8,11},{9,8},{10,9... | collective-permute-start | bytes 1376264 | tf_op jit(solution)/shard_map/ppermute | solution.py:156
  162.0 0.7 collective-permute-done.16
  162.8 1.4 fusion.1
  164.2 2.2 %collective-permute-start.17 = (bf16[224,1024]{1,0:T(8,128)(2,1)S(1)}, bf16[224,1024]{1,0:T(8,128)(2,1)S(1)}, u32[]{:S(2)}, u32[]{:S(2)}) collective-permute-start(bf16[224,1024]{1,0:T(8,128)(2,1)S(1)} %fusion.1), channel_id=1, source_target_pairs={{0,3},{1,0},{2,1},{3,2},{4,7},{5,4},{6,5},{7,6},{8,11},{9,8},{10,9... | collective-permute-start | bytes 1376264 | tf_op jit(solution)/shard_map/ppermute | solution.py:156
  166.4 2.2 %collective-permute-done.12 = bf16[224,1024]{1,0:T(8,128)(2,1)S(1)} collective-permute-done((bf16[224,1024]{1,0:T(8,128)(2,1)S(1)}, bf16[224,1024]{1,0:T(8,128)(2,1)S(1)}, u32[]{:S(2)}, u32[]{:S(2)}) %collective-permute-start.12) | collective-permute-done | bytes 458784 | tf_op jit(solution)/shard_map/ppermute | solution.py:156
  168.6 1.4 fusion
  170.1 0.3 collective-permute-start.13
  170.4 2.1 %convolution_add_fusion.base = f32[448,1024]{1,0:T(8,128)S(1)} fusion(f32[448,1024]{1,0:T(8,128)S(1)} %copy-done.11, bf16[448,2048]{1,0:T(8,128)(2,1)S(1)} %copy-done.12, bf16[1024,2048]{1,0:T(8,128)(2,1)S(1)} %copy-done.14), kind=kOutput, calls=%fused_computation | convolution fusion | flops 1879506944 | bytes 9699328 | tf_op jit(solution)/shard_map/dot_general | solution.py:231
  172.5 6.0 %collective-permute-done.14.up_soon = bf16[224,1024]{1,0:T(8,128)(2,1)S(1)} collective-permute-done((bf16[224,1024]{1,0:T(8,128)(2,1)S(1)}, bf16[224,1024]{1,0:T(8,128)(2,1)S(1)}, u32[]{:S(2)}, u32[]{:S(2)}) %collective-permute-start.14) | collective-permute-done | bytes 458784 | tf_op jit(solution)/shard_map/ppermute | solution.py:156
  178.5 4.0 %collective-permute-done.17.down_late = bf16[224,1024]{1,0:T(8,128)(2,1)S(1)} collective-permute-done((bf16[224,1024]{1,0:T(8,128)(2,1)S(1)}, bf16[224,1024]{1,0:T(8,128)(2,1)S(1)}, u32[]{:S(2)}, u32[]{:S(2)}) %collective-permute-start.17) | collective-permute-done | bytes 458784 | tf_op jit(solution)/shard_map/ppermute | solution.py:156
  182.4 5.9 %collective-permute-done.13.up_late = bf16[224,1024]{1,0:T(8,128)(2,1)S(1)} collective-permute-done((bf16[224,1024]{1,0:T(8,128)(2,1)S(1)}, bf16[224,1024]{1,0:T(8,128)(2,1)S(1)}, u32[]{:S(2)}, u32[]{:S(2)}) %collective-permute-start.13) | collective-permute-done | bytes 458784 | tf_op jit(solution)/shard_map/ppermute | solution.py:156
  188.3 1.2 shard_map.99
  (36 shorter events, 0.1 us)
Async XLA Ops:
  7.2 45.4 %copy-start.2 = (bf16[1024,256]{1,0:T(8,128)(2,1)S(1)}, bf16[1024,256]{1,0:T(8,128)(2,1)}, u32[]{:S(2)}) copy-start(bf16[1024,256]{1,0:T(8,128)(2,1)} %tokens.3) | copy-start | bytes 1572868
  7.2 45.4 %copy-start.7 = (s32[1,8]{1,0:T(1,128)S(1)}, s32[1,8]{1,0:T(1,128)}, u32[]{:S(2)}) copy-start(s32[1,8]{1,0:T(1,128)} %used.3) | copy-start | bytes 100
  7.2 45.4 %copy-start.3 = (bf16[1024,448]{0,1:T(8,128)(2,1)S(1)}, bf16[1024,448]{0,1:T(8,128)(2,1)}, u32[]{:S(2)}) copy-start(bf16[1024,448]{0,1:T(8,128)(2,1)} %param.8) | copy-start | bytes 2752516
  7.2 45.4 %copy-start.9 = (s32[1,8]{1,0:T(1,128)S(1)}, s32[1,8]{1,0:T(1,128)}, u32[]{:S(2)}) copy-start(s32[1,8]{1,0:T(1,128)} %order.3) | copy-start | bytes 100
  7.2 139.9 %all-gather.2.cloned.1.call-start = ((), (), s32[]{:S(2)}) async-start(), calls=%async_computation.5 | async-start | bytes 4718592 | tf_op jit(solution)/shard_map/all_gather | solution.py:175
  9.5 18.5 %collective-permute-start = (bf16[448,256]{1,0:T(8,128)(2,1)S(1)}, bf16[448,256]{1,0:T(8,128)(2,1)S(1)}, u32[]{:S(2)}, u32[]{:S(2)}) collective-permute-start(bf16[448,256]{1,0:T(8,128)(2,1)S(1)} %get-tuple-element.25), channel_id=1, source_target_pairs={{0,3},{1,0},{2,1},{3,2},{4,7},{5,4},{6,5},{7,6},{8,11},{9,8},{10,9... | collective-permute-start | bytes 688136 | tf_op jit(solution)/shard_map/ppermute | solution.py:156
  13.1 14.9 %collective-permute-start.1 = (bf16[448,256]{1,0:T(8,128)(2,1)S(1)}, bf16[448,256]{1,0:T(8,128)(2,1)S(1)}, u32[]{:S(2)}, u32[]{:S(2)}) collective-permute-start(bf16[448,256]{1,0:T(8,128)(2,1)S(1)} %get-tuple-element.24), channel_id=1, source_target_pairs={{0,2},{1,3},{2,0},{3,1},{4,6},{5,7},{6,4},{7,5},{8,10},{9,11},{10,... | collective-permute-start | bytes 688136 | tf_op jit(solution)/shard_map/ppermute | solution.py:156
  13.5 15.2 %collective-permute-start.2 = (bf16[448,256]{1,0:T(8,128)(2,1)S(1)}, bf16[448,256]{1,0:T(8,128)(2,1)}, u32[]{:S(2)}, u32[]{:S(2)}) collective-permute-start(bf16[448,256]{1,0:T(8,128)(2,1)S(1)} %get-tuple-element.23), channel_id=1, source_target_pairs={{0,1},{1,2},{2,3},{3,0},{4,5},{5,6},{6,7},{7,4},{8,9},{9,10},{10,1... | collective-permute-start | bytes 688136 | tf_op jit(solution)/shard_map/ppermute | solution.py:156
  25.1 1.1 copy-start.5
  26.2 1.0 copy-start.6
  28.0 0.7 copy-start.13
  78.5 14.4 %all-to-all-start.3 = ((bf16[32,32,128]{2,1,0:T(8,128)(2,1)}), bf16[32,32,128]{2,1,0:T(8,128)(2,1)S(1)}, u32[]{:S(2)}, u32[]{:S(2)}) async-start(bf16[32,32,128]{2,1,0:T(8,128)(2,1)} %broadcast_in_dim.16), calls=%async_computation.3 | async-start | bytes 524288 | tf_op jit(solution)/shard_map/all_to_all | solution.py:224
  86.4 17.7 %collective-permute-start.3 = (bf16[1344,256]{1,0:T(8,128)(2,1)}, bf16[1344,256]{1,0:T(8,128)(2,1)}, u32[]{:S(2)}, u32[]{:S(2)}) collective-permute-start(bf16[1344,256]{1,0:T(8,128)(2,1)} %constant_dynamic-update-slice_fusion.refs_0_), channel_id=1, source_target_pairs={{0,64},{64,128},{128,192},{192,0},{1,65},{65,129},{129,193},{193,1... | collective-permute-start | bytes 2064392 | tf_op jit(solution)/shard_map/ppermute | solution.py:156
  87.0 19.7 %collective-permute-start.4 = (bf16[1344,256]{1,0:T(8,128)(2,1)}, bf16[1344,256]{1,0:T(8,128)(2,1)}, u32[]{:S(2)}, u32[]{:S(2)}) collective-permute-start(bf16[1344,256]{1,0:T(8,128)(2,1)} %constant_dynamic-update-slice_fusion.refs_0_), channel_id=1, source_target_pairs={{0,192},{64,0},{128,64},{192,128},{1,193},{65,1},{129,65},{193,129... | collective-permute-start | bytes 2064392 | tf_op jit(solution)/shard_map/ppermute | solution.py:156
  94.2 1.1 copy-start.4
  95.4 1.2 copy-start.10
  96.6 48.3 %all-to-all-start.4 = ((bf16[8,2,64,768]{3,2,1,0:T(8,128)(2,1)}), bf16[8,2,64,768]{3,2,1,0:T(8,128)(2,1)S(1)}, u32[]{:S(2)}, u32[]{:S(2)}) async-start(bf16[8,2,64,768]{3,2,1,0:T(8,128)(2,1)} %bitcast.52), calls=%async_computation.4 | async-start | bytes 3145728 | tf_op jit(solution)/shard_map/all_to_all | solution.py:248
  103.9 35.7 %collective-permute-start.7 = (bf16[1344,256]{1,0:T(8,128)(2,1)}, bf16[1344,256]{1,0:T(8,128)(2,1)S(1)}, u32[]{:S(2)}, u32[]{:S(2)}) collective-permute-start(bf16[1344,256]{1,0:T(8,128)(2,1)} %constant_dynamic-update-slice_fusion.refs_0_), channel_id=1, source_target_pairs={{0,32},{32,0},{1,33},{33,1},{2,34},{34,2},{3,35},{35,3},{4,36},{36... | collective-permute-start | bytes 2064392 | tf_op jit(solution)/shard_map/ppermute | solution.py:156
  105.1 26.8 %collective-permute-start.5 = (bf16[672,256]{1,0:T(8,128)(2,1)S(1)}, bf16[672,256]{1,0:T(8,128)(2,1)S(1)}, u32[]{:S(2)}, u32[]{:S(2)}) collective-permute-start(bf16[672,256]{1,0:T(8,128)(2,1)S(1)} %slice.65), channel_id=1, source_target_pairs={{0,64},{64,128},{128,192},{192,0},{1,65},{65,129},{129,193},{193,1... | collective-permute-start | bytes 1032200 | tf_op jit(solution)/shard_map/ppermute | solution.py:156
  107.8 24.9 %collective-permute-start.6 = (bf16[672,256]{1,0:T(8,128)(2,1)S(1)}, bf16[672,256]{1,0:T(8,128)(2,1)}, u32[]{:S(2)}, u32[]{:S(2)}) collective-permute-start(bf16[672,256]{1,0:T(8,128)(2,1)S(1)} %slice.66), channel_id=1, source_target_pairs={{0,192},{64,0},{128,64},{192,128},{1,193},{65,1},{129,65},{193,129... | collective-permute-start | bytes 1032200 | tf_op jit(solution)/shard_map/ppermute | solution.py:156
  109.1 30.5 %collective-permute-start.8 = (bf16[1344,256]{1,0:T(8,128)(2,1)}, bf16[1344,256]{1,0:T(8,128)(2,1)S(1)}, u32[]{:S(2)}, u32[]{:S(2)}) collective-permute-start(bf16[1344,256]{1,0:T(8,128)(2,1)} %collective-permute-done.3.refs_1_), channel_id=1, source_target_pairs={{0,32},{32,0},{1,33},{33,1},{2,34},{34,2},{3,35},{35,3},{4,36},{36... | collective-permute-start | bytes 2064392 | tf_op jit(solution)/shard_map/ppermute | solution.py:156
  111.2 28.4 %collective-permute-start.9 = (bf16[1344,256]{1,0:T(8,128)(2,1)}, bf16[1344,256]{1,0:T(8,128)(2,1)}, u32[]{:S(2)}, u32[]{:S(2)}) collective-permute-start(bf16[1344,256]{1,0:T(8,128)(2,1)} %collective-permute-done.4.refs_2_), channel_id=1, source_target_pairs={{0,32},{32,0},{1,33},{33,1},{2,34},{34,2},{3,35},{35,3},{4,36},{36... | collective-permute-start | bytes 2064392 | tf_op jit(solution)/shard_map/ppermute | solution.py:156
  131.9 7.7 %collective-permute-start.10 = (bf16[672,256]{1,0:T(8,128)(2,1)S(1)}, bf16[672,256]{1,0:T(8,128)(2,1)}, u32[]{:S(2)}, u32[]{:S(2)}) collective-permute-start(bf16[672,256]{1,0:T(8,128)(2,1)S(1)} %collective-permute-done.5.refs_3_), channel_id=1, source_target_pairs={{0,32},{32,0},{1,33},{33,1},{2,34},{34,2},{3,35},{35,3},{4,36},{36... | collective-permute-start | bytes 1032200 | tf_op jit(solution)/shard_map/ppermute | solution.py:156
  132.6 7.0 %collective-permute-start.11 = (bf16[672,256]{1,0:T(8,128)(2,1)}, bf16[672,256]{1,0:T(8,128)(2,1)}, u32[]{:S(2)}, u32[]{:S(2)}) collective-permute-start(bf16[672,256]{1,0:T(8,128)(2,1)} %collective-permute-done.6.refs_4_), channel_id=1, source_target_pairs={{0,32},{32,0},{1,33},{33,1},{2,34},{34,2},{3,35},{35,3},{4,36},{36... | collective-permute-start | bytes 1032200 | tf_op jit(solution)/shard_map/ppermute | solution.py:156
  133.2 6.4 %copy-start.8 = (s32[4]{0:T(128)S(1)}, s32[4]{0:T(128)}, u32[]{:S(2)}) copy-start(s32[4]{0:T(128)} %pad_add_fusion.meta) | copy-start | bytes 52
  142.5 2.4 %copy-start = (bf16[3,448,2048]{2,1,0:T(8,128)(2,1)}, bf16[3,448,2048]{2,1,0:T(8,128)(2,1)S(1)}, u32[]{:S(2)}) copy-start(bf16[3,448,2048]{2,1,0:T(8,128)(2,1)S(1)} %shard_map.98) | copy-start | bytes 16515076
  147.1 5.1 %copy-start.1 = (bf16[3,448,2048]{2,1,0:T(8,128)(2,1)S(1)}, bf16[3,448,2048]{2,1,0:T(8,128)(2,1)}, u32[]{:S(2)}) copy-start(bf16[3,448,2048]{2,1,0:T(8,128)(2,1)} %copy-done) | copy-start | bytes 16515076
  151.1 5.2 %copy-start.14 = (bf16[1024,2048]{1,0:T(8,128)(2,1)S(1)}, bf16[1024,2048]{1,0:T(8,128)(2,1)}, u32[]{:S(2)}) copy-start(bf16[1024,2048]{1,0:T(8,128)(2,1)} %all-gather.2.cloned.1.call-done) | copy-start | bytes 12582916
  151.2 11.6 %collective-permute-start.16 = (bf16[224,1024]{1,0:T(8,128)(2,1)S(1)}, bf16[224,1024]{1,0:T(8,128)(2,1)S(1)}, u32[]{:S(2)}, u32[]{:S(2)}) collective-permute-start(bf16[224,1024]{1,0:T(8,128)(2,1)S(1)} %convolution_convert_fusion), channel_id=1, source_target_pairs={{0,3},{1,0},{2,1},{3,2},{4,7},{5,4},{6,5},{7,6},{8,11},{9,8},{10,9... | collective-permute-start | bytes 1376264 | tf_op jit(solution)/shard_map/ppermute | solution.py:156
  155.9 12.7 %collective-permute-start.12 = (bf16[224,1024]{1,0:T(8,128)(2,1)S(1)}, bf16[224,1024]{1,0:T(8,128)(2,1)S(1)}, u32[]{:S(2)}, u32[]{:S(2)}) collective-permute-start(bf16[224,1024]{1,0:T(8,128)(2,1)S(1)} %convolution_convert_fusion.3), channel_id=1, source_target_pairs={{0,1},{1,2},{2,3},{3,0},{4,5},{5,6},{6,7},{7,4},{8,9},{9,10},{10,1... | collective-permute-start | bytes 1376264 | tf_op jit(solution)/shard_map/ppermute | solution.py:156
  157.8 20.7 %collective-permute-start.14 = (bf16[224,1024]{1,0:T(8,128)(2,1)S(1)}, bf16[224,1024]{1,0:T(8,128)(2,1)S(1)}, u32[]{:S(2)}, u32[]{:S(2)}) collective-permute-start(bf16[224,1024]{1,0:T(8,128)(2,1)S(1)} %convolution_convert_fusion.2), channel_id=1, source_target_pairs={{0,1},{1,2},{2,3},{3,0},{4,5},{5,6},{6,7},{7,4},{8,9},{9,10},{10,1... | collective-permute-start | bytes 1376264 | tf_op jit(solution)/shard_map/ppermute | solution.py:156
  159.3 19.1 %collective-permute-start.15 = (bf16[224,1024]{1,0:T(8,128)(2,1)S(1)}, bf16[224,1024]{1,0:T(8,128)(2,1)S(1)}, u32[]{:S(2)}, u32[]{:S(2)}) collective-permute-start(bf16[224,1024]{1,0:T(8,128)(2,1)S(1)} %convolution_convert_fusion.1), channel_id=1, source_target_pairs={{0,3},{1,0},{2,1},{3,2},{4,7},{5,4},{6,5},{7,6},{8,11},{9,8},{10,9... | collective-permute-start | bytes 1376264 | tf_op jit(solution)/shard_map/ppermute | solution.py:156
  164.2 6.2 %copy-start.11 = (f32[448,1024]{1,0:T(8,128)S(1)}, f32[448,1024]{1,0:T(8,128)}, u32[]{:S(2)}) copy-start(f32[448,1024]{1,0:T(8,128)} %copy-done.10) | copy-start | bytes 5505028
  164.2 6.2 %copy-start.12 = (bf16[448,2048]{1,0:T(8,128)(2,1)S(1)}, bf16[448,2048]{1,0:T(8,128)(2,1)}, u32[]{:S(2)}) copy-start(bf16[448,2048]{1,0:T(8,128)(2,1)} %shard_map.96) | copy-start | bytes 5505028
  164.2 18.2 %collective-permute-start.17 = (bf16[224,1024]{1,0:T(8,128)(2,1)S(1)}, bf16[224,1024]{1,0:T(8,128)(2,1)S(1)}, u32[]{:S(2)}, u32[]{:S(2)}) collective-permute-start(bf16[224,1024]{1,0:T(8,128)(2,1)S(1)} %fusion.1), channel_id=1, source_target_pairs={{0,3},{1,0},{2,1},{3,2},{4,7},{5,4},{6,5},{7,6},{8,11},{9,8},{10,9... | collective-permute-start | bytes 1376264 | tf_op jit(solution)/shard_map/ppermute | solution.py:156
  170.1 18.2 %collective-permute-start.13 = (bf16[224,1024]{1,0:T(8,128)(2,1)S(1)}, bf16[224,1024]{1,0:T(8,128)(2,1)S(1)}, u32[]{:S(2)}, u32[]{:S(2)}) collective-permute-start(bf16[224,1024]{1,0:T(8,128)(2,1)S(1)} %fusion), channel_id=1, source_target_pairs={{0,1},{1,2},{2,3},{3,0},{4,5},{5,6},{6,7},{7,4},{8,9},{9,10},{10,1... | collective-permute-start | bytes 1376264 | tf_op jit(solution)/shard_map/ppermute | solution.py:156
Sparse Core Ops, SparseCore 0:
  9.8 70.1 all-gather.1

commit v5 on v4

--- a/solution.py
+++ b/solution.py
@@ -108,22 +108,21 @@
 
 
 def place_kernel(meta, *refs):
-    out = refs[-1]
-    count, units, _ = out.shape
-    width = refs[0].shape[1]
-    half = refs[3].shape[0]
-    x, core = meta[0], meta[1]
-    for other in range(2):
-        own, left, right, far_left, far_right = refs[5 * other:5 * other + 5]
-        for sources, step in (((own,), 0), ((left,), 3), ((right,), 1), ((far_left, far_right), 2)):
-            block = 2 * lax.rem(x + step, jnp.int32(4)) + (1 - core if other else core)
-            spot = pl.ds(pl.multiple_of(block * width, width), width)
-            for r in range(count):
-                for start in range(0, units, units // 2):
-                    at = r * units + start
-                    source = sources[at // half] if len(sources) == 2 else sources[0]
-                    low = at % half if len(sources) == 2 else at
-                    out[r, start:start + units // 2, spot] = source[low:low + units // 2, :]
+    got, swapped, out = refs[:3], refs[3:6], refs[6]
+    span = got[0].shape[1]
+    core = meta[1]
+    for r in range(3):
+        out[r, :, pl.ds(pl.multiple_of(core * span, span), span)] = got[r][...]
+        out[r, :, pl.ds(pl.multiple_of((1 - core) * span, span), span)] = swapped[r][...]
+
+
+def fetch_kernel(meta, *refs):
+    for source, out in zip(refs[:3], refs[3:]):
+        out[...] = source[...]
+
+
+def join_blocks_kernel(source, out):
+    out[...] = source[0]
 
 
 def copy_kernel(meta, source, out):
@@ -172,15 +171,27 @@
     meta = jnp.stack([x, core, z, y]).astype(jnp.int32)
     me_arr = me.reshape(1).astype(jnp.int32)
 
-    wide_tokens = lax.all_gather(tokens, "z", axis=1, tiled=True)
+    gathered = lax.all_gather(tokens, "z")
 
     weight_t = weight.T
-    piece = n_y * width
-    mine = lax.dynamic_slice(weight_t, (0, me * piece), (units, piece))
-    pieces = tuple(
-        hop(lax.dynamic_slice(mine, (0, lax.rem(y + n_y - r, n_y) * width), (units, width)), "y", -r)
-        for r in range(1, n_y)
-    )
+    span = n_z // 2
+
+    def block_for(r):
+        return lambda i, meta: (
+            0, (span * meta[1] + i) * n_y + lax.rem(meta[3] + n_y - r, jnp.int32(n_y))
+        )
+
+    fetched = pl.pallas_call(
+        fetch_kernel,
+        out_shape=[whole((units, span * width), BF)] * 3,
+        grid_spec=pltpu.PrefetchScalarGridSpec(
+            num_scalar_prefetch=1,
+            grid=(span,),
+            in_specs=[pl.BlockSpec((units, width), block_for(r)) for r in (1, 2, 3)],
+            out_specs=[pl.BlockSpec((units, width), lambda i, meta: (0, i))] * 3,
+        ),
+    )(meta, weight_t, weight_t, weight_t)
+    pieces = tuple(hop(item, "y", -r) for r, item in zip((1, 2, 3), fetched))
 
     down_t = jnp.transpose(down, (0, 2, 1))
     used_all = lax.all_to_all(
@@ -189,9 +200,6 @@
     picked = call(pick_kernel, whole((owners, 2, rank, packed), BF), [SMEM, SMEM, VMEM, VMEM])(
         me_arr, used_all, down_t, up
     )
-    picked, pieces = together((picked, pieces))
-    own = jnp.concatenate(pieces, axis=0)
-    from_left, from_right = hop(own, "x", 1), hop(own, "x", -1)
     factors = lax.all_to_all(picked, DP, 0, 0, tiled=True).reshape(owners * 2, rank, packed)
     cot_t = cotangent.T
     sizes = dict(rank=rank, width=width, units=units)
@@ -211,13 +219,10 @@
             out_specs=pl.BlockSpec((units, width), lambda i, meta: (0, i)),
         ),
     )(meta, weight_t)
-    middle = own.shape[0] // 2
-    far_left, far_right = hop(from_left[:middle], "x", 1), hop(from_right[middle:], "x", -1)
-    held = (own, from_left, from_right, far_left, far_right)
-    swapped = tuple(hop(item, "core", 1) for item in held)
+    swapped = tuple(hop(item, "core", 1) for item in pieces)
     wide_weight = call(
-        place_kernel, whole((n_y - 1, units, n_z * width), BF), [SMEM] + [VMEM] * 10, limit=24
-    )(meta, *held, *swapped)
+        place_kernel, whole((n_y - 1, units, n_z * width), BF), [SMEM] + [VMEM] * 6, limit=24
+    )(meta, *pieces, *swapped)
     share = rows // members
     parts = lax.all_to_all(part.reshape(members, share, 2 * rank), MP, 0, 0, tiled=True)
     summed = jnp.sum(parts.astype(F32), axis=0).astype(BF)
@@ -225,6 +230,13 @@
         jnp.broadcast_to(summed[None], (members,) + summed.shape), MP, 0, 0, tiled=True
     ).reshape(rows, 2 * rank)
 
+    wide_tokens = pl.pallas_call(
+        join_blocks_kernel,
+        out_shape=whole((rows, n_z * width), BF),
+        grid=(n_z,),
+        in_specs=[pl.BlockSpec((1, rows, width), lambda i: (i, 0, 0))],
+        out_specs=pl.BlockSpec((rows, width), lambda i: (0, i)),
+    )(gathered)
     half = units // 2
 
     def product(weights):

time: 197 us -> 205 us (1.041)
  blocking collectives: 58.1 us -> 23.9 us
  starting transfers between devices: 31.5 us -> 59.9 us
  Pallas kernels: 16 us -> 28 us
  waiting for transfers between devices: 43.9 us -> 51.1 us
  local copies, waits for them, and re-layouts: 16.4 us -> 10.9 us
    all_to_all x2 -> x0, blocking collectives: 34.3 us -> none  [the longest x1 24 us: on_device(): lax.all_to_all(part.reshape(members, share, 2 * rank), MP, 0, 0, tiled=True)]
    all_to_all x0 -> x2, waiting for transfers between devices: none -> 19 us  [the longest x1 14.5 us: on_device(): lax.all_to_all(part.reshape(members, share, 2 * rank), MP, 0, 0, tiled=True)]
    all_to_all x0 -> x2, starting transfers between devices: none -> 17 us  [the longest x1 10.5 us: on_device(): lax.all_to_all(part.reshape(members, share, 2 * rank), MP, 0, 0, tiled=True)]
    pallas_call x0 -> x2, Pallas kernels: none -> 11.5 us  [the longest x1 6.65 us: on_device(): pl.pallas_call(join_blocks_kernel, out_shape=whole((rows, n_z * width), B...]
    ppermute x18 -> x12, starting transfers between devices: 20.2 us -> 31.3 us  [hop(): return lax.ppermute(value, axis, [(i, (i + step) % n) for i in range(n)])]
    ppermute x18 -> x12, waiting for transfers between devices: 39.5 us -> 30.1 us  [hop(): return lax.ppermute(value, axis, [(i, (i + step) % n) for i in range(n)])]
    all_to_all x1, waiting for transfers between devices: 3.74 us -> 1.4 us  [on_device(): lax.all_to_all(jnp.broadcast_to(summed[None], (members,) + summed.shape),...]
  transfers between devices with their start and end apart: 21 -> 17, of which waited for: 7 -> 10; matrix products, arithmetic and copies ran while one was open for 11% -> 5% of each run, Pallas kernels for 8% -> 10%
where the time goes in v5:
time: 205 us; the launch traced here: 204 us
  starting transfers between devices  59.9 us (29%)
  waiting for transfers between devices  51.1 us (25%)
  Pallas kernels  28 us (14%)
  blocking collectives  23.9 us (12%)
  matrix products  15.5 us (8%)
  between operations  14.2 us (7%)
  local copies, waits for them, and re-layouts  10.9 us (5%)
    ppermute x12, starting transfers between devices, hop(): return lax.ppermute(value, axis, [(i, (i + step) % n) for i in range(n)])  31.3 us
    ppermute x12, waiting for transfers between devices, hop(): return lax.ppermute(value, axis, [(i, (i + step) % n) for i in range(n)])  30.1 us
    all_to_all x1, blocking collectives, on_device(): lax.all_to_all(picked, DP, 0, 0, tiled=True)  23.9 us
    dot_general x7, matrix products, product(): lax.dot_general(weights, wide_tokens, (((1,), (1,)), ((), ())), preferred...  15.5 us
    all_to_all x1, waiting for transfers between devices, on_device(): lax.all_to_all(part.reshape(members, share, 2 * rank), MP, 0, 0, tiled=True)  14.5 us
    all_to_all x1, starting transfers between devices, on_device(): lax.all_to_all(part.reshape(members, share, 2 * rank), MP, 0, 0, tiled=True)  10.5 us
    unnamed x32, local copies, waits for them, and re-layouts  8.95 us
    all_to_all x1, starting transfers between devices, on_device(): lax.all_to_all(send.reshape(owners, 2, rank, packed), DP, 0, 0, tiled=True)  7.3 us
  transfers between devices with their start and end apart: 17, of which 10 were waited for; matrix products, arithmetic and copies ran while one was open for 5% of the time, Pallas kernels for 10%

profile of v5, /device:TPU:1, one launch (start us, length us, event | category | flops | bytes accessed | tf_op | source)
XLA Modules:
  0.0 204.3 jit_solution(2450034358422609545)
XLA Ops:
  7.2 0.0 all-gather.3.cloned.1.call-start
  7.2 0.7 all-gather.3.cloned.1.call-update
  7.9 1.3 broadcast_in_dim.7
  9.2 6.5 %all-to-all-start = ((s32[8,1,8]{2,1,0:T(1,128)}), s32[8,1,8]{2,1,0:T(1,128)S(1)}, u32[]{:S(2)}, u32[]{:S(2)}) async-start(s32[8,1,8]{2,1,0:T(1,128)} %broadcast_in_dim.7), calls=%async_computation | async-start | bytes 8192 | tf_op jit(solution)/shard_map/all_to_all | solution.py:197
  15.6 4.5 %all-to-all-done = s32[8,1,8]{2,1,0:T(1,128)S(1)} async-done(((s32[8,1,8]{2,1,0:T(1,128)}), s32[8,1,8]{2,1,0:T(1,128)S(1)}, u32[]{:S(2)}, u32[]{:S(2)}) %all-to-all-start) | async-done | bytes 288 | tf_op jit(solution)/shard_map/all_to_all | solution.py:197
  20.1 1.0 copy-done.7
  21.2 0.9 copy-done.8
  22.1 0.9 shard_map.94
  23.0 23.9 %all_to_all.25 = bf16[8,2,64,768]{3,2,1,0:T(8,128)(2,1)S(1)} all-to-all(bf16[8,2,64,768]{3,2,1,0:T(8,128)(2,1)S(1)} %shard_map.94), channel_id=1, replica_groups=mesh['x'=4,'core'=2,'z'=8,'y'=4] {'x','core'}, dimensions={0} | all-to-all | bytes 3145728 | tf_op jit(solution)/shard_map/all_to_all | solution.py:203
  47.0 0.0 copy-done.10
  47.0 1.8 shard_map.95
  48.8 10.5 %all-to-all-start.2 = ((bf16[32,32,128]{2,1,0:T(8,128)(2,1)}), bf16[32,32,128]{2,1,0:T(8,128)(2,1)S(1)}, u32[]{:S(2)}, u32[]{:S(2)}) async-start(bf16[32,32,128]{2,1,0:T(8,128)(2,1)} %bitcast.12), calls=%async_computation.2 | async-start | bytes 524288 | tf_op jit(solution)/shard_map/all_to_all | solution.py:227
  59.4 14.5 %all-to-all-done.2 = bf16[32,32,128]{2,1,0:T(8,128)(2,1)S(1)} async-done(((bf16[32,32,128]{2,1,0:T(8,128)(2,1)}), bf16[32,32,128]{2,1,0:T(8,128)(2,1)S(1)}, u32[]{:S(2)}, u32[]{:S(2)}) %all-to-all-start.2) | async-done | bytes 262176 | tf_op jit(solution)/shard_map/all_to_all | solution.py:227
  73.9 0.1 reduce_sum.12
  73.9 0.7 broadcast_in_dim.16
  74.7 4.3 %all-to-all-start.3 = ((bf16[32,32,128]{2,1,0:T(8,128)(2,1)}), bf16[32,32,128]{2,1,0:T(8,128)(2,1)S(1)}, u32[]{:S(2)}, u32[]{:S(2)}) async-start(bf16[32,32,128]{2,1,0:T(8,128)(2,1)} %broadcast_in_dim.16), calls=%async_computation.3 | async-start | bytes 524288 | tf_op jit(solution)/shard_map/all_to_all | solution.py:229
  79.0 0.6 pad_add_fusion.meta
  79.6 4.8 %shard_map.99 = (bf16[448,1024]{1,0:T(8,128)(2,1)}, bf16[448,1024]{1,0:T(8,128)(2,1)}, bf16[448,1024]{1,0:T(8,128)(2,1)}) custom-call(s32[4]{0:T(128)} %pad_add_fusion.meta, bf16[448,8192]{1,0:T(8,128)(2,1)} %bitcast.53, bf16[448,8192]{1,0:T(8,128)(2,1)} %bitcast.54, bf16[448,8192]{1,0:T(8,128)(2,1)} %bitcast.55), custom_call_target="tpu_custom_call" | custom-call | tf_op jit(solution)/shard_map/pallas_call | solution.py:184
  84.4 2.4 %collective-permute-start = (bf16[448,1024]{1,0:T(8,128)(2,1)}, bf16[448,1024]{1,0:T(8,128)(2,1)}, u32[]{:S(2)}, u32[]{:S(2)}) collective-permute-start(bf16[448,1024]{1,0:T(8,128)(2,1)} %get-tuple-element.15), channel_id=1, source_target_pairs={{0,3},{1,0},{2,1},{3,2},{4,7},{5,4},{6,5},{7,6},{8,11},{9,8},{10,9... | collective-permute-start | bytes 2752520 | tf_op jit(solution)/shard_map/ppermute | solution.py:155
  86.8 0.6 collective-permute-start.1
  87.4 0.6 collective-permute-start.2
  88.0 1.4 all-to-all-done.3
  89.4 1.4 shard_map.98
  90.8 1.1 copy-done.4
  91.9 1.2 copy-done.12
  93.2 7.3 %all-to-all-start.4 = ((bf16[8,2,64,768]{3,2,1,0:T(8,128)(2,1)}), bf16[8,2,64,768]{3,2,1,0:T(8,128)(2,1)S(1)}, u32[]{:S(2)}, u32[]{:S(2)}) async-start(bf16[8,2,64,768]{3,2,1,0:T(8,128)(2,1)} %bitcast.47), calls=%async_computation.4 | async-start | bytes 3145728 | tf_op jit(solution)/shard_map/all_to_all | solution.py:260
  100.5 5.6 %collective-permute-done.refs_0_ = bf16[448,1024]{1,0:T(8,128)(2,1)} collective-permute-done((bf16[448,1024]{1,0:T(8,128)(2,1)}, bf16[448,1024]{1,0:T(8,128)(2,1)}, u32[]{:S(2)}, u32[]{:S(2)}) %collective-permute-start) | collective-permute-done | bytes 917536 | tf_op jit(solution)/shard_map/ppermute | solution.py:155
  106.0 21.8 %collective-permute-start.3 = (bf16[448,1024]{1,0:T(8,128)(2,1)}, bf16[448,1024]{1,0:T(8,128)(2,1)S(1)}, u32[]{:S(2)}, u32[]{:S(2)}) collective-permute-start(bf16[448,1024]{1,0:T(8,128)(2,1)} %collective-permute-done.refs_0_), channel_id=1, source_target_pairs={{0,32},{32,0},{1,33},{33,1},{2,34},{34,2},{3,35},{35,3},{4,36},{36... | collective-permute-start | bytes 2752520 | tf_op jit(solution)/shard_map/ppermute | solution.py:155
  127.8 0.0 collective-permute-done.1.refs_1_
  127.8 0.0 collective-permute-start.4
  127.8 2.8 %collective-permute-done.2.refs_2_ = bf16[448,1024]{1,0:T(8,128)(2,1)} collective-permute-done((bf16[448,1024]{1,0:T(8,128)(2,1)}, bf16[448,1024]{1,0:T(8,128)(2,1)}, u32[]{:S(2)}, u32[]{:S(2)}) %collective-permute-start.2) | collective-permute-done | bytes 917536 | tf_op jit(solution)/shard_map/ppermute | solution.py:155
  130.7 0.6 collective-permute-start.5
  131.3 6.3 %shard_map.96 = bf16[448,2048]{1,0:T(8,128)(2,1)} custom-call(s32[4]{0:T(128)} %pad_add_fusion.meta, bf16[448,8192]{1,0:T(8,128)(2,1)} %bitcast.56), custom_call_target="tpu_custom_call" | custom-call | tf_op jit(solution)/shard_map/pallas_call | solution.py:212
  137.6 0.0 collective-permute-done.3.refs_3_
  137.6 0.9 copy-done.5
  138.6 0.0 collective-permute-done.4.refs_4_
  138.6 0.0 collective-permute-done.5.refs_5_
  138.6 1.2 copy-done.6
  139.8 2.7 %shard_map.100 = bf16[3,448,2048]{2,1,0:T(8,128)(2,1)S(1)} custom-call(s32[4]{0:T(128)S(1)} %copy-done.9, bf16[448,1024]{1,0:T(8,128)(2,1)} %collective-permute-done.refs_0_, bf16[448,1024]{1,0:T(8,128)(2,1)} %collective-permute-done.1.refs_1_, bf16[448,1024]{1,0:T(8,128)(2,1)} %collective-permute-done.2.refs_2_, bf16[448,1024]{1,0:T(8,128)(2,1)S(1)} %copy-done.6, ...), custom_call_target="tpu_custom_call" | custom-call | tf_op jit(solution)/shard_map/pallas_call | solution.py:223
  142.4 2.4 %copy-done = bf16[3,448,2048]{2,1,0:T(8,128)(2,1)} copy-done((bf16[3,448,2048]{2,1,0:T(8,128)(2,1)}, bf16[3,448,2048]{2,1,0:T(8,128)(2,1)S(1)}, u32[]{:S(2)}) %copy-start) | copy-done | bytes 5505048
  144.8 0.0 all-to-all-done.4.terms
  144.8 2.2 %shard_map.102 = (f32[8,64,256]{2,1,0:T(8,128)}, f32[8,64,448]{2,1,0:T(8,128)}) custom-call(s32[1]{0:T(128)} %bitcast.4.me, s32[8,8]{1,0:T(8,128)S(1)} %bitcast.51, bf16[8,2,64,768]{3,2,1,0:T(8,128)(2,1)S(1)} %all-to-all-done.4.terms), custom_call_target="tpu_custom_call" | custom-call | tf_op jit(solution)/shard_map/pallas_call | solution.py:261
  147.0 6.6 %shard_map.97 = bf16[1024,2048]{1,0:T(8,128)(2,1)} custom-call(bf16[8,1024,256]{2,1,0:T(8,128)(2,1)} %bitcast.57), custom_call_target="tpu_custom_call" | custom-call | tf_op jit(solution)/shard_map/pallas_call | solution.py:233
  153.7 4.0 %convolution_convert_fusion = bf16[224,1024]{1,0:T(8,128)(2,1)S(1)} fusion(bf16[1024,2048]{1,0:T(8,128)(2,1)} %shard_map.97, bf16[3,448,2048]{2,1,0:T(8,128)(2,1)} %copy-done), kind=kOutput, calls=%fused_computation.5 | convolution fusion | flops 939753472 | bytes 5570560 | tf_op jit(solution)/shard_map/dot_general | solution.py:243
  157.7 0.1 copy-done.1
  157.7 3.8 %convolution_convert_fusion.1 = bf16[224,1024]{1,0:T(8,128)(2,1)S(1)} fusion(bf16[1024,2048]{1,0:T(8,128)(2,1)} %shard_map.97, bf16[3,448,2048]{2,1,0:T(8,128)(2,1)S(1)} %copy-done.1), kind=kOutput, calls=%fused_computation.6 | convolution fusion | flops 939753472 | bytes 5570560 | tf_op jit(solution)/shard_map/dot_general | solution.py:243
  161.5 0.7 collective-permute-start.10
  162.2 1.4 convolution_convert_fusion.3
  163.6 1.1 collective-permute-start.6
  164.7 1.4 convolution_convert_fusion.2
  166.1 1.7 collective-permute-start.9
  167.9 0.0 collective-permute-start.8
  167.9 6.0 %collective-permute-done.10 = bf16[224,1024]{1,0:T(8,128)(2,1)S(1)} collective-permute-done((bf16[224,1024]{1,0:T(8,128)(2,1)S(1)}, bf16[224,1024]{1,0:T(8,128)(2,1)S(1)}, u32[]{:S(2)}, u32[]{:S(2)}) %collective-permute-start.10) | collective-permute-done | bytes 458784 | tf_op jit(solution)/shard_map/ppermute | solution.py:155
  173.9 1.4 fusion.1
  175.3 1.6 collective-permute-start.11
  176.9 0.0 collective-permute-done.6
  176.9 1.4 fusion
  178.4 0.1 collective-permute-start.7
  178.5 2.1 %convolution_add_fusion.base = f32[448,1024]{1,0:T(8,128)S(1)} fusion(f32[448,1024]{1,0:T(8,128)S(1)} %copy-done.13, bf16[448,2048]{1,0:T(8,128)(2,1)S(1)} %copy-done.15, bf16[1024,2048]{1,0:T(8,128)(2,1)S(1)} %copy-done.14), kind=kOutput, calls=%fused_computation | convolution fusion | flops 1879506944 | bytes 9699328 | tf_op jit(solution)/shard_map/dot_general | solution.py:243
  180.6 3.1 %collective-permute-done.9.down_soon = bf16[224,1024]{1,0:T(8,128)(2,1)S(1)} collective-permute-done((bf16[224,1024]{1,0:T(8,128)(2,1)S(1)}, bf16[224,1024]{1,0:T(8,128)(2,1)S(1)}, u32[]{:S(2)}, u32[]{:S(2)}) %collective-permute-start.9) | collective-permute-done | bytes 458784 | tf_op jit(solution)/shard_map/ppermute | solution.py:155
  183.7 2.7 %collective-permute-done.8.up_soon = bf16[224,1024]{1,0:T(8,128)(2,1)S(1)} collective-permute-done((bf16[224,1024]{1,0:T(8,128)(2,1)S(1)}, bf16[224,1024]{1,0:T(8,128)(2,1)S(1)}, u32[]{:S(2)}, u32[]{:S(2)}) %collective-permute-start.8) | collective-permute-done | bytes 458784 | tf_op jit(solution)/shard_map/ppermute | solution.py:155
  186.4 7.1 %collective-permute-done.11.down_late = bf16[224,1024]{1,0:T(8,128)(2,1)S(1)} collective-permute-done((bf16[224,1024]{1,0:T(8,128)(2,1)S(1)}, bf16[224,1024]{1,0:T(8,128)(2,1)S(1)}, u32[]{:S(2)}, u32[]{:S(2)}) %collective-permute-start.11) | collective-permute-done | bytes 458784 | tf_op jit(solution)/shard_map/ppermute | solution.py:155
  193.5 2.7 %collective-permute-done.7.up_late = bf16[224,1024]{1,0:T(8,128)(2,1)S(1)} collective-permute-done((bf16[224,1024]{1,0:T(8,128)(2,1)S(1)}, bf16[224,1024]{1,0:T(8,128)(2,1)S(1)}, u32[]{:S(2)}, u32[]{:S(2)}) %collective-permute-start.7) | collective-permute-done | bytes 458784 | tf_op jit(solution)/shard_map/ppermute | solution.py:155
  196.3 1.2 shard_map.101
  (24 shorter events, 0.0 us)
Async XLA Ops:
  7.2 39.8 %copy-start.2 = (bf16[1024,256]{1,0:T(8,128)(2,1)S(1)}, bf16[1024,256]{1,0:T(8,128)(2,1)}, u32[]{:S(2)}) copy-start(bf16[1024,256]{1,0:T(8,128)(2,1)} %tokens.3) | copy-start | bytes 1572868
  7.2 39.8 %copy-start.3 = (bf16[1024,448]{0,1:T(8,128)(2,1)S(1)}, bf16[1024,448]{0,1:T(8,128)(2,1)}, u32[]{:S(2)}) copy-start(bf16[1024,448]{0,1:T(8,128)(2,1)} %param.8) | copy-start | bytes 2752516
  7.2 139.8 %all-gather.3.cloned.1.call-start = ((), (), s32[]{:S(2)}) async-start(), calls=%async_computation.5 | async-start | bytes 4718592 | tf_op jit(solution)/shard_map/all_gather | solution.py:174
  9.2 11.0 %all-to-all-start = ((s32[8,1,8]{2,1,0:T(1,128)}), s32[8,1,8]{2,1,0:T(1,128)S(1)}, u32[]{:S(2)}, u32[]{:S(2)}) async-start(s32[8,1,8]{2,1,0:T(1,128)} %broadcast_in_dim.7), calls=%async_computation | async-start | bytes 8192 | tf_op jit(solution)/shard_map/all_to_all | solution.py:197
  20.1 1.0 copy-start.7
  21.2 0.9 copy-start.8
  22.1 24.8 %copy-start.10 = (s32[1,8]{1,0:T(1,128)S(1)}, s32[1,8]{1,0:T(1,128)}, u32[]{:S(2)}) copy-start(s32[1,8]{1,0:T(1,128)} %used.3) | copy-start | bytes 100
  22.1 24.9 %copy-start.11 = (s32[1,8]{1,0:T(1,128)S(1)}, s32[1,8]{1,0:T(1,128)}, u32[]{:S(2)}) copy-start(s32[1,8]{1,0:T(1,128)} %order.3) | copy-start | bytes 100
  48.8 25.0 %all-to-all-start.2 = ((bf16[32,32,128]{2,1,0:T(8,128)(2,1)}), bf16[32,32,128]{2,1,0:T(8,128)(2,1)S(1)}, u32[]{:S(2)}, u32[]{:S(2)}) async-start(bf16[32,32,128]{2,1,0:T(8,128)(2,1)} %bitcast.12), calls=%async_computation.2 | async-start | bytes 524288 | tf_op jit(solution)/shard_map/all_to_all | solution.py:227
  74.7 14.7 %all-to-all-start.3 = ((bf16[32,32,128]{2,1,0:T(8,128)(2,1)}), bf16[32,32,128]{2,1,0:T(8,128)(2,1)S(1)}, u32[]{:S(2)}, u32[]{:S(2)}) async-start(bf16[32,32,128]{2,1,0:T(8,128)(2,1)} %broadcast_in_dim.16), calls=%async_computation.3 | async-start | bytes 524288 | tf_op jit(solution)/shard_map/all_to_all | solution.py:229
  84.4 21.7 %collective-permute-start = (bf16[448,1024]{1,0:T(8,128)(2,1)}, bf16[448,1024]{1,0:T(8,128)(2,1)}, u32[]{:S(2)}, u32[]{:S(2)}) collective-permute-start(bf16[448,1024]{1,0:T(8,128)(2,1)} %get-tuple-element.15), channel_id=1, source_target_pairs={{0,3},{1,0},{2,1},{3,2},{4,7},{5,4},{6,5},{7,6},{8,11},{9,8},{10,9... | collective-permute-start | bytes 2752520 | tf_op jit(solution)/shard_map/ppermute | solution.py:155
  86.8 41.0 %collective-permute-start.1 = (bf16[448,1024]{1,0:T(8,128)(2,1)}, bf16[448,1024]{1,0:T(8,128)(2,1)}, u32[]{:S(2)}, u32[]{:S(2)}) collective-permute-start(bf16[448,1024]{1,0:T(8,128)(2,1)} %get-tuple-element.16), channel_id=1, source_target_pairs={{0,2},{1,3},{2,0},{3,1},{4,6},{5,7},{6,4},{7,5},{8,10},{9,11},{10,... | collective-permute-start | bytes 2752520 | tf_op jit(solution)/shard_map/ppermute | solution.py:155
  87.4 43.3 %collective-permute-start.2 = (bf16[448,1024]{1,0:T(8,128)(2,1)}, bf16[448,1024]{1,0:T(8,128)(2,1)}, u32[]{:S(2)}, u32[]{:S(2)}) collective-permute-start(bf16[448,1024]{1,0:T(8,128)(2,1)} %get-tuple-element.17), channel_id=1, source_target_pairs={{0,1},{1,2},{2,3},{3,0},{4,5},{5,6},{6,7},{7,4},{8,9},{9,10},{10,1... | collective-permute-start | bytes 2752520 | tf_op jit(solution)/shard_map/ppermute | solution.py:155
  90.8 1.2 copy-start.4
  91.9 1.2 copy-start.12
  93.2 51.7 %all-to-all-start.4 = ((bf16[8,2,64,768]{3,2,1,0:T(8,128)(2,1)}), bf16[8,2,64,768]{3,2,1,0:T(8,128)(2,1)S(1)}, u32[]{:S(2)}, u32[]{:S(2)}) async-start(bf16[8,2,64,768]{3,2,1,0:T(8,128)(2,1)} %bitcast.47), calls=%async_computation.4 | async-start | bytes 3145728 | tf_op jit(solution)/shard_map/all_to_all | solution.py:260
  100.5 38.1 %copy-start.9 = (s32[4]{0:T(128)S(1)}, s32[4]{0:T(128)}, u32[]{:S(2)}) copy-start(s32[4]{0:T(128)} %pad_add_fusion.meta) | copy-start | bytes 52
  106.0 31.6 %collective-permute-start.3 = (bf16[448,1024]{1,0:T(8,128)(2,1)}, bf16[448,1024]{1,0:T(8,128)(2,1)S(1)}, u32[]{:S(2)}, u32[]{:S(2)}) collective-permute-start(bf16[448,1024]{1,0:T(8,128)(2,1)} %collective-permute-done.refs_0_), channel_id=1, source_target_pairs={{0,32},{32,0},{1,33},{33,1},{2,34},{34,2},{3,35},{35,3},{4,36},{36... | collective-permute-start | bytes 2752520 | tf_op jit(solution)/shard_map/ppermute | solution.py:155
  127.8 10.7 %collective-permute-start.4 = (bf16[448,1024]{1,0:T(8,128)(2,1)}, bf16[448,1024]{1,0:T(8,128)(2,1)}, u32[]{:S(2)}, u32[]{:S(2)}) collective-permute-start(bf16[448,1024]{1,0:T(8,128)(2,1)} %collective-permute-done.1.refs_1_), channel_id=1, source_target_pairs={{0,32},{32,0},{1,33},{33,1},{2,34},{34,2},{3,35},{35,3},{4,36},{36... | collective-permute-start | bytes 2752520 | tf_op jit(solution)/shard_map/ppermute | solution.py:155
  130.7 7.9 %collective-permute-start.5 = (bf16[448,1024]{1,0:T(8,128)(2,1)}, bf16[448,1024]{1,0:T(8,128)(2,1)}, u32[]{:S(2)}, u32[]{:S(2)}) collective-permute-start(bf16[448,1024]{1,0:T(8,128)(2,1)} %collective-permute-done.2.refs_2_), channel_id=1, source_target_pairs={{0,32},{32,0},{1,33},{33,1},{2,34},{34,2},{3,35},{35,3},{4,36},{36... | collective-permute-start | bytes 2752520 | tf_op jit(solution)/shard_map/ppermute | solution.py:155
  137.6 0.9 copy-start.5
  138.6 1.2 copy-start.6
  142.4 2.4 %copy-start = (bf16[3,448,2048]{2,1,0:T(8,128)(2,1)}, bf16[3,448,2048]{2,1,0:T(8,128)(2,1)S(1)}, u32[]{:S(2)}) copy-start(bf16[3,448,2048]{2,1,0:T(8,128)(2,1)S(1)} %shard_map.100) | copy-start | bytes 16515076
  153.7 4.1 %copy-start.1 = (bf16[3,448,2048]{2,1,0:T(8,128)(2,1)S(1)}, bf16[3,448,2048]{2,1,0:T(8,128)(2,1)}, u32[]{:S(2)}) copy-start(bf16[3,448,2048]{2,1,0:T(8,128)(2,1)} %copy-done) | copy-start | bytes 16515076
  157.7 4.5 %copy-start.14 = (bf16[1024,2048]{1,0:T(8,128)(2,1)S(1)}, bf16[1024,2048]{1,0:T(8,128)(2,1)}, u32[]{:S(2)}) copy-start(bf16[1024,2048]{1,0:T(8,128)(2,1)} %shard_map.97) | copy-start | bytes 12582916
  161.5 12.3 %collective-permute-start.10 = (bf16[224,1024]{1,0:T(8,128)(2,1)S(1)}, bf16[224,1024]{1,0:T(8,128)(2,1)S(1)}, u32[]{:S(2)}, u32[]{:S(2)}) collective-permute-start(bf16[224,1024]{1,0:T(8,128)(2,1)S(1)} %convolution_convert_fusion), channel_id=1, source_target_pairs={{0,3},{1,0},{2,1},{3,2},{4,7},{5,4},{6,5},{7,6},{8,11},{9,8},{10,9... | collective-permute-start | bytes 1376264 | tf_op jit(solution)/shard_map/ppermute | solution.py:155
  163.6 13.3 %collective-permute-start.6 = (bf16[224,1024]{1,0:T(8,128)(2,1)S(1)}, bf16[224,1024]{1,0:T(8,128)(2,1)S(1)}, u32[]{:S(2)}, u32[]{:S(2)}) collective-permute-start(bf16[224,1024]{1,0:T(8,128)(2,1)S(1)} %convolution_convert_fusion.3), channel_id=1, source_target_pairs={{0,1},{1,2},{2,3},{3,0},{4,5},{5,6},{6,7},{7,4},{8,9},{9,10},{10,1... | collective-permute-start | bytes 1376264 | tf_op jit(solution)/shard_map/ppermute | solution.py:155
  166.1 17.5 %collective-permute-start.9 = (bf16[224,1024]{1,0:T(8,128)(2,1)S(1)}, bf16[224,1024]{1,0:T(8,128)(2,1)S(1)}, u32[]{:S(2)}, u32[]{:S(2)}) collective-permute-start(bf16[224,1024]{1,0:T(8,128)(2,1)S(1)} %convolution_convert_fusion.1), channel_id=1, source_target_pairs={{0,3},{1,0},{2,1},{3,2},{4,7},{5,4},{6,5},{7,6},{8,11},{9,8},{10,9... | collective-permute-start | bytes 1376264 | tf_op jit(solution)/shard_map/ppermute | solution.py:155
  167.9 18.5 %collective-permute-start.8 = (bf16[224,1024]{1,0:T(8,128)(2,1)S(1)}, bf16[224,1024]{1,0:T(8,128)(2,1)S(1)}, u32[]{:S(2)}, u32[]{:S(2)}) collective-permute-start(bf16[224,1024]{1,0:T(8,128)(2,1)S(1)} %convolution_convert_fusion.2), channel_id=1, source_target_pairs={{0,1},{1,2},{2,3},{3,0},{4,5},{5,6},{6,7},{7,4},{8,9},{9,10},{10,1... | collective-permute-start | bytes 1376264 | tf_op jit(solution)/shard_map/ppermute | solution.py:155
  175.3 3.2 %copy-start.13 = (f32[448,1024]{1,0:T(8,128)S(1)}, f32[448,1024]{1,0:T(8,128)}, u32[]{:S(2)}) copy-start(f32[448,1024]{1,0:T(8,128)} %copy-done.12) | copy-start | bytes 5505028
  175.3 3.2 %copy-start.15 = (bf16[448,2048]{1,0:T(8,128)(2,1)S(1)}, bf16[448,2048]{1,0:T(8,128)(2,1)}, u32[]{:S(2)}) copy-start(bf16[448,2048]{1,0:T(8,128)(2,1)} %shard_map.96) | copy-start | bytes 5505028
  175.3 18.2 %collective-permute-start.11 = (bf16[224,1024]{1,0:T(8,128)(2,1)S(1)}, bf16[224,1024]{1,0:T(8,128)(2,1)S(1)}, u32[]{:S(2)}, u32[]{:S(2)}) collective-permute-start(bf16[224,1024]{1,0:T(8,128)(2,1)S(1)} %fusion.1), channel_id=1, source_target_pairs={{0,3},{1,0},{2,1},{3,2},{4,7},{5,4},{6,5},{7,6},{8,11},{9,8},{10,9... | collective-permute-start | bytes 1376264 | tf_op jit(solution)/shard_map/ppermute | solution.py:155
  178.4 17.9 %collective-permute-start.7 = (bf16[224,1024]{1,0:T(8,128)(2,1)S(1)}, bf16[224,1024]{1,0:T(8,128)(2,1)S(1)}, u32[]{:S(2)}, u32[]{:S(2)}) collective-permute-start(bf16[224,1024]{1,0:T(8,128)(2,1)S(1)} %fusion), channel_id=1, source_target_pairs={{0,1},{1,2},{2,3},{3,0},{4,5},{5,6},{6,7},{7,4},{8,9},{9,10},{10,1... | collective-permute-start | bytes 1376264 | tf_op jit(solution)/shard_map/ppermute | solution.py:155
Sparse Core Ops, SparseCore 0:
  9.8 64.0 all-gather.2

commit v6 on v5

--- a/solution.py
+++ b/solution.py
@@ -107,26 +107,50 @@
                 grad_b[local] += terms[group, place, :, width:width + units].astype(F32)
 
 
-def place_kernel(meta, *refs):
-    got, swapped, out = refs[:3], refs[3:6], refs[6]
-    span = got[0].shape[1]
+def times_rows(meta, got, swapped, tokens):
+    span = got.shape[1]
     core = meta[1]
-    for r in range(3):
-        out[r, :, pl.ds(pl.multiple_of(core * span, span), span)] = got[r][...]
-        out[r, :, pl.ds(pl.multiple_of((1 - core) * span, span), span)] = swapped[r][...]
+    total = None
+    for source, block in ((got, core), (swapped, 1 - core)):
+        place = pl.ds(pl.multiple_of(block * span, span), span)
+        term = lax.dot_general(
+            source[...], tokens[:, place], (((1,), (1,)), ((), ())), preferred_element_type=F32
+        )
+        total = term if total is None else total + term
+    return total
+
+
+def shared_kernel(meta, got2, swap2, got1, swap1, got3, swap3, tokens, *outs):
+    far_up, far_down, up_soon, down_soon, up_late, down_late = outs
+    half = far_up.shape[0]
+    far = times_rows(meta, got2, swap2, tokens)
+    far_up[...] = far[:half].astype(BF)
+    far_down[...] = far[half:].astype(BF)
+    near = times_rows(meta, got1, swap1, tokens)
+    up_late[...] = near[:half]
+    up_soon[...] = near[half:].astype(BF)
+    near = times_rows(meta, got3, swap3, tokens)
+    down_soon[...] = near[:half].astype(BF)
+    down_late[...] = near[half:]
+
+
+def own_kernel(meta, *refs):
+    weights, tokens, delta, out, rows = refs[:-4], *refs[-4:]
+    width = weights[0].shape[1]
+
+    @pl.when(pl.program_id(0) == 0)
+    def _():
+        for block, source in enumerate(weights):
+            rows[:, block * width:(block + 1) * width] = source[...]
+
+    out[...] = delta[...] + lax.dot_general(
+        rows[...], tokens[...], (((1,), (1,)), ((), ())), preferred_element_type=F32
+    )
 
 
 def fetch_kernel(meta, *refs):
     for source, out in zip(refs[:3], refs[3:]):
         out[...] = source[...]
-
-
-def join_blocks_kernel(source, out):
-    out[...] = source[0]
-
-
-def copy_kernel(meta, source, out):
-    out[...] = source[...]
 
 
 def join_kernel(base, up_late, up_soon, down_soon, down_late, out):
@@ -139,7 +163,7 @@
     ).astype(BF)
 
 
-def call(kernel, outs, specs, scratch=(), limit=16):
+def call(kernel, outs, specs, scratch=(), limit=8):
     return pl.pallas_call(
         kernel,
         out_shape=outs,
@@ -171,7 +195,7 @@
     meta = jnp.stack([x, core, z, y]).astype(jnp.int32)
     me_arr = me.reshape(1).astype(jnp.int32)
 
-    gathered = lax.all_gather(tokens, "z")
+    gathered = lax.all_gather(tokens, "z", axis=1, tiled=True)
 
     weight_t = weight.T
     span = n_z // 2
@@ -191,7 +215,6 @@
             out_specs=[pl.BlockSpec((units, width), lambda i, meta: (0, i))] * 3,
         ),
     )(meta, weight_t, weight_t, weight_t)
-    pieces = tuple(hop(item, "y", -r) for r, item in zip((1, 2, 3), fetched))
 
     down_t = jnp.transpose(down, (0, 2, 1))
     used_all = lax.all_to_all(
@@ -200,6 +223,8 @@
     picked = call(pick_kernel, whole((owners, 2, rank, packed), BF), [SMEM, SMEM, VMEM, VMEM])(
         me_arr, used_all, down_t, up
     )
+    picked, fetched = together((picked, fetched))
+    pieces = tuple(hop(item, "y", -r) for r, item in zip((1, 2, 3), fetched))
     factors = lax.all_to_all(picked, DP, 0, 0, tiled=True).reshape(owners * 2, rank, packed)
     cot_t = cotangent.T
     sizes = dict(rank=rank, width=width, units=units)
@@ -208,49 +233,53 @@
         whole((rows, 2 * rank), BF),
         [SMEM, SMEM, VMEM, VMEM, VMEM],
     )(used, order, factors, tokens, cot_t)
-    part, weight_t = together((part, weight_t))
-    own_weight = pl.pallas_call(
-        copy_kernel,
-        out_shape=whole((units, n_z * width), BF),
-        grid_spec=pltpu.PrefetchScalarGridSpec(
-            num_scalar_prefetch=1,
-            grid=(n_z,),
-            in_specs=[pl.BlockSpec((units, width), lambda i, meta: (0, i * n_y + meta[3]))],
-            out_specs=pl.BlockSpec((units, width), lambda i, meta: (0, i)),
-        ),
-    )(meta, weight_t)
-    swapped = tuple(hop(item, "core", 1) for item in pieces)
-    wide_weight = call(
-        place_kernel, whole((n_y - 1, units, n_z * width), BF), [SMEM] + [VMEM] * 6, limit=24
-    )(meta, *pieces, *swapped)
     share = rows // members
     parts = lax.all_to_all(part.reshape(members, share, 2 * rank), MP, 0, 0, tiled=True)
     summed = jnp.sum(parts.astype(F32), axis=0).astype(BF)
+    summed, pieces = together((summed, pieces))
+    swapped = tuple(hop(item, "core", 1) for item in pieces)
     both = lax.all_to_all(
         jnp.broadcast_to(summed[None], (members,) + summed.shape), MP, 0, 0, tiled=True
     ).reshape(rows, 2 * rank)
 
-    wide_tokens = pl.pallas_call(
-        join_blocks_kernel,
-        out_shape=whole((rows, n_z * width), BF),
-        grid=(n_z,),
-        in_specs=[pl.BlockSpec((1, rows, width), lambda i: (i, 0, 0))],
-        out_specs=pl.BlockSpec((rows, width), lambda i: (0, i)),
-    )(gathered)
-    half = units // 2
-
-    def product(weights):
-        return lax.dot_general(
-            weights, wide_tokens, (((1,), (1,)), ((), ())), preferred_element_type=F32
-        )
-
-    near, far, back = (wide_weight[r] for r in range(3))
-    far_up = hop(product(far[:half]).astype(BF), "y", 1)
-    far_down = hop(product(far[half:]).astype(BF), "y", -1)
-    up_soon = hop(product(near[half:]).astype(BF), "y", 1)
-    down_soon = hop(product(back[:half]).astype(BF), "y", -1)
-    up_late = hop((product(near[:half]) + far_up.astype(F32)).astype(BF), "y", 1)
-    down_late = hop((product(back[half:]) + far_down.astype(F32)).astype(BF), "y", -1)
+    half, step = units // 2, 256
+    side = span * width
+    narrow = pltpu.HBM((half, rows), BF)
+    part_block = pl.BlockSpec((half, step), lambda i, meta: (0, i))
+    full_block = pl.BlockSpec((units, step), lambda i, meta: (0, i))
+    token_block = pl.BlockSpec((step, n_z * width), lambda i, meta: (i, 0))
+    all_rows = pl.BlockSpec((units, side), lambda i, meta: (0, 0))
+
+    def over_tokens(kernel, outs, ins, out_specs, scratch, work=1):
+        return pl.pallas_call(
+            kernel,
+            out_shape=outs,
+            grid_spec=pltpu.PrefetchScalarGridSpec(
+                num_scalar_prefetch=1,
+                grid=(rows // step,),
+                in_specs=ins,
+                out_specs=out_specs,
+                scratch_shapes=scratch,
+            ),
+            compiler_params=pltpu.CompilerParams(vmem_limit_bytes=48 * 1024 * 1024),
+            cost_estimate=pl.CostEstimate(flops=work, bytes_accessed=work, transcendentals=0),
+        )
+
+    got1, got2, got3 = pieces
+    swap1, swap2, swap3 = swapped
+    broad = pltpu.HBM((half, rows), F32)
+    far_up, far_down, up_soon, down_soon, up_late, down_late = over_tokens(
+        shared_kernel,
+        [narrow] * 4 + [broad] * 2,
+        [all_rows] * 6 + [token_block],
+        [part_block] * 6,
+        [],
+    )(meta, got2, swap2, got1, swap1, got3, swap3, gathered)
+    both, far_up, far_down = together((both, far_up, far_down))
+    far_up, far_down = hop(far_up, "y", 1), hop(far_down, "y", -1)
+    up_soon, down_soon = hop(up_soon, "y", 1), hop(down_soon, "y", -1)
+    up_late = hop((up_late + far_up.astype(F32)).astype(BF), "y", 1)
+    down_late = hop((down_late + far_down.astype(F32)).astype(BF), "y", -1)
 
     send, delta = call(
         functools.partial(grads_kernel, **sizes),
@@ -264,7 +293,17 @@
         [SMEM, SMEM, VMEM],
     )(me_arr, used_all, terms)
 
-    base = together(product(own_weight) + delta)
+    def own_block(block):
+        return pl.BlockSpec((units, width), lambda i, meta: (0, block * n_y + meta[3]))
+
+    base = over_tokens(
+        own_kernel,
+        whole((units, rows), F32),
+        [own_block(block) for block in range(n_z)] + [token_block, full_block],
+        full_block,
+        [pltpu.VMEM((units, n_z * width), BF)],
+        work=20_000_000_000,
+    )(meta, *[weight_t] * n_z, gathered, delta)
     out = call(join_kernel, whole((units, rows), BF), [VMEM] * 5)(
         base, up_late, up_soon, down_soon, down_late
     )

time: 205 us -> 145 us (0.71)
  waiting for transfers between devices: 51.1 us -> 28.4 us
  starting transfers between devices: 59.9 us -> 37.9 us
  matrix products: 15.5 us -> 0 us
  local copies, waits for them, and re-layouts: 10.9 us -> 4.45 us
  blocking collectives: 23.9 us -> 26.5 us
  other arithmetic: 0.65 us -> 3.11 us
  Pallas kernels: 28 us -> 30.1 us
    ppermute x12, waiting for transfers between devices: 30.1 us -> 7.07 us  [hop(): return lax.ppermute(value, axis, [(i, (i + step) % n) for i in range(n)])]
    ppermute x12, starting transfers between devices: 31.3 us -> 10.3 us  [hop(): return lax.ppermute(value, axis, [(i, (i + step) % n) for i in range(n)])]
    dot_general x7 -> x0, matrix products: 15.5 us -> none  [product(): lax.dot_general(weights, wide_tokens, (((1,), (1,)), ((), ())), preferred...]
    unnamed x32 -> x24, local copies, waits for them, and re-layouts: 8.95 us -> 2.47 us
    all_to_all x1, starting transfers between devices: 10.5 us -> 4.97 us  [on_device(): lax.all_to_all(picked, DP, 0, 0, tiled=True)]
    all_to_all x1, waiting for transfers between devices: 4.52 us -> 0.01 us  [on_device(): lax.all_to_all(jnp.broadcast_to(used[None], (owners,) + used.shape), DP,...]
    all_to_all x1, starting transfers between devices: 4.3 us -> 8.66 us  [on_device(): lax.all_to_all(jnp.broadcast_to(summed[None], (members,) + summed.shape),...]
    all_to_all x1, waiting for transfers between devices: 14.5 us -> 17.7 us  [on_device(): lax.all_to_all(picked, DP, 0, 0, tiled=True)]
  transfers between devices with their start and end apart: 17 -> 17, of which waited for: 10 -> 5; matrix products, arithmetic and copies ran while one was open for 5% -> 4% of each run, Pallas kernels for 10% -> 19%
where the time goes in v6:
time: 145 us
  starting transfers between devices  37.9 us (26%)
  Pallas kernels  30.1 us (21%)
  waiting for transfers between devices  28.4 us (20%)
  blocking collectives  26.5 us (18%)
  between operations  14.2 us (10%)
  local copies, waits for them, and re-layouts  4.45 us (3%)
  other arithmetic  3.11 us (2%)
    all_to_all x1, blocking collectives, on_device(): lax.all_to_all(part.reshape(members, share, 2 * rank), MP, 0, 0, tiled=True)  26.5 us
    all_to_all x1, waiting for transfers between devices, on_device(): lax.all_to_all(picked, DP, 0, 0, tiled=True)  17.7 us
    pallas_call x1, Pallas kernels, on_device(): over_tokens(shared_kernel, [narrow] * 4 + [broad] * 2, [all_rows] * 6 + [...  10.9 us
    ppermute x12, starting transfers between devices, hop(): return lax.ppermute(value, axis, [(i, (i + step) % n) for i in range(n)])  10.3 us
    all_to_all x1, starting transfers between devices, on_device(): lax.all_to_all(jnp.broadcast_to(summed[None], (members,) + summed.shape),...  8.66 us
    all_to_all x1, starting transfers between devices, on_device(): lax.all_to_all(send.reshape(owners, 2, rank, packed), DP, 0, 0, tiled=True)  7.52 us
    ppermute x12, waiting for transfers between devices, hop(): return lax.ppermute(value, axis, [(i, (i + step) % n) for i in range(n)])  7.07 us
    all_to_all x1, starting transfers between devices, on_device(): lax.all_to_all(jnp.broadcast_to(used[None], (owners,) + used.shape), DP,...  6.45 us
  transfers between devices with their start and end apart: 17, of which 5 were waited for; matrix products, arithmetic and copies ran while one was open for 4% of the time, Pallas kernels for 19%

profile of v6, /device:TPU:1, one launch (start us, length us, event | category | flops | bytes accessed | tf_op | source)
XLA Modules:
  0.0 144.7 jit_solution(15548535342343226193)
XLA Ops:
  7.2 0.0 all-gather.2.cloned.1.call-start
  7.2 0.7 all-gather.2.cloned.1.call-update
  7.9 1.3 broadcast_in_dim.7
  9.2 6.5 %all-to-all-start = ((s32[8,1,8]{2,1,0:T(1,128)}), s32[8,1,8]{2,1,0:T(1,128)S(1)}, u32[]{:S(2)}, u32[]{:S(2)}) async-start(s32[8,1,8]{2,1,0:T(1,128)} %broadcast_in_dim.7), calls=%async_computation | async-start | bytes 8192 | tf_op jit(solution)/shard_map/all_to_all | solution.py:220
  15.6 0.6 pad_add_fusion.meta
  16.2 4.9 %shard_map.95 = (bf16[448,1024]{1,0:T(8,128)(2,1)}, bf16[448,1024]{1,0:T(8,128)(2,1)}, bf16[448,1024]{1,0:T(8,128)(2,1)}) custom-call(s32[4]{0:T(128)} %pad_add_fusion.meta, bf16[448,8192]{1,0:T(8,128)(2,1)} %bitcast.27, bf16[448,8192]{1,0:T(8,128)(2,1)} %bitcast.28, bf16[448,8192]{1,0:T(8,128)(2,1)} %bitcast.29), custom_call_target="tpu_custom_call" | custom-call | tf_op jit(solution)/shard_map/pallas_call | solution.py:208
  21.2 0.0 all-to-all-done
  21.2 0.0 copy-done.3
  21.2 0.0 copy-done.4
  21.2 2.1 %shard_map.94 = bf16[8,2,64,768]{3,2,1,0:T(8,128)(2,1)} custom-call(s32[1]{0:T(128)} %bitcast.5.me, s32[8,8]{1,0:T(8,128)S(1)} %bitcast.24, bf16[8,64,256]{2,1,0:T(8,128)(2,1)S(1)} %bitcast.23, bf16[8,64,448]{2,1,0:T(8,128)(2,1)S(1)} %copy-done.3), custom_call_target="tpu_custom_call" | custom-call | tf_op jit(solution)/shard_map/pallas_call | solution.py:223
  23.3 5.0 %all-to-all-start.1 = ((bf16[8,2,64,768]{3,2,1,0:T(8,128)(2,1)}), bf16[8,2,64,768]{3,2,1,0:T(8,128)(2,1)S(1)}, u32[]{:S(2)}, u32[]{:S(2)}) async-start(bf16[8,2,64,768]{3,2,1,0:T(8,128)(2,1)} %shard_map.94), calls=%async_computation.1 | async-start | bytes 3145728 | tf_op jit(solution)/shard_map/all_to_all | solution.py:228
  28.2 2.1 %collective-permute-start = (bf16[448,1024]{1,0:T(8,128)(2,1)}, bf16[448,1024]{1,0:T(8,128)(2,1)}, u32[]{:S(2)}, u32[]{:S(2)}) collective-permute-start(bf16[448,1024]{1,0:T(8,128)(2,1)} %get-tuple-element.31), channel_id=1, source_target_pairs={{0,3},{1,0},{2,1},{3,2},{4,7},{5,4},{6,5},{7,6},{8,11},{9,8},{10,9... | collective-permute-start | bytes 2752520 | tf_op jit(solution)/shard_map/ppermute | solution.py:179
  30.3 0.3 collective-permute-start.1
  30.6 0.7 collective-permute-start.2
  31.3 17.7 %all-to-all-done.1 = bf16[8,2,64,768]{3,2,1,0:T(8,128)(2,1)S(1)} async-done(((bf16[8,2,64,768]{3,2,1,0:T(8,128)(2,1)}), bf16[8,2,64,768]{3,2,1,0:T(8,128)(2,1)S(1)}, u32[]{:S(2)}, u32[]{:S(2)}) %all-to-all-start.1) | async-done | bytes 1572896 | tf_op jit(solution)/shard_map/all_to_all | solution.py:228
  49.1 0.0 copy-done
  49.1 0.0 copy-done.1
  49.1 0.0 copy-done.6
  49.1 0.0 copy-done.7
  49.1 0.0 copy-start.5
  49.1 1.1 shard_map.96
  50.2 26.5 %all_to_all.25 = bf16[32,32,128]{2,1,0:T(8,128)(2,1)S(1)} all-to-all(bf16[32,32,128]{2,1,0:T(8,128)(2,1)S(1)} %bitcast.22), channel_id=1, replica_groups=mesh['x'=4,'core'=2,'z'=8,'y'=4] {'z','y'}, dimensions={0} | all-to-all | bytes 524288 | tf_op jit(solution)/shard_map/all_to_all | solution.py:237
  76.8 0.1 reduce_sum.12
  76.8 0.0 collective-permute-done.got1
  76.8 0.0 collective-permute-done.1.got2
  76.8 0.0 collective-permute-done.2.got3
  76.9 0.6 collective-permute-start.3
  77.5 0.1 collective-permute-start.4
  77.6 0.4 collective-permute-start.5
  78.0 0.7 broadcast_in_dim.16
  78.7 8.7 %all-to-all-start.3 = ((bf16[32,32,128]{2,1,0:T(8,128)(2,1)}), bf16[32,32,128]{2,1,0:T(8,128)(2,1)S(1)}, u32[]{:S(2)}, u32[]{:S(2)}) async-start(bf16[32,32,128]{2,1,0:T(8,128)(2,1)} %broadcast_in_dim.16), calls=%async_computation.3 | async-start | bytes 524288 | tf_op jit(solution)/shard_map/all_to_all | solution.py:241
  87.4 0.0 collective-permute-done.3.swap2
  87.4 0.0 collective-permute-done.4.swap1
  87.4 0.0 collective-permute-done.5.swap3
  87.4 0.0 all-gather.2.cloned.1.call-done.tokens.refs_8_
  87.4 0.0 copy-done.5
  87.4 10.9 %shard_map.97 = (bf16[224,1024]{1,0:T(8,128)(2,1)}, bf16[224,1024]{1,0:T(8,128)(2,1)}, bf16[224,1024]{1,0:T(8,128)(2,1)}, bf16[224,1024]{1,0:T(8,128)(2,1)}, f32[224,1024]{1,0:T(8,128)}, /*index=5*/f32[224,1024]{1,0:T(8,128)}) custom-call(s32[4]{0:T(128)S(1)} %copy-done.5, bf16[448,1024]{1,0:T(8,128)(2,1)} %collective-permute-done.1.got2, ...), custom_call_target="tpu_custom_call" | custom-call | flops 1 | bytes 1 | tf_op jit(solution)/shard_map/pallas_call | solution.py:271
  98.3 1.0 all-to-all-done.3
  99.3 1.6 %collective-permute-start.10 = (bf16[224,1024]{1,0:T(8,128)(2,1)}, bf16[224,1024]{1,0:T(8,128)(2,1)}, u32[]{:S(2)}, u32[]{:S(2)}) collective-permute-start(bf16[224,1024]{1,0:T(8,128)(2,1)} %get-tuple-element.47), channel_id=1, source_target_pairs={{0,3},{1,0},{2,1},{3,2},{4,7},{5,4},{6,5},{7,6},{8,11},{9,8},{10,9... | collective-permute-start | bytes 1376264 | tf_op jit(solution)/shard_map/ppermute | solution.py:179
  100.9 0.0 collective-permute-start.6
  100.9 1.4 shard_map.98
  102.3 0.0 copy-start.2
  102.3 1.1 copy-done.2
  103.4 1.3 copy-done.8
  104.7 0.4 collective-permute-start.8
  105.1 2.3 %collective-permute-start.9 = (bf16[224,1024]{1,0:T(8,128)(2,1)}, bf16[224,1024]{1,0:T(8,128)(2,1)S(1)}, u32[]{:S(2)}, u32[]{:S(2)}) collective-permute-start(bf16[224,1024]{1,0:T(8,128)(2,1)} %get-tuple-element.45), channel_id=1, source_target_pairs={{0,3},{1,0},{2,1},{3,2},{4,7},{5,4},{6,5},{7,6},{8,11},{9,8},{10,9... | collective-permute-start | bytes 1376264 | tf_op jit(solution)/shard_map/ppermute | solution.py:179
  107.4 7.5 %all-to-all-start.4 = ((bf16[8,2,64,768]{3,2,1,0:T(8,128)(2,1)}), bf16[8,2,64,768]{3,2,1,0:T(8,128)(2,1)S(1)}, u32[]{:S(2)}, u32[]{:S(2)}) async-start(bf16[8,2,64,768]{3,2,1,0:T(8,128)(2,1)} %bitcast.20), calls=%async_computation.4 | async-start | bytes 3145728 | tf_op jit(solution)/shard_map/all_to_all | solution.py:289
  114.9 0.0 collective-permute-done.10
  114.9 0.0 copy-done.11
  114.9 0.0 copy-start.9
  114.9 1.3 add_convert_fusion
  116.2 1.2 collective-permute-start.11
  117.4 0.0 collective-permute-done.6
  117.4 0.0 copy-done.10
  117.4 1.2 add_convert_fusion.1
  118.6 0.6 collective-permute-start.7
  119.2 6.2 %shard_map.99.base = f32[448,1024]{1,0:T(8,128)S(1)} custom-call(s32[4]{0:T(128)S(1)} %copy-done.5, bf16[448,8192]{1,0:T(8,128)(2,1)} %bitcast.30, bf16[448,8192]{1,0:T(8,128)(2,1)} %bitcast.31, bf16[448,8192]{1,0:T(8,128)(2,1)} %bitcast.32, bf16[448,8192]{1,0:T(8,128)(2,1)} %bitcast.33, bf16[448,8192]{1,0:T(8,128)(2,1)} %bitcast.34, ...), custom_call_target="tpu_custom_call" | custom-call | flops 20000000000 | bytes 20000000000 | tf_op jit(solution)/shard_map/pallas_call | solution.py:299
  125.4 0.0 collective-permute-done.8.up_soon
  125.4 0.0 collective-permute-done.9.down_soon
  125.4 3.7 %collective-permute-done.11.down_late = bf16[224,1024]{1,0:T(8,128)(2,1)S(1)} collective-permute-done((bf16[224,1024]{1,0:T(8,128)(2,1)S(1)}, bf16[224,1024]{1,0:T(8,128)(2,1)S(1)}, u32[]{:S(2)}, u32[]{:S(2)}) %collective-permute-start.11) | collective-permute-done | bytes 458784 | tf_op jit(solution)/shard_map/ppermute | solution.py:179
  129.1 3.3 %collective-permute-done.7.up_late = bf16[224,1024]{1,0:T(8,128)(2,1)S(1)} collective-permute-done((bf16[224,1024]{1,0:T(8,128)(2,1)S(1)}, bf16[224,1024]{1,0:T(8,128)(2,1)S(1)}, u32[]{:S(2)}, u32[]{:S(2)}) %collective-permute-start.7) | collective-permute-done | bytes 458784 | tf_op jit(solution)/shard_map/ppermute | solution.py:179
  132.5 1.2 shard_map.100
  133.7 1.9 %all-to-all-done.4.terms = bf16[8,2,64,768]{3,2,1,0:T(8,128)(2,1)S(1)} async-done(((bf16[8,2,64,768]{3,2,1,0:T(8,128)(2,1)}), bf16[8,2,64,768]{3,2,1,0:T(8,128)(2,1)S(1)}, u32[]{:S(2)}, u32[]{:S(2)}) %all-to-all-start.4) | async-done | bytes 1572896 | tf_op jit(solution)/shard_map/all_to_all | solution.py:289
  135.6 2.2 %shard_map.101 = (f32[8,64,256]{2,1,0:T(8,128)}, f32[8,64,448]{2,1,0:T(8,128)}) custom-call(s32[1]{0:T(128)} %bitcast.5.me, s32[8,8]{1,0:T(8,128)S(1)} %bitcast.25, bf16[8,2,64,768]{3,2,1,0:T(8,128)(2,1)S(1)} %all-to-all-done.4.terms), custom_call_target="tpu_custom_call" | custom-call | tf_op jit(solution)/shard_map/pallas_call | solution.py:290
  (10 shorter events, 0.0 us)
Async XLA Ops:
  7.2 80.3 %all-gather.2.cloned.1.call-start = ((), (), s32[]{:S(2)}) async-start(), calls=%async_computation.5 | async-start | bytes 4718592 | tf_op jit(solution)/shard_map/all_gather | solution.py:198
  9.2 12.0 %all-to-all-start = ((s32[8,1,8]{2,1,0:T(1,128)}), s32[8,1,8]{2,1,0:T(1,128)S(1)}, u32[]{:S(2)}, u32[]{:S(2)}) async-start(s32[8,1,8]{2,1,0:T(1,128)} %broadcast_in_dim.7), calls=%async_computation | async-start | bytes 8192 | tf_op jit(solution)/shard_map/all_to_all | solution.py:220
  16.2 5.0 %copy-start.3 = (bf16[8,64,448]{2,1,0:T(8,128)(2,1)S(1)}, bf16[8,64,448]{2,1,0:T(8,128)(2,1)}, u32[]{:S(2)}) copy-start(bf16[8,64,448]{2,1,0:T(8,128)(2,1)} %up.1) | copy-start | bytes 1376260
  16.2 5.0 %copy-start.4 = (bf16[8,256,64]{1,2,0:T(8,128)(2,1)S(1)}, bf16[8,256,64]{1,2,0:T(8,128)(2,1)}, u32[]{:S(2)}) copy-start(bf16[8,256,64]{1,2,0:T(8,128)(2,1)} %param.10) | copy-start | bytes 786436
  23.3 25.8 %copy-start = (bf16[1024,256]{1,0:T(8,128)(2,1)S(1)}, bf16[1024,256]{1,0:T(8,128)(2,1)}, u32[]{:S(2)}) copy-start(bf16[1024,256]{1,0:T(8,128)(2,1)} %tokens.3) | copy-start | bytes 1572868
  23.3 25.8 %copy-start.1 = (bf16[1024,448]{0,1:T(8,128)(2,1)S(1)}, bf16[1024,448]{0,1:T(8,128)(2,1)}, u32[]{:S(2)}) copy-start(bf16[1024,448]{0,1:T(8,128)(2,1)} %param.8) | copy-start | bytes 2752516
  23.3 25.8 %copy-start.6 = (s32[1,8]{1,0:T(1,128)S(1)}, s32[1,8]{1,0:T(1,128)}, u32[]{:S(2)}) copy-start(s32[1,8]{1,0:T(1,128)} %used.3) | copy-start | bytes 100
  23.3 25.8 %copy-start.7 = (s32[1,8]{1,0:T(1,128)S(1)}, s32[1,8]{1,0:T(1,128)}, u32[]{:S(2)}) copy-start(s32[1,8]{1,0:T(1,128)} %order.3) | copy-start | bytes 100
  23.3 25.8 %all-to-all-start.1 = ((bf16[8,2,64,768]{3,2,1,0:T(8,128)(2,1)}), bf16[8,2,64,768]{3,2,1,0:T(8,128)(2,1)S(1)}, u32[]{:S(2)}, u32[]{:S(2)}) async-start(bf16[8,2,64,768]{3,2,1,0:T(8,128)(2,1)} %shard_map.94), calls=%async_computation.1 | async-start | bytes 3145728 | tf_op jit(solution)/shard_map/all_to_all | solution.py:228
  28.2 48.6 %collective-permute-start = (bf16[448,1024]{1,0:T(8,128)(2,1)}, bf16[448,1024]{1,0:T(8,128)(2,1)}, u32[]{:S(2)}, u32[]{:S(2)}) collective-permute-start(bf16[448,1024]{1,0:T(8,128)(2,1)} %get-tuple-element.31), channel_id=1, source_target_pairs={{0,3},{1,0},{2,1},{3,2},{4,7},{5,4},{6,5},{7,6},{8,11},{9,8},{10,9... | collective-permute-start | bytes 2752520 | tf_op jit(solution)/shard_map/ppermute | solution.py:179
  30.3 46.5 %collective-permute-start.1 = (bf16[448,1024]{1,0:T(8,128)(2,1)}, bf16[448,1024]{1,0:T(8,128)(2,1)}, u32[]{:S(2)}, u32[]{:S(2)}) collective-permute-start(bf16[448,1024]{1,0:T(8,128)(2,1)} %get-tuple-element.32), channel_id=1, source_target_pairs={{0,2},{1,3},{2,0},{3,1},{4,6},{5,7},{6,4},{7,5},{8,10},{9,11},{10,... | collective-permute-start | bytes 2752520 | tf_op jit(solution)/shard_map/ppermute | solution.py:179
  30.6 46.2 %collective-permute-start.2 = (bf16[448,1024]{1,0:T(8,128)(2,1)}, bf16[448,1024]{1,0:T(8,128)(2,1)}, u32[]{:S(2)}, u32[]{:S(2)}) collective-permute-start(bf16[448,1024]{1,0:T(8,128)(2,1)} %get-tuple-element.33), channel_id=1, source_target_pairs={{0,1},{1,2},{2,3},{3,0},{4,5},{5,6},{6,7},{7,4},{8,9},{9,10},{10,1... | collective-permute-start | bytes 2752520 | tf_op jit(solution)/shard_map/ppermute | solution.py:179
  49.1 38.4 %copy-start.5 = (s32[4]{0:T(128)S(1)}, s32[4]{0:T(128)}, u32[]{:S(2)}) copy-start(s32[4]{0:T(128)} %pad_add_fusion.meta) | copy-start | bytes 52
  76.9 10.5 %collective-permute-start.3 = (bf16[448,1024]{1,0:T(8,128)(2,1)}, bf16[448,1024]{1,0:T(8,128)(2,1)}, u32[]{:S(2)}, u32[]{:S(2)}) collective-permute-start(bf16[448,1024]{1,0:T(8,128)(2,1)} %collective-permute-done.1.got2), channel_id=1, source_target_pairs={{0,32},{32,0},{1,33},{33,1},{2,34},{34,2},{3,35},{35,3},{4,36},{36... | collective-permute-start | bytes 2752520 | tf_op jit(solution)/shard_map/ppermute | solution.py:179
  77.5 9.9 %collective-permute-start.4 = (bf16[448,1024]{1,0:T(8,128)(2,1)}, bf16[448,1024]{1,0:T(8,128)(2,1)}, u32[]{:S(2)}, u32[]{:S(2)}) collective-permute-start(bf16[448,1024]{1,0:T(8,128)(2,1)} %collective-permute-done.got1), channel_id=1, source_target_pairs={{0,32},{32,0},{1,33},{33,1},{2,34},{34,2},{3,35},{35,3},{4,36},{36... | collective-permute-start | bytes 2752520 | tf_op jit(solution)/shard_map/ppermute | solution.py:179
  77.6 9.8 %collective-permute-start.5 = (bf16[448,1024]{1,0:T(8,128)(2,1)}, bf16[448,1024]{1,0:T(8,128)(2,1)}, u32[]{:S(2)}, u32[]{:S(2)}) collective-permute-start(bf16[448,1024]{1,0:T(8,128)(2,1)} %collective-permute-done.2.got3), channel_id=1, source_target_pairs={{0,32},{32,0},{1,33},{33,1},{2,34},{34,2},{3,35},{35,3},{4,36},{36... | collective-permute-start | bytes 2752520 | tf_op jit(solution)/shard_map/ppermute | solution.py:179
  78.7 20.6 %all-to-all-start.3 = ((bf16[32,32,128]{2,1,0:T(8,128)(2,1)}), bf16[32,32,128]{2,1,0:T(8,128)(2,1)S(1)}, u32[]{:S(2)}, u32[]{:S(2)}) async-start(bf16[32,32,128]{2,1,0:T(8,128)(2,1)} %broadcast_in_dim.16), calls=%async_computation.3 | async-start | bytes 524288 | tf_op jit(solution)/shard_map/all_to_all | solution.py:241
  99.3 15.6 %collective-permute-start.10 = (bf16[224,1024]{1,0:T(8,128)(2,1)}, bf16[224,1024]{1,0:T(8,128)(2,1)}, u32[]{:S(2)}, u32[]{:S(2)}) collective-permute-start(bf16[224,1024]{1,0:T(8,128)(2,1)} %get-tuple-element.47), channel_id=1, source_target_pairs={{0,3},{1,0},{2,1},{3,2},{4,7},{5,4},{6,5},{7,6},{8,11},{9,8},{10,9... | collective-permute-start | bytes 1376264 | tf_op jit(solution)/shard_map/ppermute | solution.py:179
  100.9 16.6 %collective-permute-start.6 = (bf16[224,1024]{1,0:T(8,128)(2,1)}, bf16[224,1024]{1,0:T(8,128)(2,1)}, u32[]{:S(2)}, u32[]{:S(2)}) collective-permute-start(bf16[224,1024]{1,0:T(8,128)(2,1)} %get-tuple-element.43), channel_id=1, source_target_pairs={{0,1},{1,2},{2,3},{3,0},{4,5},{5,6},{6,7},{7,4},{8,9},{9,10},{10,1... | collective-permute-start | bytes 1376264 | tf_op jit(solution)/shard_map/ppermute | solution.py:179
  102.3 1.2 copy-start.2
  103.4 1.3 copy-start.8
  104.7 10.2 %copy-start.11 = (f32[224,1024]{1,0:T(8,128)S(1)}, f32[224,1024]{1,0:T(8,128)}, u32[]{:S(2)}) copy-start(f32[224,1024]{1,0:T(8,128)} %get-tuple-element.46) | copy-start | bytes 2752516
  104.7 20.7 %collective-permute-start.8 = (bf16[224,1024]{1,0:T(8,128)(2,1)}, bf16[224,1024]{1,0:T(8,128)(2,1)S(1)}, u32[]{:S(2)}, u32[]{:S(2)}) collective-permute-start(bf16[224,1024]{1,0:T(8,128)(2,1)} %get-tuple-element.44), channel_id=1, source_target_pairs={{0,1},{1,2},{2,3},{3,0},{4,5},{5,6},{6,7},{7,4},{8,9},{9,10},{10,1... | collective-permute-start | bytes 1376264 | tf_op jit(solution)/shard_map/ppermute | solution.py:179
  105.1 20.4 %collective-permute-start.9 = (bf16[224,1024]{1,0:T(8,128)(2,1)}, bf16[224,1024]{1,0:T(8,128)(2,1)S(1)}, u32[]{:S(2)}, u32[]{:S(2)}) collective-permute-start(bf16[224,1024]{1,0:T(8,128)(2,1)} %get-tuple-element.45), channel_id=1, source_target_pairs={{0,3},{1,0},{2,1},{3,2},{4,7},{5,4},{6,5},{7,6},{8,11},{9,8},{10,9... | collective-permute-start | bytes 1376264 | tf_op jit(solution)/shard_map/ppermute | solution.py:179
  107.4 28.2 %all-to-all-start.4 = ((bf16[8,2,64,768]{3,2,1,0:T(8,128)(2,1)}), bf16[8,2,64,768]{3,2,1,0:T(8,128)(2,1)S(1)}, u32[]{:S(2)}, u32[]{:S(2)}) async-start(bf16[8,2,64,768]{3,2,1,0:T(8,128)(2,1)} %bitcast.20), calls=%async_computation.4 | async-start | bytes 3145728 | tf_op jit(solution)/shard_map/all_to_all | solution.py:289
  114.9 2.5 %copy-start.10 = (f32[224,1024]{1,0:T(8,128)S(1)}, f32[224,1024]{1,0:T(8,128)}, u32[]{:S(2)}) copy-start(f32[224,1024]{1,0:T(8,128)} %get-tuple-element.42) | copy-start | bytes 2752516
  114.9 4.3 %copy-start.9 = (f32[448,1024]{1,0:T(8,128)S(1)}, f32[448,1024]{1,0:T(8,128)}, u32[]{:S(2)}) copy-start(f32[448,1024]{1,0:T(8,128)} %copy-done.8) | copy-start | bytes 5505028
  116.2 12.9 %collective-permute-start.11 = (bf16[224,1024]{1,0:T(8,128)(2,1)S(1)}, bf16[224,1024]{1,0:T(8,128)(2,1)S(1)}, u32[]{:S(2)}, u32[]{:S(2)}) collective-permute-start(bf16[224,1024]{1,0:T(8,128)(2,1)S(1)} %add_convert_fusion), channel_id=1, source_target_pairs={{0,3},{1,0},{2,1},{3,2},{4,7},{5,4},{6,5},{7,6},{8,11},{9,8},{10,9... | collective-permute-start | bytes 1376264 | tf_op jit(solution)/shard_map/ppermute | solution.py:179
  118.6 13.9 %collective-permute-start.7 = (bf16[224,1024]{1,0:T(8,128)(2,1)S(1)}, bf16[224,1024]{1,0:T(8,128)(2,1)S(1)}, u32[]{:S(2)}, u32[]{:S(2)}) collective-permute-start(bf16[224,1024]{1,0:T(8,128)(2,1)S(1)} %add_convert_fusion.1), channel_id=1, source_target_pairs={{0,1},{1,2},{2,3},{3,0},{4,5},{5,6},{6,7},{7,4},{8,9},{9,10},{10,1... | collective-permute-start | bytes 1376264 | tf_op jit(solution)/shard_map/ppermute | solution.py:179
Sparse Core Ops, SparseCore 0:
  9.7 70.0 all-gather.1

commit v7 on v6

--- a/solution.py
+++ b/solution.py
@@ -69,7 +69,7 @@
         out[i * length:(i + 1) * length, :] = both.T.astype(BF)
 
 
-def grads_kernel(used, order, factors, tokens, cot, both, send, delta, *, rank, width, units):
+def grads_kernel(used, order, tokens, cot, both, send, *, rank, width, units):
     sequences = order.shape[1]
     length = tokens.shape[0] // sequences
     per_owner = sequences
@@ -85,10 +85,6 @@
         )
         send[place, :, 0:width] = term_a.astype(BF)
         send[place, :, width:width + units] = term_b.astype(BF)
-        up = factors[place][:, width:width + units]
-        delta[:, span] = 2.0 * lax.dot_general(
-            up, inputs, (((0,), (0,)), ((), ())), preferred_element_type=F32
-        )
 
 
 def sum_kernel(me, used, terms, grad_a, grad_b):
@@ -107,6 +103,17 @@
                 grad_b[local] += terms[group, place, :, width:width + units].astype(F32)
 
 
+def join_rows(meta, tokens, wide):
+    own, f1, b1, f2, b2, f3, b3, f4, b4 = tokens
+    width = own.shape[1]
+    first = pl.program_id(0) < pl.num_programs(0) // 2
+    for step, block in ((0, own[...]), (1, b1[...]), (2, b2[...]), (3, b3[...]),
+                        (4, jnp.where(first, f4[...], b4[...])),
+                        (5, f3[...]), (6, f2[...]), (7, f1[...])):
+        place = lax.rem(meta[2] + step, jnp.int32(8)) * width
+        wide[:, pl.ds(pl.multiple_of(place, width), width)] = block
+
+
 def times_rows(meta, got, swapped, tokens):
     span = got.shape[1]
     core = meta[1]
@@ -120,9 +127,10 @@
     return total
 
 
-def shared_kernel(meta, got2, swap2, got1, swap1, got3, swap3, tokens, *outs):
-    far_up, far_down, up_soon, down_soon, up_late, down_late = outs
+def shared_kernel(meta, got2, swap2, got1, swap1, got3, swap3, *refs):
+    far_up, far_down, up_soon, down_soon, up_late, down_late, tokens = refs[9:]
     half = far_up.shape[0]
+    join_rows(meta, refs[:9], tokens)
     far = times_rows(meta, got2, swap2, tokens)
     far_up[...] = far[:half].astype(BF)
     far_down[...] = far[half:].astype(BF)
@@ -134,23 +142,55 @@
     down_late[...] = near[half:]
 
 
-def own_kernel(meta, *refs):
-    weights, tokens, delta, out, rows = refs[:-4], *refs[-4:]
+def own_kernel(meta, used, order, *refs):
+    weights, blocks, factors = refs[:8], refs[8:17], refs[17:-4]
+    both, out, rows, tokens = refs[-4:]
     width = weights[0].shape[1]
+    units = rows.shape[0]
+    join_rows(meta, blocks, tokens)
 
     @pl.when(pl.program_id(0) == 0)
     def _():
         for block, source in enumerate(weights):
             rows[:, block * width:(block + 1) * width] = source[...]
 
-    out[...] = delta[...] + lax.dot_general(
+    base = lax.dot_general(
         rows[...], tokens[...], (((1,), (1,)), ((), ())), preferred_element_type=F32
     )
-
-
-def fetch_kernel(meta, *refs):
-    for source, out in zip(refs[:3], refs[3:]):
-        out[...] = source[...]
+    length = both.shape[0] // len(factors)
+    for k, adapter in enumerate(factors):
+        span = slice(k * length, (k + 1) * length)
+        rank = adapter.shape[1]
+        inputs = both[span, :].astype(F32).T.astype(BF)[0:rank, :]
+        delta = lax.dot_general(
+            adapter[0, :, width:width + units], inputs, (((0,), (0,)), ((), ())),
+            preferred_element_type=F32,
+        )
+        out[:, span] = base[:, span] + 2.0 * delta
+
+
+def fetch_kernel(meta, weight, *refs):
+    outs, sems = refs[:3], refs[3]
+    width = outs[0].shape[1] // 4
+    copies = []
+    for r in (1, 2, 3):
+        to = lax.rem(meta[3] + 4 - r, jnp.int32(4))
+        for i in range(4):
+            place = ((4 * meta[1] + i) * 4 + to) * width
+            copies.append(pltpu.make_async_copy(
+                weight.at[:, pl.ds(pl.multiple_of(place, width), width)],
+                outs[r - 1].at[:, i * width:(i + 1) * width],
+                sems.at[4 * (r - 1) + i],
+            ))
+    for copy in copies:
+        copy.start()
+    for copy in copies:
+        copy.wait()
+
+
+def late_kernel(up, far_up, down, far_down, out_up, out_down):
+    out_up[...] = (up[...] + far_up[...].astype(F32)).astype(BF)
+    out_down[...] = (down[...] + far_down[...].astype(F32)).astype(BF)
 
 
 def join_kernel(base, up_late, up_soon, down_soon, down_late, out):
@@ -172,6 +212,10 @@
         scratch_shapes=scratch,
         compiler_params=pltpu.CompilerParams(vmem_limit_bytes=limit * 1024 * 1024),
     )
+
+
+def in_hbm(value):
+    return pltpu.with_memory_space_constraint(value, pltpu.HBM)
 
 
 def hop(value, axis, step):
@@ -195,26 +239,19 @@
     meta = jnp.stack([x, core, z, y]).astype(jnp.int32)
     me_arr = me.reshape(1).astype(jnp.int32)
 
-    gathered = lax.all_gather(tokens, "z", axis=1, tiled=True)
+    f1, b1 = hop(tokens, "z", 1), hop(tokens, "z", -1)
 
     weight_t = weight.T
     span = n_z // 2
 
-    def block_for(r):
-        return lambda i, meta: (
-            0, (span * meta[1] + i) * n_y + lax.rem(meta[3] + n_y - r, jnp.int32(n_y))
-        )
-
+    anywhere = pl.BlockSpec(memory_space=pl.ANY)
     fetched = pl.pallas_call(
         fetch_kernel,
         out_shape=[whole((units, span * width), BF)] * 3,
-        grid_spec=pltpu.PrefetchScalarGridSpec(
-            num_scalar_prefetch=1,
-            grid=(span,),
-            in_specs=[pl.BlockSpec((units, width), block_for(r)) for r in (1, 2, 3)],
-            out_specs=[pl.BlockSpec((units, width), lambda i, meta: (0, i))] * 3,
-        ),
-    )(meta, weight_t, weight_t, weight_t)
+        in_specs=[SMEM, anywhere],
+        out_specs=[VMEM] * 3,
+        scratch_shapes=[pltpu.SemaphoreType.DMA((12,))],
+    )(meta, weight_t)
 
     down_t = jnp.transpose(down, (0, 2, 1))
     used_all = lax.all_to_all(
@@ -223,9 +260,14 @@
     picked = call(pick_kernel, whole((owners, 2, rank, packed), BF), [SMEM, SMEM, VMEM, VMEM])(
         me_arr, used_all, down_t, up
     )
-    picked, fetched = together((picked, fetched))
+    picked, fetched, f1, b1 = together((picked, fetched, f1, b1))
     pieces = tuple(hop(item, "y", -r) for r, item in zip((1, 2, 3), fetched))
     factors = lax.all_to_all(picked, DP, 0, 0, tiled=True).reshape(owners * 2, rank, packed)
+    f2, b2 = hop(f1, "z", 1), hop(b1, "z", -1)
+    factors, f2, b2 = (factors, f2, b2)
+    f3, b3 = hop(f2, "z", 1), hop(b2, "z", -1)
+    half_rows = rows // 2
+    f4, b4 = hop(f3[:half_rows], "z", 1), hop(b3[half_rows:], "z", -1)
     cot_t = cotangent.T
     sizes = dict(rank=rank, width=width, units=units)
     part = call(
@@ -236,27 +278,33 @@
     share = rows // members
     parts = lax.all_to_all(part.reshape(members, share, 2 * rank), MP, 0, 0, tiled=True)
     summed = jnp.sum(parts.astype(F32), axis=0).astype(BF)
-    summed, pieces = together((summed, pieces))
+    summed, pieces, f4, b4 = together((summed, pieces, f4, b4))
+    gathered = (tokens, f1, b1, f2, b2, f3, b3, f4, b4)
     swapped = tuple(hop(item, "core", 1) for item in pieces)
     both = lax.all_to_all(
         jnp.broadcast_to(summed[None], (members,) + summed.shape), MP, 0, 0, tiled=True
     ).reshape(rows, 2 * rank)
 
     half, step = units // 2, 256
+    steps = rows // step
     side = span * width
     narrow = pltpu.HBM((half, rows), BF)
-    part_block = pl.BlockSpec((half, step), lambda i, meta: (0, i))
-    full_block = pl.BlockSpec((units, step), lambda i, meta: (0, i))
-    token_block = pl.BlockSpec((step, n_z * width), lambda i, meta: (i, 0))
-    all_rows = pl.BlockSpec((units, side), lambda i, meta: (0, 0))
-
-    def over_tokens(kernel, outs, ins, out_specs, scratch, work=1):
+    part_block = pl.BlockSpec((half, step), lambda i, *_: (0, i))
+    full_block = pl.BlockSpec((units, step), lambda i, *_: (0, i))
+    token_block = pl.BlockSpec((step, width), lambda i, *_: (i, 0))
+    early_block = pl.BlockSpec((step, width), lambda i, *_: (jnp.minimum(i, steps // 2 - 1), 0))
+    late_block = pl.BlockSpec((step, width), lambda i, *_: (jnp.maximum(i - steps // 2, 0), 0))
+    token_blocks = [token_block] * 7 + [early_block, late_block]
+    wide = pltpu.VMEM((step, n_z * width), BF)
+    all_rows = pl.BlockSpec((units, side), lambda i, *_: (0, 0))
+
+    def over_tokens(kernel, outs, ins, out_specs, scratch, work=1, scalars=1):
         return pl.pallas_call(
             kernel,
             out_shape=outs,
             grid_spec=pltpu.PrefetchScalarGridSpec(
-                num_scalar_prefetch=1,
-                grid=(rows // step,),
+                num_scalar_prefetch=scalars,
+                grid=(steps,),
                 in_specs=ins,
                 out_specs=out_specs,
                 scratch_shapes=scratch,
@@ -271,21 +319,23 @@
     far_up, far_down, up_soon, down_soon, up_late, down_late = over_tokens(
         shared_kernel,
         [narrow] * 4 + [broad] * 2,
-        [all_rows] * 6 + [token_block],
+        [all_rows] * 6 + token_blocks,
         [part_block] * 6,
-        [],
-    )(meta, got2, swap2, got1, swap1, got3, swap3, gathered)
-    both, far_up, far_down = together((both, far_up, far_down))
+        [wide],
+    )(meta, got2, swap2, got1, swap1, got3, swap3, *gathered)
+    both = together((both, far_up, far_down))[0]
     far_up, far_down = hop(far_up, "y", 1), hop(far_down, "y", -1)
     up_soon, down_soon = hop(up_soon, "y", 1), hop(down_soon, "y", -1)
-    up_late = hop((up_late + far_up.astype(F32)).astype(BF), "y", 1)
-    down_late = hop((down_late + far_down.astype(F32)).astype(BF), "y", -1)
-
-    send, delta = call(
+    up_late, down_late = call(late_kernel, (narrow, narrow), [VMEM] * 4)(
+        in_hbm(up_late), far_up, in_hbm(down_late), far_down
+    )
+    up_late, down_late = hop(up_late, "y", 1), hop(down_late, "y", -1)
+
+    send = call(
         functools.partial(grads_kernel, **sizes),
-        (whole((owners * 2, rank, packed), BF), whole((units, rows), F32)),
-        [SMEM, SMEM, VMEM, VMEM, VMEM, VMEM],
-    )(used, order, factors, tokens, cot_t, both)
+        pltpu.HBM((owners * 2, rank, packed), BF),
+        [SMEM, SMEM, VMEM, VMEM, VMEM],
+    )(used, order, tokens, cot_t, both)
     terms = lax.all_to_all(send.reshape(owners, 2, rank, packed), DP, 0, 0, tiled=True)
     grad_a, grad_b = call(
         sum_kernel,
@@ -294,18 +344,30 @@
     )(me_arr, used_all, terms)
 
     def own_block(block):
-        return pl.BlockSpec((units, width), lambda i, meta: (0, block * n_y + meta[3]))
+        return pl.BlockSpec((units, width), lambda i, meta, *_: (0, block * n_y + meta[3]))
+
+    slots = used.shape[1]
+    together_in_step = step * order.shape[1] // rows
+
+    def adapter_block(k):
+        return pl.BlockSpec((1, rank, packed), lambda i, meta, used, order: (
+            place_of(used, order, together_in_step * i + k, per_owner, slots), 0, 0
+        ))
 
     base = over_tokens(
         own_kernel,
         whole((units, rows), F32),
-        [own_block(block) for block in range(n_z)] + [token_block, full_block],
+        [own_block(block) for block in range(n_z)] + token_blocks
+        + [adapter_block(k) for k in range(together_in_step)]
+        + [pl.BlockSpec((step, 2 * rank), lambda i, *_: (i, 0))],
         full_block,
-        [pltpu.VMEM((units, n_z * width), BF)],
+        [pltpu.VMEM((units, n_z * width), BF), wide],
         work=20_000_000_000,
-    )(meta, *[weight_t] * n_z, gathered, delta)
+        scalars=3,
+    )(meta, used, order, *[weight_t] * n_z, *gathered, *[factors] * together_in_step, both)
+    base, grad_a, grad_b = together((base, grad_a, grad_b))
     out = call(join_kernel, whole((units, rows), BF), [VMEM] * 5)(
-        base, up_late, up_soon, down_soon, down_late
+        in_hbm(base), up_late, up_soon, down_soon, down_late
     )
     return out.T, jnp.transpose(grad_a, (0, 2, 1)), grad_b
 

time: 145 us -> 138 us (0.952)
  blocking collectives: 26.5 us -> 0 us
  starting transfers between devices: 37.9 us -> 56.9 us
  between operations: 14.2 us -> 0.86 us
  Pallas kernels: 30.1 us -> 37.9 us
  waiting for transfers between devices: 28.4 us -> 32.6 us
  local copies, waits for them, and re-layouts: 4.45 us -> 6.95 us
    all_to_all x1 -> x0, blocking collectives: 26.5 us -> none  [on_device(): lax.all_to_all(part.reshape(members, share, 2 * rank), MP, 0, 0, tiled=True)]
    ppermute x12 -> x20, starting transfers between devices: 10.3 us -> 26.7 us  [hop(): return lax.ppermute(value, axis, [(i, (i + step) % n) for i in range(n)])]
    all_to_all x0 -> x1, waiting for transfers between devices: none -> 14.6 us  [on_device(): lax.all_to_all(part.reshape(members, share, 2 * rank), MP, 0, 0, tiled=True)]
    all_to_all x1, waiting for transfers between devices: 17.7 us -> 4.35 us  [on_device(): lax.all_to_all(picked, DP, 0, 0, tiled=True)]
    all_to_all x0 -> x1, starting transfers between devices: none -> 8.65 us  [on_device(): lax.all_to_all(part.reshape(members, share, 2 * rank), MP, 0, 0, tiled=True)]
    pallas_call x2 -> x3, Pallas kernels: 12.3 us -> 17.2 us  [the longest x1 11.6 us: on_device(): over_tokens(shared_kernel, [narrow] * 4 + [broad] * 2, [all_rows] * 6 + t...]
    all_to_all x1, waiting for transfers between devices: 1.89 us -> 4.76 us  [on_device(): lax.all_to_all(send.reshape(owners, 2, rank, packed), DP, 0, 0, tiled=True)]
    all_to_all x1, starting transfers between devices: 8.66 us -> 6.02 us  [on_device(): lax.all_to_all(jnp.broadcast_to(summed[None], (members,) + summed.shape),...]
  transfers between devices with their start and end apart: 17 -> 25, of which waited for: 5 -> 5; matrix products, arithmetic and copies ran while one was open for 4% -> 5% of each run, Pallas kernels for 19% -> 25%
where the time goes in v7:
time: 138 us; the launch traced here: 137 us
  starting transfers between devices  56.9 us (41%)
  Pallas kernels  37.9 us (27%)
  waiting for transfers between devices  32.6 us (24%)
  local copies, waits for them, and re-layouts  6.95 us (5%)
  other arithmetic  2.19 us (2%)
    ppermute x20, starting transfers between devices, hop(): return lax.ppermute(value, axis, [(i, (i + step) % n) for i in range(n)])  26.7 us
    all_to_all x1, waiting for transfers between devices, on_device(): lax.all_to_all(part.reshape(members, share, 2 * rank), MP, 0, 0, tiled=True)  14.6 us
    pallas_call x1, Pallas kernels, on_device(): over_tokens(shared_kernel, [narrow] * 4 + [broad] * 2, [all_rows] * 6 + t...  11.6 us
    ppermute x20, waiting for transfers between devices, hop(): return lax.ppermute(value, axis, [(i, (i + step) % n) for i in range(n)])  8.9 us
    all_to_all x1, starting transfers between devices, on_device(): lax.all_to_all(part.reshape(members, share, 2 * rank), MP, 0, 0, tiled=True)  8.65 us
    pallas_call x1, Pallas kernels, on_device(): over_tokens(own_kernel, whole((units, rows), F32), [own_block(block) for...  7.74 us
    all_to_all x1, starting transfers between devices, on_device(): lax.all_to_all(jnp.broadcast_to(summed[None], (members,) + summed.shape),...  6.02 us
    all_to_all x1, starting transfers between devices, on_device(): lax.all_to_all(send.reshape(owners, 2, rank, packed), DP, 0, 0, tiled=True)  5.35 us
  transfers between devices with their start and end apart: 25, of which 5 were waited for; matrix products, arithmetic and copies ran while one was open for 5% of the time, Pallas kernels for 25%

profile of v7, /device:TPU:1, one launch (start us, length us, event | category | flops | bytes accessed | tf_op | source)
XLA Modules:
  0.0 137.5 jit_solution(14253226965151275472)
XLA Ops:
  0.6 2.5 %collective-permute-start = (bf16[1024,256]{1,0:T(8,128)(2,1)}, bf16[1024,256]{1,0:T(8,128)(2,1)}, u32[]{:S(2)}, u32[]{:S(2)}) collective-permute-start(bf16[1024,256]{1,0:T(8,128)(2,1)} %tokens.3), channel_id=1, source_target_pairs={{0,4},{4,8},{8,12},{12,16},{16,20},{20,24},{24,28},{28,0},{1,5},{5... | collective-permute-start | bytes 1572872 | tf_op jit(solution)/shard_map/ppermute | solution.py:223
  3.2 4.0 %collective-permute-start.1 = (bf16[1024,256]{1,0:T(8,128)(2,1)}, bf16[1024,256]{1,0:T(8,128)(2,1)S(1)}, u32[]{:S(2)}, u32[]{:S(2)}) collective-permute-start(bf16[1024,256]{1,0:T(8,128)(2,1)} %tokens.3), channel_id=1, source_target_pairs={{0,28},{4,0},{8,4},{12,8},{16,12},{20,16},{24,20},{28,24},{1,29},{... | collective-permute-start | bytes 1572872 | tf_op jit(solution)/shard_map/ppermute | solution.py:223
  7.2 1.2 broadcast_in_dim.7
  8.5 5.3 %all-to-all-start = ((s32[8,1,8]{2,1,0:T(1,128)}), s32[8,1,8]{2,1,0:T(1,128)S(1)}, u32[]{:S(2)}, u32[]{:S(2)}) async-start(s32[8,1,8]{2,1,0:T(1,128)} %broadcast_in_dim.7), calls=%async_computation | async-start | bytes 8192 | tf_op jit(solution)/shard_map/all_to_all | solution.py:257
  13.7 0.6 pad_add_fusion.meta
  14.3 4.4 %shard_map.95 = (bf16[448,1024]{1,0:T(8,128)(2,1)}, bf16[448,1024]{1,0:T(8,128)(2,1)}, bf16[448,1024]{1,0:T(8,128)(2,1)}) custom-call(s32[4]{0:T(128)} %pad_add_fusion.meta, bf16[448,8192]{1,0:T(8,128)(2,1)} %bitcast.26), custom_call_target="tpu_custom_call" | custom-call | tf_op jit(solution)/shard_map/pallas_call | solution.py:248
  18.7 2.1 %shard_map.94 = bf16[8,2,64,768]{3,2,1,0:T(8,128)(2,1)} custom-call(s32[1]{0:T(128)} %bitcast.5.me, s32[8,8]{1,0:T(8,128)S(1)} %bitcast.23, bf16[8,64,256]{2,1,0:T(8,128)(2,1)S(1)} %bitcast.22, bf16[8,64,448]{2,1,0:T(8,128)(2,1)S(1)} %copy-done.9), custom_call_target="tpu_custom_call" | custom-call | tf_op jit(solution)/shard_map/pallas_call | solution.py:260
  20.8 0.0 collective-permute-done.refs_1_.refs_9_
  20.8 0.0 collective-permute-done.1.refs_2_.refs_10_
  20.8 0.0 copy-start
  20.9 0.0 copy-start.2
  20.9 0.0 copy-start.11
  20.9 0.0 copy-start.13
  20.9 4.9 %all-to-all-start.1 = ((bf16[8,2,64,768]{3,2,1,0:T(8,128)(2,1)}), bf16[8,2,64,768]{3,2,1,0:T(8,128)(2,1)S(1)}, u32[]{:S(2)}, u32[]{:S(2)}) async-start(bf16[8,2,64,768]{3,2,1,0:T(8,128)(2,1)} %shard_map.94), calls=%async_computation.1 | async-start | bytes 3145728 | tf_op jit(solution)/shard_map/all_to_all | solution.py:265
  25.8 1.7 %collective-permute-start.3 = (bf16[1024,256]{1,0:T(8,128)(2,1)S(1)}, bf16[1024,256]{1,0:T(8,128)(2,1)}, u32[]{:S(2)}, u32[]{:S(2)}) collective-permute-start(bf16[1024,256]{1,0:T(8,128)(2,1)S(1)} %collective-permute-done.1.refs_2_.refs_10_), channel_id=1, source_target_pairs={{0,28},{4,0},{8,4},{12,8},{16,12},{20,16},{24,20},{28,24},{1,29},{... | collective-permute-start | bytes 1572872 | tf_op jit(solution)/shard_map/ppermute | solution.py:223
  27.5 2.7 %collective-permute-start.6 = (bf16[448,1024]{1,0:T(8,128)(2,1)}, bf16[448,1024]{1,0:T(8,128)(2,1)}, u32[]{:S(2)}, u32[]{:S(2)}) collective-permute-start(bf16[448,1024]{1,0:T(8,128)(2,1)} %get-tuple-element.38), channel_id=1, source_target_pairs={{0,3},{1,0},{2,1},{3,2},{4,7},{5,4},{6,5},{7,6},{8,11},{9,8},{10,9... | collective-permute-start | bytes 2752520 | tf_op jit(solution)/shard_map/ppermute | solution.py:223
  30.2 0.3 collective-permute-start.7
  30.6 0.7 collective-permute-start.8
  31.3 8.2 %collective-permute-done.3.refs_4_.refs_12_ = bf16[1024,256]{1,0:T(8,128)(2,1)} collective-permute-done((bf16[1024,256]{1,0:T(8,128)(2,1)S(1)}, bf16[1024,256]{1,0:T(8,128)(2,1)}, u32[]{:S(2)}, u32[]{:S(2)}) %collective-permute-start.3) | collective-permute-done | bytes 524320 | tf_op jit(solution)/shard_map/ppermute | solution.py:223
  39.4 2.9 %collective-permute-start.5 = (bf16[1024,256]{1,0:T(8,128)(2,1)}, bf16[1024,256]{1,0:T(8,128)(2,1)S(1)}, u32[]{:S(2)}, u32[]{:S(2)}) collective-permute-start(bf16[1024,256]{1,0:T(8,128)(2,1)} %collective-permute-done.3.refs_4_.refs_12_), channel_id=1, source_target_pairs={{0,28},{4,0},{8,4},{12,8},{16,12},{20,16},{24,20},{28,24},{1,29},{... | collective-permute-start | bytes 1572872 | tf_op jit(solution)/shard_map/ppermute | solution.py:223
  42.3 0.0 collective-permute-done.2.refs_3_.refs_11_
  42.3 0.0 collective-permute-start.4
  42.3 4.4 %all-to-all-done.1 = bf16[8,2,64,768]{3,2,1,0:T(8,128)(2,1)S(1)} async-done(((bf16[8,2,64,768]{3,2,1,0:T(8,128)(2,1)}), bf16[8,2,64,768]{3,2,1,0:T(8,128)(2,1)S(1)}, u32[]{:S(2)}, u32[]{:S(2)}) %all-to-all-start.1) | async-done | bytes 1572896 | tf_op jit(solution)/shard_map/all_to_all | solution.py:265
  46.7 1.1 shard_map.96
  47.8 0.7 copy-done.5
  48.6 8.6 %all-to-all-start.2 = ((bf16[32,32,128]{2,1,0:T(8,128)(2,1)}), bf16[32,32,128]{2,1,0:T(8,128)(2,1)}, u32[]{:S(2)}, u32[]{:S(2)}) async-start(bf16[32,32,128]{2,1,0:T(8,128)(2,1)} %bitcast.21), calls=%async_computation.2 | async-start | bytes 524288 | tf_op jit(solution)/shard_map/all_to_all | solution.py:279
  57.2 0.8 slice.9
  58.0 2.4 %collective-permute-start.10 = (bf16[512,256]{1,0:T(8,128)(2,1)}, bf16[512,256]{1,0:T(8,128)(2,1)}, u32[]{:S(2)}, u32[]{:S(2)}) collective-permute-start(bf16[512,256]{1,0:T(8,128)(2,1)} %slice.9), channel_id=1, source_target_pairs={{0,28},{4,0},{8,4},{12,8},{16,12},{20,16},{24,20},{28,24},{1,29},{... | collective-permute-start | bytes 786440 | tf_op jit(solution)/shard_map/ppermute | solution.py:223
  60.4 0.0 collective-permute-done.4.refs_5_.refs_13_
  60.4 1.7 %slice.8 = bf16[512,256]{1,0:T(8,128)(2,1)} slice(bf16[1024,256]{1,0:T(8,128)(2,1)} %collective-permute-done.4.refs_5_.refs_13_), slice={[0:512], [0:256]} | slice | bytes 524288 | tf_op jit(solution)/shard_map/slice | solution.py:270
  62.1 0.0 collective-permute-start.9
  62.1 14.6 %all-to-all-done.2 = bf16[32,32,128]{2,1,0:T(8,128)(2,1)} async-done(((bf16[32,32,128]{2,1,0:T(8,128)(2,1)}), bf16[32,32,128]{2,1,0:T(8,128)(2,1)}, u32[]{:S(2)}, u32[]{:S(2)}) %all-to-all-start.2) | async-done | bytes 262176 | tf_op jit(solution)/shard_map/all_to_all | solution.py:279
  76.7 1.6 %reduce_sum.12 = bf16[32,128]{1,0:T(8,128)(2,1)} reduce(bf16[32,32,128]{2,1,0:T(8,128)(2,1)} %all-to-all-done.2, bf16[]{:T(256)} %constant.23.clone.1), dimensions={0}, to_apply=%region_0.0 | reduce | flops 126976 | bytes 270338 | tf_op jit(solution)/shard_map/reduce_sum | solution.py:280
  78.3 0.0 collective-permute-done.6.got1
  78.3 0.0 collective-permute-done.7.got2
  78.3 0.0 collective-permute-done.8.got3
  78.3 0.0 collective-permute-done.10.refs_8_.refs_16_
  78.3 0.7 collective-permute-start.11
  79.1 0.1 collective-permute-start.12
  79.2 0.4 collective-permute-start.13
  79.6 1.4 %broadcast_in_dim.16 = bf16[32,32,128]{2,1,0:T(8,128)(2,1)} broadcast(bf16[32,128]{1,0:T(8,128)(2,1)} %reduce_sum.12), dimensions={1,2} | broadcast | bytes 270336 | tf_op jit(solution)/shard_map/broadcast_in_dim | solution.py:285
  81.0 6.0 %all-to-all-start.3 = ((bf16[32,32,128]{2,1,0:T(8,128)(2,1)}), bf16[32,32,128]{2,1,0:T(8,128)(2,1)}, u32[]{:S(2)}, u32[]{:S(2)}) async-start(bf16[32,32,128]{2,1,0:T(8,128)(2,1)} %broadcast_in_dim.16), calls=%async_computation.3 | async-start | bytes 524288 | tf_op jit(solution)/shard_map/all_to_all | solution.py:284
  87.0 0.0 collective-permute-done.11.swap2
  87.1 0.0 collective-permute-done.12.swap1
  87.1 0.0 copy-start.7
  87.1 1.0 copy-done.7
  88.1 11.6 %shard_map.97 = (bf16[224,1024]{1,0:T(8,128)(2,1)}, bf16[224,1024]{1,0:T(8,128)(2,1)}, bf16[224,1024]{1,0:T(8,128)(2,1)}, bf16[224,1024]{1,0:T(8,128)(2,1)}, f32[224,1024]{1,0:T(8,128)}, /*index=5*/f32[224,1024]{1,0:T(8,128)}) custom-call(s32[4]{0:T(128)S(1)} %copy-done.12, bf16[448,1024]{1,0:T(8,128)(2,1)} %collective-permute-done.7.got2, ...), custom_call_target="tpu_custom_call" | custom-call | flops 1 | bytes 1 | tf_op jit(solution)/shard_map/pallas_call | solution.py:319
  99.8 1.2 collective-permute-start.14
  101.0 1.5 %collective-permute-start.15 = (bf16[224,1024]{1,0:T(8,128)(2,1)}, bf16[224,1024]{1,0:T(8,128)(2,1)}, u32[]{:S(2)}, u32[]{:S(2)}) collective-permute-start(bf16[224,1024]{1,0:T(8,128)(2,1)} %get-tuple-element.48), channel_id=1, source_target_pairs={{0,3},{1,0},{2,1},{3,2},{4,7},{5,4},{6,5},{7,6},{8,11},{9,8},{10,9... | collective-permute-start | bytes 1376264 | tf_op jit(solution)/shard_map/ppermute | solution.py:223
  102.5 0.0 all-to-all-done.3
  102.5 2.8 %shard_map.99 = bf16[16,64,768]{2,1,0:T(8,128)(2,1)} custom-call(s32[1,8]{1,0:T(1,128)S(1)} %copy-done.11, s32[1,8]{1,0:T(1,128)S(1)} %copy-done.13, bf16[1024,256]{1,0:T(8,128)(2,1)S(1)} %copy-done, bf16[448,1024]{1,0:T(8,128)(2,1)S(1)} %bitcast.20, bf16[1024,128]{1,0:T(8,128)(2,1)} %bitcast.12.refs_19_.both), custom_call_target="tpu_custom_call" | custom-call | tf_op jit(solution)/shard_map/pallas_call | solution.py:334
  105.4 5.3 %all-to-all-start.4 = ((bf16[8,2,64,768]{3,2,1,0:T(8,128)(2,1)}), bf16[8,2,64,768]{3,2,1,0:T(8,128)(2,1)S(1)}, u32[]{:S(2)}, u32[]{:S(2)}) async-start(bf16[8,2,64,768]{3,2,1,0:T(8,128)(2,1)} %bitcast.35), calls=%async_computation.4 | async-start | bytes 3145728 | tf_op jit(solution)/shard_map/all_to_all | solution.py:339
  110.7 0.3 collective-permute-start.17
  111.0 2.4 %collective-permute-start.18 = (bf16[224,1024]{1,0:T(8,128)(2,1)}, bf16[224,1024]{1,0:T(8,128)(2,1)}, u32[]{:S(2)}, u32[]{:S(2)}) collective-permute-start(bf16[224,1024]{1,0:T(8,128)(2,1)} %get-tuple-element.57), channel_id=1, source_target_pairs={{0,3},{1,0},{2,1},{3,2},{4,7},{5,4},{6,5},{7,6},{8,11},{9,8},{10,9... | collective-permute-start | bytes 1376264 | tf_op jit(solution)/shard_map/ppermute | solution.py:223
  113.5 0.0 collective-permute-done.14.far_up
  113.5 0.0 collective-permute-done.15.far_down
  113.5 2.8 %shard_map.101 = (bf16[224,1024]{1,0:T(8,128)(2,1)}, bf16[224,1024]{1,0:T(8,128)(2,1)}) custom-call(f32[224,1024]{1,0:T(8,128)} %get-tuple-element.53.up, bf16[224,1024]{1,0:T(8,128)(2,1)} %collective-permute-done.14.far_up, f32[224,1024]{1,0:T(8,128)} %get-tuple-element.54.down, bf16[224,1024]{1,0:T(8,128)(2,1)} %collective-permute-done.15.far_down), custom_call_target="tpu_custom_call" | custom-call | tf_op jit(solution)/shard_map/pallas_call | solution.py:329
  116.2 0.1 collective-permute-start.16
  116.4 2.6 %collective-permute-start.19 = (bf16[224,1024]{1,0:T(8,128)(2,1)}, bf16[224,1024]{1,0:T(8,128)(2,1)}, u32[]{:S(2)}, u32[]{:S(2)}) collective-permute-start(bf16[224,1024]{1,0:T(8,128)(2,1)} %get-tuple-element.58), channel_id=1, source_target_pairs={{0,3},{1,0},{2,1},{3,2},{4,7},{5,4},{6,5},{7,6},{8,11},{9,8},{10,9... | collective-permute-start | bytes 1376264 | tf_op jit(solution)/shard_map/ppermute | solution.py:223
  118.9 7.7 %shard_map.98.base = f32[448,1024]{1,0:T(8,128)} custom-call(s32[4]{0:T(128)S(1)} %copy-done.12, s32[1,8]{1,0:T(1,128)S(1)} %copy-done.11, s32[1,8]{1,0:T(1,128)S(1)} %copy-done.13, bf16[448,8192]{1,0:T(8,128)(2,1)} %bitcast.27, bf16[448,8192]{1,0:T(8,128)(2,1)} %bitcast.28, bf16[448,8192]{1,0:T(8,128)(2,1)} %bitcast.29, bf16[448,8192]{1,0:T(8,128)(2,1)} %bitcast.30, ...), custom_call_target="tpu_custom_call" | custom-call | flops 20000000000 | bytes 20000000000 | tf_op jit(solution)/shard_map/pallas_call | solution.py:357
  126.7 4.8 %all-to-all-done.4.terms = bf16[8,2,64,768]{3,2,1,0:T(8,128)(2,1)S(1)} async-done(((bf16[8,2,64,768]{3,2,1,0:T(8,128)(2,1)}), bf16[8,2,64,768]{3,2,1,0:T(8,128)(2,1)S(1)}, u32[]{:S(2)}, u32[]{:S(2)}) %all-to-all-start.4) | async-done | bytes 1572896 | tf_op jit(solution)/shard_map/all_to_all | solution.py:339
  131.4 2.1 %shard_map.100 = (f32[8,64,256]{2,1,0:T(8,128)}, f32[8,64,448]{2,1,0:T(8,128)}) custom-call(s32[1]{0:T(128)} %bitcast.5.me, s32[8,8]{1,0:T(8,128)S(1)} %bitcast.24, bf16[8,2,64,768]{3,2,1,0:T(8,128)(2,1)S(1)} %all-to-all-done.4.terms), custom_call_target="tpu_custom_call" | custom-call | tf_op jit(solution)/shard_map/pallas_call | solution.py:340
  133.6 0.7 collective-permute-done.16.up_late
  134.3 3.2 %shard_map.102 = bf16[448,1024]{1,0:T(8,128)(2,1)} custom-call(f32[448,1024]{1,0:T(8,128)} %shard_map.98.base, bf16[224,1024]{1,0:T(8,128)(2,1)} %collective-permute-done.16.up_late, bf16[224,1024]{1,0:T(8,128)(2,1)} %collective-permute-done.17.up_soon, bf16[224,1024]{1,0:T(8,128)(2,1)} %collective-permute-done.18.down_soon, ...), custom_call_target="tpu_custom_call" | custom-call | tf_op jit(solution)/shard_map/pallas_call | solution.py:369
  (29 shorter events, 0.1 us)
Async XLA Ops:
  0.6 20.2 %collective-permute-start = (bf16[1024,256]{1,0:T(8,128)(2,1)}, bf16[1024,256]{1,0:T(8,128)(2,1)}, u32[]{:S(2)}, u32[]{:S(2)}) collective-permute-start(bf16[1024,256]{1,0:T(8,128)(2,1)} %tokens.3), channel_id=1, source_target_pairs={{0,4},{4,8},{8,12},{12,16},{16,20},{20,24},{24,28},{28,0},{1,5},{5... | collective-permute-start | bytes 1572872 | tf_op jit(solution)/shard_map/ppermute | solution.py:223
  3.2 17.7 %collective-permute-start.1 = (bf16[1024,256]{1,0:T(8,128)(2,1)}, bf16[1024,256]{1,0:T(8,128)(2,1)S(1)}, u32[]{:S(2)}, u32[]{:S(2)}) collective-permute-start(bf16[1024,256]{1,0:T(8,128)(2,1)} %tokens.3), channel_id=1, source_target_pairs={{0,28},{4,0},{8,4},{12,8},{16,12},{20,16},{24,20},{28,24},{1,29},{... | collective-permute-start | bytes 1572872 | tf_op jit(solution)/shard_map/ppermute | solution.py:223
  8.5 10.2 %all-to-all-start = ((s32[8,1,8]{2,1,0:T(1,128)}), s32[8,1,8]{2,1,0:T(1,128)S(1)}, u32[]{:S(2)}, u32[]{:S(2)}) async-start(s32[8,1,8]{2,1,0:T(1,128)} %broadcast_in_dim.7), calls=%async_computation | async-start | bytes 8192 | tf_op jit(solution)/shard_map/all_to_all | solution.py:257
  14.3 4.4 %copy-start.9 = (bf16[8,64,448]{2,1,0:T(8,128)(2,1)S(1)}, bf16[8,64,448]{2,1,0:T(8,128)(2,1)}, u32[]{:S(2)}) copy-start(bf16[8,64,448]{2,1,0:T(8,128)(2,1)} %up.1) | copy-start | bytes 1376260
  14.3 4.4 %copy-start.10 = (bf16[8,256,64]{1,2,0:T(8,128)(2,1)S(1)}, bf16[8,256,64]{1,2,0:T(8,128)(2,1)}, u32[]{:S(2)}) copy-start(bf16[8,256,64]{1,2,0:T(8,128)(2,1)} %param.10) | copy-start | bytes 786436
  20.8 5.0 %copy-start.6 = (bf16[1024,256]{1,0:T(8,128)(2,1)}, bf16[1024,256]{1,0:T(8,128)(2,1)S(1)}, u32[]{:S(2)}) copy-start(bf16[1024,256]{1,0:T(8,128)(2,1)S(1)} %collective-permute-done.1.refs_2_.refs_10_) | copy-start | bytes 1572868
  20.8 25.8 %copy-start = (bf16[1024,256]{1,0:T(8,128)(2,1)S(1)}, bf16[1024,256]{1,0:T(8,128)(2,1)}, u32[]{:S(2)}) copy-start(bf16[1024,256]{1,0:T(8,128)(2,1)} %tokens.3) | copy-start | bytes 1572868
  20.9 25.8 %copy-start.2 = (bf16[1024,448]{0,1:T(8,128)(2,1)S(1)}, bf16[1024,448]{0,1:T(8,128)(2,1)}, u32[]{:S(2)}) copy-start(bf16[1024,448]{0,1:T(8,128)(2,1)} %param.8) | copy-start | bytes 2752516
  20.9 25.8 %copy-start.11 = (s32[1,8]{1,0:T(1,128)S(1)}, s32[1,8]{1,0:T(1,128)}, u32[]{:S(2)}) copy-start(s32[1,8]{1,0:T(1,128)} %used.5) | copy-start | bytes 100
  20.9 25.8 %copy-start.13 = (s32[1,8]{1,0:T(1,128)S(1)}, s32[1,8]{1,0:T(1,128)}, u32[]{:S(2)}) copy-start(s32[1,8]{1,0:T(1,128)} %order.5) | copy-start | bytes 100
  20.9 25.8 %all-to-all-start.1 = ((bf16[8,2,64,768]{3,2,1,0:T(8,128)(2,1)}), bf16[8,2,64,768]{3,2,1,0:T(8,128)(2,1)S(1)}, u32[]{:S(2)}, u32[]{:S(2)}) async-start(bf16[8,2,64,768]{3,2,1,0:T(8,128)(2,1)} %shard_map.94), calls=%async_computation.1 | async-start | bytes 3145728 | tf_op jit(solution)/shard_map/all_to_all | solution.py:265
  25.8 13.6 %collective-permute-start.3 = (bf16[1024,256]{1,0:T(8,128)(2,1)S(1)}, bf16[1024,256]{1,0:T(8,128)(2,1)}, u32[]{:S(2)}, u32[]{:S(2)}) collective-permute-start(bf16[1024,256]{1,0:T(8,128)(2,1)S(1)} %collective-permute-done.1.refs_2_.refs_10_), channel_id=1, source_target_pairs={{0,28},{4,0},{8,4},{12,8},{16,12},{20,16},{24,20},{28,24},{1,29},{... | collective-permute-start | bytes 1572872 | tf_op jit(solution)/shard_map/ppermute | solution.py:223
  27.5 14.8 %collective-permute-start.2 = (bf16[1024,256]{1,0:T(8,128)(2,1)}, bf16[1024,256]{1,0:T(8,128)(2,1)}, u32[]{:S(2)}, u32[]{:S(2)}) collective-permute-start(bf16[1024,256]{1,0:T(8,128)(2,1)} %collective-permute-done.refs_1_.refs_9_), channel_id=1, source_target_pairs={{0,4},{4,8},{8,12},{12,16},{16,20},{20,24},{24,28},{28,0},{1,5},{5... | collective-permute-start | bytes 1572872 | tf_op jit(solution)/shard_map/ppermute | solution.py:223
  27.5 50.8 %collective-permute-start.6 = (bf16[448,1024]{1,0:T(8,128)(2,1)}, bf16[448,1024]{1,0:T(8,128)(2,1)}, u32[]{:S(2)}, u32[]{:S(2)}) collective-permute-start(bf16[448,1024]{1,0:T(8,128)(2,1)} %get-tuple-element.38), channel_id=1, source_target_pairs={{0,3},{1,0},{2,1},{3,2},{4,7},{5,4},{6,5},{7,6},{8,11},{9,8},{10,9... | collective-permute-start | bytes 2752520 | tf_op jit(solution)/shard_map/ppermute | solution.py:223
  30.2 48.1 %collective-permute-start.7 = (bf16[448,1024]{1,0:T(8,128)(2,1)}, bf16[448,1024]{1,0:T(8,128)(2,1)}, u32[]{:S(2)}, u32[]{:S(2)}) collective-permute-start(bf16[448,1024]{1,0:T(8,128)(2,1)} %get-tuple-element.39), channel_id=1, source_target_pairs={{0,2},{1,3},{2,0},{3,1},{4,6},{5,7},{6,4},{7,5},{8,10},{9,11},{10,... | collective-permute-start | bytes 2752520 | tf_op jit(solution)/shard_map/ppermute | solution.py:223
  30.6 47.7 %collective-permute-start.8 = (bf16[448,1024]{1,0:T(8,128)(2,1)}, bf16[448,1024]{1,0:T(8,128)(2,1)}, u32[]{:S(2)}, u32[]{:S(2)}) collective-permute-start(bf16[448,1024]{1,0:T(8,128)(2,1)} %get-tuple-element.40), channel_id=1, source_target_pairs={{0,1},{1,2},{2,3},{3,0},{4,5},{5,6},{6,7},{7,4},{8,9},{9,10},{10,1... | collective-permute-start | bytes 2752520 | tf_op jit(solution)/shard_map/ppermute | solution.py:223
  39.4 17.8 %collective-permute-start.5 = (bf16[1024,256]{1,0:T(8,128)(2,1)}, bf16[1024,256]{1,0:T(8,128)(2,1)S(1)}, u32[]{:S(2)}, u32[]{:S(2)}) collective-permute-start(bf16[1024,256]{1,0:T(8,128)(2,1)} %collective-permute-done.3.refs_4_.refs_12_), channel_id=1, source_target_pairs={{0,28},{4,0},{8,4},{12,8},{16,12},{20,16},{24,20},{28,24},{1,29},{... | collective-permute-start | bytes 1572872 | tf_op jit(solution)/shard_map/ppermute | solution.py:223
  42.3 18.1 %collective-permute-start.4 = (bf16[1024,256]{1,0:T(8,128)(2,1)}, bf16[1024,256]{1,0:T(8,128)(2,1)}, u32[]{:S(2)}, u32[]{:S(2)}) collective-permute-start(bf16[1024,256]{1,0:T(8,128)(2,1)} %collective-permute-done.2.refs_3_.refs_11_), channel_id=1, source_target_pairs={{0,4},{4,8},{8,12},{12,16},{16,20},{20,24},{24,28},{28,0},{1,5},{5... | collective-permute-start | bytes 1572872 | tf_op jit(solution)/shard_map/ppermute | solution.py:223
  47.8 0.7 copy-start.5
  48.6 38.5 %copy-start.12 = (s32[4]{0:T(128)S(1)}, s32[4]{0:T(128)}, u32[]{:S(2)}) copy-start(s32[4]{0:T(128)} %pad_add_fusion.meta) | copy-start | bytes 52
  48.6 28.2 %all-to-all-start.2 = ((bf16[32,32,128]{2,1,0:T(8,128)(2,1)}), bf16[32,32,128]{2,1,0:T(8,128)(2,1)}, u32[]{:S(2)}, u32[]{:S(2)}) async-start(bf16[32,32,128]{2,1,0:T(8,128)(2,1)} %bitcast.21), calls=%async_computation.2 | async-start | bytes 524288 | tf_op jit(solution)/shard_map/all_to_all | solution.py:279
  57.2 42.5 %copy-start.3 = (bf16[1024,256]{1,0:T(8,128)(2,1)}, bf16[1024,256]{1,0:T(8,128)(2,1)S(1)}, u32[]{:S(2)}) copy-start(bf16[1024,256]{1,0:T(8,128)(2,1)S(1)} %collective-permute-done.5.refs_6_.refs_14_) | copy-start | bytes 1572868
  58.0 20.3 %collective-permute-start.10 = (bf16[512,256]{1,0:T(8,128)(2,1)}, bf16[512,256]{1,0:T(8,128)(2,1)}, u32[]{:S(2)}, u32[]{:S(2)}) collective-permute-start(bf16[512,256]{1,0:T(8,128)(2,1)} %slice.9), channel_id=1, source_target_pairs={{0,28},{4,0},{8,4},{12,8},{16,12},{20,16},{24,20},{28,24},{1,29},{... | collective-permute-start | bytes 786440 | tf_op jit(solution)/shard_map/ppermute | solution.py:223
  62.1 16.2 %collective-permute-start.9 = (bf16[512,256]{1,0:T(8,128)(2,1)}, bf16[512,256]{1,0:T(8,128)(2,1)}, u32[]{:S(2)}, u32[]{:S(2)}) collective-permute-start(bf16[512,256]{1,0:T(8,128)(2,1)} %slice.8), channel_id=1, source_target_pairs={{0,4},{4,8},{8,12},{12,16},{16,20},{20,24},{24,28},{28,0},{1,5},{5... | collective-permute-start | bytes 786440 | tf_op jit(solution)/shard_map/ppermute | solution.py:223
  78.3 8.7 %collective-permute-start.11 = (bf16[448,1024]{1,0:T(8,128)(2,1)}, bf16[448,1024]{1,0:T(8,128)(2,1)}, u32[]{:S(2)}, u32[]{:S(2)}) collective-permute-start(bf16[448,1024]{1,0:T(8,128)(2,1)} %collective-permute-done.7.got2), channel_id=1, source_target_pairs={{0,32},{32,0},{1,33},{33,1},{2,34},{34,2},{3,35},{35,3},{4,36},{36... | collective-permute-start | bytes 2752520 | tf_op jit(solution)/shard_map/ppermute | solution.py:223
  79.1 8.0 %collective-permute-start.12 = (bf16[448,1024]{1,0:T(8,128)(2,1)}, bf16[448,1024]{1,0:T(8,128)(2,1)}, u32[]{:S(2)}, u32[]{:S(2)}) collective-permute-start(bf16[448,1024]{1,0:T(8,128)(2,1)} %collective-permute-done.6.got1), channel_id=1, source_target_pairs={{0,32},{32,0},{1,33},{33,1},{2,34},{34,2},{3,35},{35,3},{4,36},{36... | collective-permute-start | bytes 2752520 | tf_op jit(solution)/shard_map/ppermute | solution.py:223
  79.2 7.9 %collective-permute-start.13 = (bf16[448,1024]{1,0:T(8,128)(2,1)}, bf16[448,1024]{1,0:T(8,128)(2,1)}, u32[]{:S(2)}, u32[]{:S(2)}) collective-permute-start(bf16[448,1024]{1,0:T(8,128)(2,1)} %collective-permute-done.8.got3), channel_id=1, source_target_pairs={{0,32},{32,0},{1,33},{33,1},{2,34},{34,2},{3,35},{35,3},{4,36},{36... | collective-permute-start | bytes 2752520 | tf_op jit(solution)/shard_map/ppermute | solution.py:223
  81.0 21.5 %all-to-all-start.3 = ((bf16[32,32,128]{2,1,0:T(8,128)(2,1)}), bf16[32,32,128]{2,1,0:T(8,128)(2,1)}, u32[]{:S(2)}, u32[]{:S(2)}) async-start(bf16[32,32,128]{2,1,0:T(8,128)(2,1)} %broadcast_in_dim.16), calls=%async_computation.3 | async-start | bytes 524288 | tf_op jit(solution)/shard_map/all_to_all | solution.py:284
  87.1 1.0 copy-start.7
  99.8 13.7 %collective-permute-start.14 = (bf16[224,1024]{1,0:T(8,128)(2,1)}, bf16[224,1024]{1,0:T(8,128)(2,1)}, u32[]{:S(2)}, u32[]{:S(2)}) collective-permute-start(bf16[224,1024]{1,0:T(8,128)(2,1)} %get-tuple-element.47), channel_id=1, source_target_pairs={{0,1},{1,2},{2,3},{3,0},{4,5},{5,6},{6,7},{7,4},{8,9},{9,10},{10,1... | collective-permute-start | bytes 1376264 | tf_op jit(solution)/shard_map/ppermute | solution.py:223
  101.0 12.5 %collective-permute-start.15 = (bf16[224,1024]{1,0:T(8,128)(2,1)}, bf16[224,1024]{1,0:T(8,128)(2,1)}, u32[]{:S(2)}, u32[]{:S(2)}) collective-permute-start(bf16[224,1024]{1,0:T(8,128)(2,1)} %get-tuple-element.48), channel_id=1, source_target_pairs={{0,3},{1,0},{2,1},{3,2},{4,7},{5,4},{6,5},{7,6},{8,11},{9,8},{10,9... | collective-permute-start | bytes 1376264 | tf_op jit(solution)/shard_map/ppermute | solution.py:223
  105.4 26.1 %all-to-all-start.4 = ((bf16[8,2,64,768]{3,2,1,0:T(8,128)(2,1)}), bf16[8,2,64,768]{3,2,1,0:T(8,128)(2,1)S(1)}, u32[]{:S(2)}, u32[]{:S(2)}) async-start(bf16[8,2,64,768]{3,2,1,0:T(8,128)(2,1)} %bitcast.35), calls=%async_computation.4 | async-start | bytes 3145728 | tf_op jit(solution)/shard_map/all_to_all | solution.py:339
  110.7 8.2 %copy-start.1 = (bf16[1024,256]{1,0:T(8,128)(2,1)S(1)}, bf16[1024,256]{1,0:T(8,128)(2,1)}, u32[]{:S(2)}) copy-start(bf16[1024,256]{1,0:T(8,128)(2,1)} %tokens.3) | copy-start | bytes 1572868
  110.7 8.2 %copy-start.4 = (bf16[1024,256]{1,0:T(8,128)(2,1)S(1)}, bf16[1024,256]{1,0:T(8,128)(2,1)}, u32[]{:S(2)}) copy-start(bf16[1024,256]{1,0:T(8,128)(2,1)} %copy-done.3) | copy-start | bytes 1572868
  110.7 8.2 %copy-start.8 = (bf16[1024,256]{1,0:T(8,128)(2,1)S(1)}, bf16[1024,256]{1,0:T(8,128)(2,1)}, u32[]{:S(2)}) copy-start(bf16[1024,256]{1,0:T(8,128)(2,1)} %copy-done.6) | copy-start | bytes 1572868
  110.7 22.9 %collective-permute-start.17 = (bf16[224,1024]{1,0:T(8,128)(2,1)}, bf16[224,1024]{1,0:T(8,128)(2,1)}, u32[]{:S(2)}, u32[]{:S(2)}) collective-permute-start(bf16[224,1024]{1,0:T(8,128)(2,1)} %get-tuple-element.56), channel_id=1, source_target_pairs={{0,1},{1,2},{2,3},{3,0},{4,5},{5,6},{6,7},{7,4},{8,9},{9,10},{10,1... | collective-permute-start | bytes 1376264 | tf_op jit(solution)/shard_map/ppermute | solution.py:223
  111.0 22.6 %collective-permute-start.18 = (bf16[224,1024]{1,0:T(8,128)(2,1)}, bf16[224,1024]{1,0:T(8,128)(2,1)}, u32[]{:S(2)}, u32[]{:S(2)}) collective-permute-start(bf16[224,1024]{1,0:T(8,128)(2,1)} %get-tuple-element.57), channel_id=1, source_target_pairs={{0,3},{1,0},{2,1},{3,2},{4,7},{5,4},{6,5},{7,6},{8,11},{9,8},{10,9... | collective-permute-start | bytes 1376264 | tf_op jit(solution)/shard_map/ppermute | solution.py:223
  116.2 18.1 %collective-permute-start.16 = (bf16[224,1024]{1,0:T(8,128)(2,1)}, bf16[224,1024]{1,0:T(8,128)(2,1)}, u32[]{:S(2)}, u32[]{:S(2)}) collective-permute-start(bf16[224,1024]{1,0:T(8,128)(2,1)} %get-tuple-element.55), channel_id=1, source_target_pairs={{0,1},{1,2},{2,3},{3,0},{4,5},{5,6},{6,7},{7,4},{8,9},{9,10},{10,1... | collective-permute-start | bytes 1376264 | tf_op jit(solution)/shard_map/ppermute | solution.py:223
  116.4 17.9 %collective-permute-start.19 = (bf16[224,1024]{1,0:T(8,128)(2,1)}, bf16[224,1024]{1,0:T(8,128)(2,1)}, u32[]{:S(2)}, u32[]{:S(2)}) collective-permute-start(bf16[224,1024]{1,0:T(8,128)(2,1)} %get-tuple-element.58), channel_id=1, source_target_pairs={{0,3},{1,0},{2,1},{3,2},{4,7},{5,4},{6,5},{7,6},{8,11},{9,8},{10,9... | collective-permute-start | bytes 1376264 | tf_op jit(solution)/shard_map/ppermute | solution.py:223

commit v8 on v7

--- a/solution.py
+++ b/solution.py
@@ -67,6 +67,22 @@
         )
         both = jnp.concatenate([inputs, back], axis=0)
         out[i * length:(i + 1) * length, :] = both.T.astype(BF)
+
+
+def total_kernel(parts, out):
+    total = parts[0].astype(F32)
+    for i in range(1, parts.shape[0]):
+        total += parts[i].astype(F32)
+    for i in range(out.shape[0]):
+        out[i] = total
+
+
+def round_kernel(totals, out):
+    total = totals[0]
+    for i in range(1, totals.shape[0]):
+        total += totals[i]
+    for i in range(out.shape[0]):
+        out[i] = total.astype(BF)
 
 
 def grads_kernel(used, order, tokens, cot, both, send, *, rank, width, units):
@@ -226,7 +242,6 @@
 def on_device(tokens, cotangent, weight, down, up, used, order):
     n_y, n_z = lax.axis_size("y"), lax.axis_size("z")
     owners = lax.axis_size(DP)
-    members = n_y * n_z
     rows, width = tokens.shape
     units = weight.shape[1]
     per_owner, _, rank = down.shape
@@ -275,15 +290,15 @@
         whole((rows, 2 * rank), BF),
         [SMEM, SMEM, VMEM, VMEM, VMEM],
     )(used, order, factors, tokens, cot_t)
-    share = rows // members
-    parts = lax.all_to_all(part.reshape(members, share, 2 * rank), MP, 0, 0, tiled=True)
-    summed = jnp.sum(parts.astype(F32), axis=0).astype(BF)
+    share = rows // n_z
+    parts = lax.all_to_all(part.reshape(n_z, share, 2 * rank), "z", 0, 0, tiled=True)
+    total = call(total_kernel, whole((n_y, share, 2 * rank), F32), [VMEM])(parts)
+    totals = lax.all_to_all(total, "y", 0, 0, tiled=True)
+    summed = call(round_kernel, whole((n_z, share, 2 * rank), BF), [VMEM])(totals)
     summed, pieces, f4, b4 = together((summed, pieces, f4, b4))
     gathered = (tokens, f1, b1, f2, b2, f3, b3, f4, b4)
     swapped = tuple(hop(item, "core", 1) for item in pieces)
-    both = lax.all_to_all(
-        jnp.broadcast_to(summed[None], (members,) + summed.shape), MP, 0, 0, tiled=True
-    ).reshape(rows, 2 * rank)
+    both = lax.all_to_all(summed, "z", 0, 0, tiled=True).reshape(rows, 2 * rank)
 
     half, step = units // 2, 256
     steps = rows // step
@@ -325,7 +340,6 @@
     )(meta, got2, swap2, got1, swap1, got3, swap3, *gathered)
     both = together((both, far_up, far_down))[0]
     far_up, far_down = hop(far_up, "y", 1), hop(far_down, "y", -1)
-    up_soon, down_soon = hop(up_soon, "y", 1), hop(down_soon, "y", -1)
     up_late, down_late = call(late_kernel, (narrow, narrow), [VMEM] * 4)(
         in_hbm(up_late), far_up, in_hbm(down_late), far_down
     )
@@ -336,6 +350,8 @@
         pltpu.HBM((owners * 2, rank, packed), BF),
         [SMEM, SMEM, VMEM, VMEM, VMEM],
     )(used, order, tokens, cot_t, both)
+    send, up_soon, down_soon = together((send, up_soon, down_soon))
+    up_soon, down_soon = hop(up_soon, "y", 1), hop(down_soon, "y", -1)
     terms = lax.all_to_all(send.reshape(owners, 2, rank, packed), DP, 0, 0, tiled=True)
     grad_a, grad_b = call(
         sum_kernel,

time: 138 us -> 137 us (level)
  blocking collectives: 0 us -> 12.3 us
  waiting for transfers between devices: 32.6 us -> 23.3 us
  starting transfers between devices: 56.9 us -> 53.9 us
  other arithmetic: 2.19 us -> 0.67 us
    all_to_all x0 -> x1, blocking collectives: none -> 12.3 us  [on_device(): totals = lax.all_to_all(total, 'y', 0, 0, tiled=True)]
    all_to_all x2, waiting for transfers between devices: 14.6 us -> 3.48 us  [the longest x1 3.48 us: on_device(): lax.all_to_all(part.reshape(n_z, share, 2 * rank), 'z', 0, 0, tiled=True)]
    all_to_all x2, starting transfers between devices: 14.7 us -> 8.27 us  [the longest x1 4.22 us: on_device(): both = lax.all_to_all(summed, 'z', 0, 0, tiled=True).reshape(rows, 2 * rank)]
    ppermute x20, waiting for transfers between devices: 8.9 us -> 11.8 us  [hop(): return lax.ppermute(value, axis, [(i, (i + step) % n) for i in range(n)])]
    ppermute x20, starting transfers between devices: 26.7 us -> 28.7 us  [hop(): return lax.ppermute(value, axis, [(i, (i + step) % n) for i in range(n)])]
    reduce_sum x1 -> x0, other arithmetic: 1.6 us -> none  [on_device(): summed = jnp.sum(parts.astype(F32), axis=0).astype(BF)]
    broadcast_in_dim x1 -> x0, local copies, waits for them, and re-layouts: 1.44 us -> none  [on_device(): jnp.broadcast_to(summed[None], (members,) + summed.shape)]
  transfers between devices with their start and end apart: 25 -> 25, of which waited for: 5 -> 8; matrix products, arithmetic and copies ran while one was open for 5% -> 3% of each run, Pallas kernels for 25% -> 26%
where the time goes in v8:
time: 137 us; the launch traced here: 136 us
  starting transfers between devices  53.9 us (39%)
  Pallas kernels  38.9 us (28%)
  waiting for transfers between devices  23.3 us (17%)
  blocking collectives  12.3 us (9%)
  local copies, waits for them, and re-layouts  6.14 us (4%)
    ppermute x20, starting transfers between devices, hop(): return lax.ppermute(value, axis, [(i, (i + step) % n) for i in range(n)])  28.7 us
    all_to_all x1, blocking collectives, on_device(): totals = lax.all_to_all(total, 'y', 0, 0, tiled=True)  12.3 us
    ppermute x20, waiting for transfers between devices, hop(): return lax.ppermute(value, axis, [(i, (i + step) % n) for i in range(n)])  11.8 us
    pallas_call x1, Pallas kernels, on_device(): over_tokens(shared_kernel, [narrow] * 4 + [broad] * 2, [all_rows] * 6 + t...  11.6 us
    pallas_call x1, Pallas kernels, on_device(): over_tokens(own_kernel, whole((units, rows), F32), [own_block(block) for...  7.75 us
    all_to_all x1, starting transfers between devices, on_device(): lax.all_to_all(picked, DP, 0, 0, tiled=True)  6.3 us
    all_to_all x1, starting transfers between devices, on_device(): lax.all_to_all(send.reshape(owners, 2, rank, packed), DP, 0, 0, tiled=True)  5.36 us
    all_to_all x1, starting transfers between devices, on_device(): lax.all_to_all(jnp.broadcast_to(used[None], (owners,) + used.shape), DP,...  5.25 us
  transfers between devices with their start and end apart: 25, of which 8 were waited for; matrix products, arithmetic and copies ran while one was open for 3% of the time, Pallas kernels for 26%

profile of v8, /device:TPU:1, one launch (start us, length us, event | category | flops | bytes accessed | tf_op | source)
XLA Modules:
  0.0 136.0 jit_solution(12922976250437631959)
XLA Ops:
  0.6 6.5 %collective-permute-start.1 = (bf16[1024,256]{1,0:T(8,128)(2,1)}, bf16[1024,256]{1,0:T(8,128)(2,1)}, u32[]{:S(2)}, u32[]{:S(2)}) collective-permute-start(bf16[1024,256]{1,0:T(8,128)(2,1)} %tokens.3), channel_id=1, source_target_pairs={{0,28},{4,0},{8,4},{12,8},{16,12},{20,16},{24,20},{28,24},{1,29},{... | collective-permute-start | bytes 1572872 | tf_op jit(solution)/shard_map/ppermute | solution.py:239
  7.1 0.0 collective-permute-start
  7.1 1.2 broadcast_in_dim.9
  8.4 5.3 %all-to-all-start = ((s32[8,1,8]{2,1,0:T(1,128)}), s32[8,1,8]{2,1,0:T(1,128)S(1)}, u32[]{:S(2)}, u32[]{:S(2)}) async-start(s32[8,1,8]{2,1,0:T(1,128)} %broadcast_in_dim.9), calls=%async_computation | async-start | bytes 8192 | tf_op jit(solution)/shard_map/all_to_all | solution.py:272
  13.6 0.7 pad_add_fusion.meta
  14.3 4.4 %shard_map.95 = (bf16[448,1024]{1,0:T(8,128)(2,1)}, bf16[448,1024]{1,0:T(8,128)(2,1)}, bf16[448,1024]{1,0:T(8,128)(2,1)}) custom-call(s32[4]{0:T(128)} %pad_add_fusion.meta, bf16[448,8192]{1,0:T(8,128)(2,1)} %bitcast.26), custom_call_target="tpu_custom_call" | custom-call | tf_op jit(solution)/shard_map/pallas_call | solution.py:263
  18.7 0.0 all-to-all-done
  18.7 2.0 %shard_map.94 = bf16[8,2,64,768]{3,2,1,0:T(8,128)(2,1)} custom-call(s32[1]{0:T(128)} %bitcast.5.me, s32[8,8]{1,0:T(8,128)S(1)} %bitcast.23, bf16[8,64,256]{2,1,0:T(8,128)(2,1)S(1)} %bitcast.22, bf16[8,64,448]{2,1,0:T(8,128)(2,1)S(1)} %copy-done.10), custom_call_target="tpu_custom_call" | custom-call | tf_op jit(solution)/shard_map/pallas_call | solution.py:275
  20.8 0.0 collective-permute-done.1.refs_2_.refs_10_
  20.8 0.2 collective-permute-done.refs_1_.refs_9_
  21.0 0.0 copy-start.14
  21.0 6.3 %all-to-all-start.1 = ((bf16[8,2,64,768]{3,2,1,0:T(8,128)(2,1)}), bf16[8,2,64,768]{3,2,1,0:T(8,128)(2,1)S(1)}, u32[]{:S(2)}, u32[]{:S(2)}) async-start(bf16[8,2,64,768]{3,2,1,0:T(8,128)(2,1)} %shard_map.94), calls=%async_computation.1 | async-start | bytes 3145728 | tf_op jit(solution)/shard_map/all_to_all | solution.py:280
  27.3 0.0 collective-permute-start.2
  27.3 2.7 %collective-permute-start.3 = (bf16[1024,256]{1,0:T(8,128)(2,1)}, bf16[1024,256]{1,0:T(8,128)(2,1)}, u32[]{:S(2)}, u32[]{:S(2)}) collective-permute-start(bf16[1024,256]{1,0:T(8,128)(2,1)} %collective-permute-done.1.refs_2_.refs_10_), channel_id=1, source_target_pairs={{0,28},{4,0},{8,4},{12,8},{16,12},{20,16},{24,20},{28,24},{1,29},{... | collective-permute-start | bytes 1572872 | tf_op jit(solution)/shard_map/ppermute | solution.py:239
  30.0 2.7 %collective-permute-start.6 = (bf16[448,1024]{1,0:T(8,128)(2,1)}, bf16[448,1024]{1,0:T(8,128)(2,1)}, u32[]{:S(2)}, u32[]{:S(2)}) collective-permute-start(bf16[448,1024]{1,0:T(8,128)(2,1)} %get-tuple-element.41), channel_id=1, source_target_pairs={{0,3},{1,0},{2,1},{3,2},{4,7},{5,4},{6,5},{7,6},{8,11},{9,8},{10,9... | collective-permute-start | bytes 2752520 | tf_op jit(solution)/shard_map/ppermute | solution.py:239
  32.8 0.3 collective-permute-start.7
  33.1 0.7 collective-permute-start.8
  33.8 8.3 %collective-permute-done.2.refs_3_.refs_11_ = bf16[1024,256]{1,0:T(8,128)(2,1)} collective-permute-done((bf16[1024,256]{1,0:T(8,128)(2,1)S(1)}, bf16[1024,256]{1,0:T(8,128)(2,1)}, u32[]{:S(2)}, u32[]{:S(2)}) %collective-permute-start.2) | collective-permute-done | bytes 524320 | tf_op jit(solution)/shard_map/ppermute | solution.py:239
  42.1 0.0 collective-permute-start.4
  42.1 0.0 collective-permute-done.3.refs_4_.refs_12_
  42.2 2.7 %collective-permute-start.5 = (bf16[1024,256]{1,0:T(8,128)(2,1)}, bf16[1024,256]{1,0:T(8,128)(2,1)}, u32[]{:S(2)}, u32[]{:S(2)}) collective-permute-start(bf16[1024,256]{1,0:T(8,128)(2,1)} %collective-permute-done.3.refs_4_.refs_12_), channel_id=1, source_target_pairs={{0,28},{4,0},{8,4},{12,8},{16,12},{20,16},{24,20},{28,24},{1,29},{... | collective-permute-start | bytes 1572872 | tf_op jit(solution)/shard_map/ppermute | solution.py:239
  44.8 3.3 %all-to-all-done.1 = bf16[8,2,64,768]{3,2,1,0:T(8,128)(2,1)S(1)} async-done(((bf16[8,2,64,768]{3,2,1,0:T(8,128)(2,1)}), bf16[8,2,64,768]{3,2,1,0:T(8,128)(2,1)S(1)}, u32[]{:S(2)}, u32[]{:S(2)}) %all-to-all-start.1) | async-done | bytes 1572896 | tf_op jit(solution)/shard_map/all_to_all | solution.py:280
  48.2 1.1 shard_map.96
  49.3 0.7 copy-done.5
  50.0 4.0 %all-to-all-start.2 = ((bf16[8,128,128]{2,1,0:T(8,128)(2,1)}), bf16[8,128,128]{2,1,0:T(8,128)(2,1)}, u32[]{:S(2)}, u32[]{:S(2)}) async-start(bf16[8,128,128]{2,1,0:T(8,128)(2,1)} %bitcast.21), calls=%async_computation.2 | async-start | bytes 524288 | tf_op jit(solution)/shard_map/all_to_all | solution.py:294
  54.1 2.2 %collective-permute-done.4.refs_5_.refs_13_ = bf16[1024,256]{1,0:T(8,128)(2,1)S(1)} collective-permute-done((bf16[1024,256]{1,0:T(8,128)(2,1)}, bf16[1024,256]{1,0:T(8,128)(2,1)S(1)}, u32[]{:S(2)}, u32[]{:S(2)}) %collective-permute-start.4) | collective-permute-done | bytes 524320 | tf_op jit(solution)/shard_map/ppermute | solution.py:239
  56.3 0.8 slice.8
  57.0 0.0 collective-permute-start.9
  57.0 0.0 collective-permute-done.5.refs_6_.refs_14_
  57.0 1.7 %slice.9 = bf16[512,256]{1,0:T(8,128)(2,1)} slice(bf16[1024,256]{1,0:T(8,128)(2,1)} %collective-permute-done.5.refs_6_.refs_14_), slice={[512:1024], [0:256]} | slice | bytes 524288 | tf_op jit(solution)/shard_map/slice | solution.py:285
  58.7 2.7 %collective-permute-start.10 = (bf16[512,256]{1,0:T(8,128)(2,1)}, bf16[512,256]{1,0:T(8,128)(2,1)}, u32[]{:S(2)}, u32[]{:S(2)}) collective-permute-start(bf16[512,256]{1,0:T(8,128)(2,1)} %slice.9), channel_id=1, source_target_pairs={{0,28},{4,0},{8,4},{12,8},{16,12},{20,16},{24,20},{28,24},{1,29},{... | collective-permute-start | bytes 786440 | tf_op jit(solution)/shard_map/ppermute | solution.py:239
  61.3 3.5 %all-to-all-done.2.parts = bf16[8,128,128]{2,1,0:T(8,128)(2,1)} async-done(((bf16[8,128,128]{2,1,0:T(8,128)(2,1)}), bf16[8,128,128]{2,1,0:T(8,128)(2,1)}, u32[]{:S(2)}, u32[]{:S(2)}) %all-to-all-start.2) | async-done | bytes 262176 | tf_op jit(solution)/shard_map/all_to_all | solution.py:294
  64.8 1.0 shard_map.97
  65.8 12.3 %all_to_all.30.totals = f32[4,128,128]{2,1,0:T(8,128)S(1)} all-to-all(f32[4,128,128]{2,1,0:T(8,128)S(1)} %shard_map.97), channel_id=1, replica_groups=mesh['x'=4,'core'=2,'z'=8,'y'=4] {'y'}, dimensions={0} | all-to-all | bytes 524288 | tf_op jit(solution)/shard_map/all_to_all | solution.py:296
  78.2 0.7 copy-done.6
  78.9 0.0 collective-permute-done.6.got1
  78.9 0.0 collective-permute-done.7.got2
  78.9 0.0 collective-permute-done.8.got3
  78.9 0.0 collective-permute-done.9.refs_7_.refs_15_
  78.9 0.0 collective-permute-done.10.refs_8_.refs_16_
  78.9 1.7 %collective-permute-start.11 = (bf16[448,1024]{1,0:T(8,128)(2,1)}, bf16[448,1024]{1,0:T(8,128)(2,1)}, u32[]{:S(2)}, u32[]{:S(2)}) collective-permute-start(bf16[448,1024]{1,0:T(8,128)(2,1)} %collective-permute-done.7.got2), channel_id=1, source_target_pairs={{0,32},{32,0},{1,33},{33,1},{2,34},{34,2},{3,35},{35,3},{4,36},{36... | collective-permute-start | bytes 2752520 | tf_op jit(solution)/shard_map/ppermute | solution.py:239
  80.6 0.1 collective-permute-start.12
  80.7 0.4 collective-permute-start.13
  81.1 4.2 %all-to-all-start.4 = ((bf16[8,128,128]{2,1,0:T(8,128)(2,1)}), bf16[8,128,128]{2,1,0:T(8,128)(2,1)}, u32[]{:S(2)}, u32[]{:S(2)}) async-start(bf16[8,128,128]{2,1,0:T(8,128)(2,1)} %copy-done.6), calls=%async_computation.4 | async-start | bytes 524288 | tf_op jit(solution)/shard_map/all_to_all | solution.py:301
  85.3 0.0 collective-permute-done.11.swap2
  85.4 0.0 collective-permute-done.12.swap1
  85.4 0.3 collective-permute-done.13.swap3
  85.7 1.0 copy-done.8
  86.7 11.6 %shard_map.99 = (bf16[224,1024]{1,0:T(8,128)(2,1)}, bf16[224,1024]{1,0:T(8,128)(2,1)}, bf16[224,1024]{1,0:T(8,128)(2,1)}, bf16[224,1024]{1,0:T(8,128)(2,1)}, f32[224,1024]{1,0:T(8,128)}, /*index=5*/f32[224,1024]{1,0:T(8,128)}) custom-call(s32[4]{0:T(128)S(1)} %copy-done.13, bf16[448,1024]{1,0:T(8,128)(2,1)} %collective-permute-done.7.got2, ...), custom_call_target="tpu_custom_call" | custom-call | flops 1 | bytes 1 | tf_op jit(solution)/shard_map/pallas_call | solution.py:334
  98.3 0.1 collective-permute-start.14
  98.4 2.7 %collective-permute-start.15 = (bf16[224,1024]{1,0:T(8,128)(2,1)}, bf16[224,1024]{1,0:T(8,128)(2,1)}, u32[]{:S(2)}, u32[]{:S(2)}) collective-permute-start(bf16[224,1024]{1,0:T(8,128)(2,1)} %get-tuple-element.51), channel_id=1, source_target_pairs={{0,3},{1,0},{2,1},{3,2},{4,7},{5,4},{6,5},{7,6},{8,11},{9,8},{10,9... | collective-permute-start | bytes 1376264 | tf_op jit(solution)/shard_map/ppermute | solution.py:239
  101.1 0.0 all-to-all-done.4
  101.1 2.8 %shard_map.101 = bf16[16,64,768]{2,1,0:T(8,128)(2,1)} custom-call(s32[1,8]{1,0:T(1,128)S(1)} %copy-done.12, s32[1,8]{1,0:T(1,128)S(1)} %copy-done.14, bf16[1024,256]{1,0:T(8,128)(2,1)S(1)} %copy-done, bf16[448,1024]{1,0:T(8,128)(2,1)S(1)} %bitcast.20, bf16[1024,128]{1,0:T(8,128)(2,1)} %bitcast.12.refs_19_.both), custom_call_target="tpu_custom_call" | custom-call | tf_op jit(solution)/shard_map/pallas_call | solution.py:348
  103.9 5.4 %all-to-all-start.5 = ((bf16[8,2,64,768]{3,2,1,0:T(8,128)(2,1)}), bf16[8,2,64,768]{3,2,1,0:T(8,128)(2,1)S(1)}, u32[]{:S(2)}, u32[]{:S(2)}) async-start(bf16[8,2,64,768]{3,2,1,0:T(8,128)(2,1)} %bitcast.35), calls=%async_computation.5 | async-start | bytes 3145728 | tf_op jit(solution)/shard_map/all_to_all | solution.py:355
  109.3 0.1 collective-permute-start.17
  109.4 2.7 %collective-permute-start.18 = (bf16[224,1024]{1,0:T(8,128)(2,1)}, bf16[224,1024]{1,0:T(8,128)(2,1)}, u32[]{:S(2)}, u32[]{:S(2)}) collective-permute-start(bf16[224,1024]{1,0:T(8,128)(2,1)} %get-tuple-element.63), channel_id=1, source_target_pairs={{0,3},{1,0},{2,1},{3,2},{4,7},{5,4},{6,5},{7,6},{8,11},{9,8},{10,9... | collective-permute-start | bytes 1376264 | tf_op jit(solution)/shard_map/ppermute | solution.py:239
  112.1 2.8 %shard_map.103 = (bf16[224,1024]{1,0:T(8,128)(2,1)}, bf16[224,1024]{1,0:T(8,128)(2,1)}) custom-call(f32[224,1024]{1,0:T(8,128)} %get-tuple-element.59.up, bf16[224,1024]{1,0:T(8,128)(2,1)} %collective-permute-done.14.far_up, f32[224,1024]{1,0:T(8,128)} %get-tuple-element.60.down, bf16[224,1024]{1,0:T(8,128)(2,1)} %collective-permute-done.15.far_down), custom_call_target="tpu_custom_call" | custom-call | tf_op jit(solution)/shard_map/pallas_call | solution.py:343
  114.8 2.7 %collective-permute-start.19 = (bf16[224,1024]{1,0:T(8,128)(2,1)}, bf16[224,1024]{1,0:T(8,128)(2,1)}, u32[]{:S(2)}, u32[]{:S(2)}) collective-permute-start(bf16[224,1024]{1,0:T(8,128)(2,1)} %get-tuple-element.64), channel_id=1, source_target_pairs={{0,3},{1,0},{2,1},{3,2},{4,7},{5,4},{6,5},{7,6},{8,11},{9,8},{10,9... | collective-permute-start | bytes 1376264 | tf_op jit(solution)/shard_map/ppermute | solution.py:239
  117.5 7.8 %shard_map.100.base = f32[448,1024]{1,0:T(8,128)} custom-call(s32[4]{0:T(128)S(1)} %copy-done.13, s32[1,8]{1,0:T(1,128)S(1)} %copy-done.12, s32[1,8]{1,0:T(1,128)S(1)} %copy-done.14, bf16[448,8192]{1,0:T(8,128)(2,1)} %bitcast.27, bf16[448,8192]{1,0:T(8,128)(2,1)} %bitcast.28, bf16[448,8192]{1,0:T(8,128)(2,1)} %bitcast.29, bf16[448,8192]{1,0:T(8,128)(2,1)} %bitcast.30, ...), custom_call_target="tpu_custom_call" | custom-call | flops 20000000000 | bytes 20000000000 | tf_op jit(solution)/shard_map/pallas_call | solution.py:373
  125.3 4.7 %all-to-all-done.5.terms = bf16[8,2,64,768]{3,2,1,0:T(8,128)(2,1)S(1)} async-done(((bf16[8,2,64,768]{3,2,1,0:T(8,128)(2,1)}), bf16[8,2,64,768]{3,2,1,0:T(8,128)(2,1)S(1)}, u32[]{:S(2)}, u32[]{:S(2)}) %all-to-all-start.5) | async-done | bytes 1572896 | tf_op jit(solution)/shard_map/all_to_all | solution.py:355
  130.0 2.1 %shard_map.102 = (f32[8,64,256]{2,1,0:T(8,128)}, f32[8,64,448]{2,1,0:T(8,128)}) custom-call(s32[1]{0:T(128)} %bitcast.5.me, s32[8,8]{1,0:T(8,128)S(1)} %bitcast.24, bf16[8,2,64,768]{3,2,1,0:T(8,128)(2,1)S(1)} %all-to-all-done.5.terms), custom_call_target="tpu_custom_call" | custom-call | tf_op jit(solution)/shard_map/pallas_call | solution.py:356
  132.2 0.7 collective-permute-done.16.up_late
  132.9 0.0 collective-permute-done.19.down_late
  132.9 3.2 %shard_map.104 = bf16[448,1024]{1,0:T(8,128)(2,1)} custom-call(f32[448,1024]{1,0:T(8,128)} %shard_map.100.base, bf16[224,1024]{1,0:T(8,128)(2,1)} %collective-permute-done.16.up_late, bf16[224,1024]{1,0:T(8,128)(2,1)} %collective-permute-done.17.up_soon, bf16[224,1024]{1,0:T(8,128)(2,1)} %collective-permute-done.18.down_soon, ...), custom_call_target="tpu_custom_call" | custom-call | tf_op jit(solution)/shard_map/pallas_call | solution.py:385
  (32 shorter events, 0.1 us)
Async XLA Ops:
  0.6 20.2 %collective-permute-start.1 = (bf16[1024,256]{1,0:T(8,128)(2,1)}, bf16[1024,256]{1,0:T(8,128)(2,1)}, u32[]{:S(2)}, u32[]{:S(2)}) collective-permute-start(bf16[1024,256]{1,0:T(8,128)(2,1)} %tokens.3), channel_id=1, source_target_pairs={{0,28},{4,0},{8,4},{12,8},{16,12},{20,16},{24,20},{28,24},{1,29},{... | collective-permute-start | bytes 1572872 | tf_op jit(solution)/shard_map/ppermute | solution.py:239
  7.1 13.9 %collective-permute-start = (bf16[1024,256]{1,0:T(8,128)(2,1)}, bf16[1024,256]{1,0:T(8,128)(2,1)S(1)}, u32[]{:S(2)}, u32[]{:S(2)}) collective-permute-start(bf16[1024,256]{1,0:T(8,128)(2,1)} %tokens.3), channel_id=1, source_target_pairs={{0,4},{4,8},{8,12},{12,16},{16,20},{20,24},{24,28},{28,0},{1,5},{5... | collective-permute-start | bytes 1572872 | tf_op jit(solution)/shard_map/ppermute | solution.py:239
  8.4 10.3 %all-to-all-start = ((s32[8,1,8]{2,1,0:T(1,128)}), s32[8,1,8]{2,1,0:T(1,128)S(1)}, u32[]{:S(2)}, u32[]{:S(2)}) async-start(s32[8,1,8]{2,1,0:T(1,128)} %broadcast_in_dim.9), calls=%async_computation | async-start | bytes 8192 | tf_op jit(solution)/shard_map/all_to_all | solution.py:272
  14.3 4.4 %copy-start.10 = (bf16[8,64,448]{2,1,0:T(8,128)(2,1)S(1)}, bf16[8,64,448]{2,1,0:T(8,128)(2,1)}, u32[]{:S(2)}) copy-start(bf16[8,64,448]{2,1,0:T(8,128)(2,1)} %up.1) | copy-start | bytes 1376260
  14.3 4.4 %copy-start.11 = (bf16[8,256,64]{1,2,0:T(8,128)(2,1)S(1)}, bf16[8,256,64]{1,2,0:T(8,128)(2,1)}, u32[]{:S(2)}) copy-start(bf16[8,256,64]{1,2,0:T(8,128)(2,1)} %param.10) | copy-start | bytes 786436
  21.0 6.3 %copy-start.7 = (bf16[1024,256]{1,0:T(8,128)(2,1)}, bf16[1024,256]{1,0:T(8,128)(2,1)S(1)}, u32[]{:S(2)}) copy-start(bf16[1024,256]{1,0:T(8,128)(2,1)S(1)} %collective-permute-done.refs_1_.refs_9_) | copy-start | bytes 1572868
  21.0 27.2 %copy-start = (bf16[1024,256]{1,0:T(8,128)(2,1)S(1)}, bf16[1024,256]{1,0:T(8,128)(2,1)}, u32[]{:S(2)}) copy-start(bf16[1024,256]{1,0:T(8,128)(2,1)} %tokens.3) | copy-start | bytes 1572868
  21.0 27.2 %copy-start.2 = (bf16[1024,448]{0,1:T(8,128)(2,1)S(1)}, bf16[1024,448]{0,1:T(8,128)(2,1)}, u32[]{:S(2)}) copy-start(bf16[1024,448]{0,1:T(8,128)(2,1)} %param.8) | copy-start | bytes 2752516
  21.0 27.2 %copy-start.12 = (s32[1,8]{1,0:T(1,128)S(1)}, s32[1,8]{1,0:T(1,128)}, u32[]{:S(2)}) copy-start(s32[1,8]{1,0:T(1,128)} %used.5) | copy-start | bytes 100
  21.0 27.2 %copy-start.14 = (s32[1,8]{1,0:T(1,128)S(1)}, s32[1,8]{1,0:T(1,128)}, u32[]{:S(2)}) copy-start(s32[1,8]{1,0:T(1,128)} %order.5) | copy-start | bytes 100
  21.0 27.1 %all-to-all-start.1 = ((bf16[8,2,64,768]{3,2,1,0:T(8,128)(2,1)}), bf16[8,2,64,768]{3,2,1,0:T(8,128)(2,1)S(1)}, u32[]{:S(2)}, u32[]{:S(2)}) async-start(bf16[8,2,64,768]{3,2,1,0:T(8,128)(2,1)} %shard_map.94), calls=%async_computation.1 | async-start | bytes 3145728 | tf_op jit(solution)/shard_map/all_to_all | solution.py:280
  27.3 14.8 %collective-permute-start.2 = (bf16[1024,256]{1,0:T(8,128)(2,1)S(1)}, bf16[1024,256]{1,0:T(8,128)(2,1)}, u32[]{:S(2)}, u32[]{:S(2)}) collective-permute-start(bf16[1024,256]{1,0:T(8,128)(2,1)S(1)} %collective-permute-done.refs_1_.refs_9_), channel_id=1, source_target_pairs={{0,4},{4,8},{8,12},{12,16},{16,20},{20,24},{24,28},{28,0},{1,5},{5... | collective-permute-start | bytes 1572872 | tf_op jit(solution)/shard_map/ppermute | solution.py:239
  27.3 14.8 %collective-permute-start.3 = (bf16[1024,256]{1,0:T(8,128)(2,1)}, bf16[1024,256]{1,0:T(8,128)(2,1)}, u32[]{:S(2)}, u32[]{:S(2)}) collective-permute-start(bf16[1024,256]{1,0:T(8,128)(2,1)} %collective-permute-done.1.refs_2_.refs_10_), channel_id=1, source_target_pairs={{0,28},{4,0},{8,4},{12,8},{16,12},{20,16},{24,20},{28,24},{1,29},{... | collective-permute-start | bytes 1572872 | tf_op jit(solution)/shard_map/ppermute | solution.py:239
  30.0 48.8 %collective-permute-start.6 = (bf16[448,1024]{1,0:T(8,128)(2,1)}, bf16[448,1024]{1,0:T(8,128)(2,1)}, u32[]{:S(2)}, u32[]{:S(2)}) collective-permute-start(bf16[448,1024]{1,0:T(8,128)(2,1)} %get-tuple-element.41), channel_id=1, source_target_pairs={{0,3},{1,0},{2,1},{3,2},{4,7},{5,4},{6,5},{7,6},{8,11},{9,8},{10,9... | collective-permute-start | bytes 2752520 | tf_op jit(solution)/shard_map/ppermute | solution.py:239
  32.8 46.1 %collective-permute-start.7 = (bf16[448,1024]{1,0:T(8,128)(2,1)}, bf16[448,1024]{1,0:T(8,128)(2,1)}, u32[]{:S(2)}, u32[]{:S(2)}) collective-permute-start(bf16[448,1024]{1,0:T(8,128)(2,1)} %get-tuple-element.42), channel_id=1, source_target_pairs={{0,2},{1,3},{2,0},{3,1},{4,6},{5,7},{6,4},{7,5},{8,10},{9,11},{10,... | collective-permute-start | bytes 2752520 | tf_op jit(solution)/shard_map/ppermute | solution.py:239
  33.1 45.8 %collective-permute-start.8 = (bf16[448,1024]{1,0:T(8,128)(2,1)}, bf16[448,1024]{1,0:T(8,128)(2,1)}, u32[]{:S(2)}, u32[]{:S(2)}) collective-permute-start(bf16[448,1024]{1,0:T(8,128)(2,1)} %get-tuple-element.43), channel_id=1, source_target_pairs={{0,1},{1,2},{2,3},{3,0},{4,5},{5,6},{6,7},{7,4},{8,9},{9,10},{10,1... | collective-permute-start | bytes 2752520 | tf_op jit(solution)/shard_map/ppermute | solution.py:239
  42.1 14.1 %collective-permute-start.4 = (bf16[1024,256]{1,0:T(8,128)(2,1)}, bf16[1024,256]{1,0:T(8,128)(2,1)S(1)}, u32[]{:S(2)}, u32[]{:S(2)}) collective-permute-start(bf16[1024,256]{1,0:T(8,128)(2,1)} %collective-permute-done.2.refs_3_.refs_11_), channel_id=1, source_target_pairs={{0,4},{4,8},{8,12},{12,16},{16,20},{20,24},{24,28},{28,0},{1,5},{5... | collective-permute-start | bytes 1572872 | tf_op jit(solution)/shard_map/ppermute | solution.py:239
  42.2 14.9 %collective-permute-start.5 = (bf16[1024,256]{1,0:T(8,128)(2,1)}, bf16[1024,256]{1,0:T(8,128)(2,1)}, u32[]{:S(2)}, u32[]{:S(2)}) collective-permute-start(bf16[1024,256]{1,0:T(8,128)(2,1)} %collective-permute-done.3.refs_4_.refs_12_), channel_id=1, source_target_pairs={{0,28},{4,0},{8,4},{12,8},{16,12},{20,16},{24,20},{28,24},{1,29},{... | collective-permute-start | bytes 1572872 | tf_op jit(solution)/shard_map/ppermute | solution.py:239
  49.3 0.7 copy-start.5
  50.0 14.8 %all-to-all-start.2 = ((bf16[8,128,128]{2,1,0:T(8,128)(2,1)}), bf16[8,128,128]{2,1,0:T(8,128)(2,1)}, u32[]{:S(2)}, u32[]{:S(2)}) async-start(bf16[8,128,128]{2,1,0:T(8,128)(2,1)} %bitcast.21), calls=%async_computation.2 | async-start | bytes 524288 | tf_op jit(solution)/shard_map/all_to_all | solution.py:294
  54.1 31.6 %copy-start.13 = (s32[4]{0:T(128)S(1)}, s32[4]{0:T(128)}, u32[]{:S(2)}) copy-start(s32[4]{0:T(128)} %pad_add_fusion.meta) | copy-start | bytes 52
  56.3 29.4 %copy-start.3 = (bf16[1024,256]{1,0:T(8,128)(2,1)}, bf16[1024,256]{1,0:T(8,128)(2,1)S(1)}, u32[]{:S(2)}) copy-start(bf16[1024,256]{1,0:T(8,128)(2,1)S(1)} %collective-permute-done.4.refs_5_.refs_13_) | copy-start | bytes 1572868
  57.0 21.9 %collective-permute-start.9 = (bf16[512,256]{1,0:T(8,128)(2,1)}, bf16[512,256]{1,0:T(8,128)(2,1)}, u32[]{:S(2)}, u32[]{:S(2)}) collective-permute-start(bf16[512,256]{1,0:T(8,128)(2,1)} %slice.8), channel_id=1, source_target_pairs={{0,4},{4,8},{8,12},{12,16},{16,20},{20,24},{24,28},{28,0},{1,5},{5... | collective-permute-start | bytes 786440 | tf_op jit(solution)/shard_map/ppermute | solution.py:239
  58.7 20.2 %collective-permute-start.10 = (bf16[512,256]{1,0:T(8,128)(2,1)}, bf16[512,256]{1,0:T(8,128)(2,1)}, u32[]{:S(2)}, u32[]{:S(2)}) collective-permute-start(bf16[512,256]{1,0:T(8,128)(2,1)} %slice.9), channel_id=1, source_target_pairs={{0,28},{4,0},{8,4},{12,8},{16,12},{20,16},{24,20},{28,24},{1,29},{... | collective-permute-start | bytes 786440 | tf_op jit(solution)/shard_map/ppermute | solution.py:239
  78.2 0.7 copy-start.6
  78.9 6.4 %collective-permute-start.11 = (bf16[448,1024]{1,0:T(8,128)(2,1)}, bf16[448,1024]{1,0:T(8,128)(2,1)}, u32[]{:S(2)}, u32[]{:S(2)}) collective-permute-start(bf16[448,1024]{1,0:T(8,128)(2,1)} %collective-permute-done.7.got2), channel_id=1, source_target_pairs={{0,32},{32,0},{1,33},{33,1},{2,34},{34,2},{3,35},{35,3},{4,36},{36... | collective-permute-start | bytes 2752520 | tf_op jit(solution)/shard_map/ppermute | solution.py:239
  80.6 4.8 %collective-permute-start.12 = (bf16[448,1024]{1,0:T(8,128)(2,1)}, bf16[448,1024]{1,0:T(8,128)(2,1)}, u32[]{:S(2)}, u32[]{:S(2)}) collective-permute-start(bf16[448,1024]{1,0:T(8,128)(2,1)} %collective-permute-done.6.got1), channel_id=1, source_target_pairs={{0,32},{32,0},{1,33},{33,1},{2,34},{34,2},{3,35},{35,3},{4,36},{36... | collective-permute-start | bytes 2752520 | tf_op jit(solution)/shard_map/ppermute | solution.py:239
  80.7 5.0 %collective-permute-start.13 = (bf16[448,1024]{1,0:T(8,128)(2,1)}, bf16[448,1024]{1,0:T(8,128)(2,1)}, u32[]{:S(2)}, u32[]{:S(2)}) collective-permute-start(bf16[448,1024]{1,0:T(8,128)(2,1)} %collective-permute-done.8.got3), channel_id=1, source_target_pairs={{0,32},{32,0},{1,33},{33,1},{2,34},{34,2},{3,35},{35,3},{4,36},{36... | collective-permute-start | bytes 2752520 | tf_op jit(solution)/shard_map/ppermute | solution.py:239
  81.1 20.0 %all-to-all-start.4 = ((bf16[8,128,128]{2,1,0:T(8,128)(2,1)}), bf16[8,128,128]{2,1,0:T(8,128)(2,1)}, u32[]{:S(2)}, u32[]{:S(2)}) async-start(bf16[8,128,128]{2,1,0:T(8,128)(2,1)} %copy-done.6), calls=%async_computation.4 | async-start | bytes 524288 | tf_op jit(solution)/shard_map/all_to_all | solution.py:301
  85.7 1.0 copy-start.8
  98.3 13.7 %collective-permute-start.14 = (bf16[224,1024]{1,0:T(8,128)(2,1)}, bf16[224,1024]{1,0:T(8,128)(2,1)}, u32[]{:S(2)}, u32[]{:S(2)}) collective-permute-start(bf16[224,1024]{1,0:T(8,128)(2,1)} %get-tuple-element.50), channel_id=1, source_target_pairs={{0,1},{1,2},{2,3},{3,0},{4,5},{5,6},{6,7},{7,4},{8,9},{9,10},{10,1... | collective-permute-start | bytes 1376264 | tf_op jit(solution)/shard_map/ppermute | solution.py:239
  98.4 13.7 %collective-permute-start.15 = (bf16[224,1024]{1,0:T(8,128)(2,1)}, bf16[224,1024]{1,0:T(8,128)(2,1)}, u32[]{:S(2)}, u32[]{:S(2)}) collective-permute-start(bf16[224,1024]{1,0:T(8,128)(2,1)} %get-tuple-element.51), channel_id=1, source_target_pairs={{0,3},{1,0},{2,1},{3,2},{4,7},{5,4},{6,5},{7,6},{8,11},{9,8},{10,9... | collective-permute-start | bytes 1376264 | tf_op jit(solution)/shard_map/ppermute | solution.py:239
  103.9 26.1 %all-to-all-start.5 = ((bf16[8,2,64,768]{3,2,1,0:T(8,128)(2,1)}), bf16[8,2,64,768]{3,2,1,0:T(8,128)(2,1)S(1)}, u32[]{:S(2)}, u32[]{:S(2)}) async-start(bf16[8,2,64,768]{3,2,1,0:T(8,128)(2,1)} %bitcast.35), calls=%async_computation.5 | async-start | bytes 3145728 | tf_op jit(solution)/shard_map/all_to_all | solution.py:355
  109.3 8.2 %copy-start.1 = (bf16[1024,256]{1,0:T(8,128)(2,1)S(1)}, bf16[1024,256]{1,0:T(8,128)(2,1)}, u32[]{:S(2)}) copy-start(bf16[1024,256]{1,0:T(8,128)(2,1)} %tokens.3) | copy-start | bytes 1572868
  109.3 8.2 %copy-start.4 = (bf16[1024,256]{1,0:T(8,128)(2,1)S(1)}, bf16[1024,256]{1,0:T(8,128)(2,1)}, u32[]{:S(2)}) copy-start(bf16[1024,256]{1,0:T(8,128)(2,1)} %copy-done.3) | copy-start | bytes 1572868
  109.3 8.2 %copy-start.9 = (bf16[1024,256]{1,0:T(8,128)(2,1)S(1)}, bf16[1024,256]{1,0:T(8,128)(2,1)}, u32[]{:S(2)}) copy-start(bf16[1024,256]{1,0:T(8,128)(2,1)} %copy-done.7) | copy-start | bytes 1572868
  109.3 22.9 %collective-permute-start.17 = (bf16[224,1024]{1,0:T(8,128)(2,1)}, bf16[224,1024]{1,0:T(8,128)(2,1)}, u32[]{:S(2)}, u32[]{:S(2)}) collective-permute-start(bf16[224,1024]{1,0:T(8,128)(2,1)} %get-tuple-element.62), channel_id=1, source_target_pairs={{0,1},{1,2},{2,3},{3,0},{4,5},{5,6},{6,7},{7,4},{8,9},{9,10},{10,1... | collective-permute-start | bytes 1376264 | tf_op jit(solution)/shard_map/ppermute | solution.py:239
  109.4 22.8 %collective-permute-start.18 = (bf16[224,1024]{1,0:T(8,128)(2,1)}, bf16[224,1024]{1,0:T(8,128)(2,1)}, u32[]{:S(2)}, u32[]{:S(2)}) collective-permute-start(bf16[224,1024]{1,0:T(8,128)(2,1)} %get-tuple-element.63), channel_id=1, source_target_pairs={{0,3},{1,0},{2,1},{3,2},{4,7},{5,4},{6,5},{7,6},{8,11},{9,8},{10,9... | collective-permute-start | bytes 1376264 | tf_op jit(solution)/shard_map/ppermute | solution.py:239
  114.8 18.0 %collective-permute-start.16 = (bf16[224,1024]{1,0:T(8,128)(2,1)}, bf16[224,1024]{1,0:T(8,128)(2,1)}, u32[]{:S(2)}, u32[]{:S(2)}) collective-permute-start(bf16[224,1024]{1,0:T(8,128)(2,1)} %get-tuple-element.61), channel_id=1, source_target_pairs={{0,1},{1,2},{2,3},{3,0},{4,5},{5,6},{6,7},{7,4},{8,9},{9,10},{10,1... | collective-permute-start | bytes 1376264 | tf_op jit(solution)/shard_map/ppermute | solution.py:239
  114.8 18.0 %collective-permute-start.19 = (bf16[224,1024]{1,0:T(8,128)(2,1)}, bf16[224,1024]{1,0:T(8,128)(2,1)}, u32[]{:S(2)}, u32[]{:S(2)}) collective-permute-start(bf16[224,1024]{1,0:T(8,128)(2,1)} %get-tuple-element.64), channel_id=1, source_target_pairs={{0,3},{1,0},{2,1},{3,2},{4,7},{5,4},{6,5},{7,6},{8,11},{9,8},{10,9... | collective-permute-start | bytes 1376264 | tf_op jit(solution)/shard_map/ppermute | solution.py:239
